TPU v7x, 32 devices: a whole 2x2x4 slice. The times are simulated.
32 devices in a mesh: batch: 8 (over z, x), chan: 4 (over y, core).
Axes of the slice: x: 2, y: 2, z: 4, core: 2. Of those that a mesh axis runs over, the one named last changes fastest.
Arguments:
- images: bfloat16 [32, 16, 24, 1024], P('batch', None, None, 'chan'), may hold values from -12 to 12
- heights: int32 [32], replicated, may hold values from 4 to 8
- widths: int32 [32], replicated, may hold values from 6 to 12
- reduce_first: bfloat16 [1024, 512], P(None, 'chan'), may hold values from -0.1875 to 0.1875
- spatial_first: bfloat16 [3, 3, 512, 512], P(None, None, None, 'chan'), may hold values from -0.09375 to 0.09375
- expand_first: bfloat16 [512, 2048], P(None, 'chan'), may hold values from -0.25 to 0.25
- shortcut: bfloat16 [1024, 2048], P(None, 'chan'), may hold values from -0.1875 to 0.1875
- reduce_second: bfloat16 [2048, 512], P(None, 'chan'), may hold values from -0.125 to 0.125
- spatial_second: bfloat16 [3, 3, 512, 512], P(None, None, None, 'chan'), may hold values from -0.09375 to 0.09375
- expand_second: bfloat16 [512, 2048], P(None, 'chan'), may hold values from -0.25 to 0.25
- gain_mid: float32 [4, 512], P(None, 'chan'), may hold values from 0.5 to 1.5
- bias_mid: float32 [4, 512], P(None, 'chan'), may hold values from -3 to 3
- gain_out: float32 [3, 2048], P(None, 'chan'), may hold values from 0.5 to 1.5
- bias_out: float32 [3, 2048], P(None, 'chan'), may hold values from -3 to 3
- cotangent: bfloat16 [32, 8, 12, 2048], P('batch', None, None, 'chan'), may hold values from -6 to 6
Outputs:
- block_out: float32 [32, 8, 12, 2048], P('batch', None, None, 'chan')
- images_grad: float32 [32, 16, 24, 1024], P('batch', None, None, 'chan')
- reduce_first_grad: float32 [1024, 512], P(None, 'chan')
- spatial_first_grad: float32 [3, 3, 512, 512], P(None, None, None, 'chan')
- expand_first_grad: float32 [512, 2048], P(None, 'chan')
- shortcut_grad: float32 [1024, 2048], P(None, 'chan')
- reduce_second_grad: float32 [2048, 512], P(None, 'chan')
- spatial_second_grad: float32 [3, 3, 512, 512], P(None, None, None, 'chan')
- expand_second_grad: float32 [512, 2048], P(None, 'chan')
- gain_mid_grad: float32 [4, 512], P(None, 'chan')
- bias_mid_grad: float32 [4, 512], P(None, 'chan')
- gain_out_grad: float32 [3, 2048], P(None, 'chan')
- bias_out_grad: float32 [3, 2048], P(None, 'chan')
- mean_mid_batch: float32 [4, 512], P(None, 'chan')
- var_mid_batch: float32 [4, 512], P(None, 'chan')
- mean_out_batch: float32 [3, 2048], P(None, 'chan')
- var_out_batch: float32 [3, 2048], P(None, 'chan')
All inputs are finite; a program needn't handle non-finite values.
Results may differ from a plain program's by a relative error of at most 0.029.
Values may be sent and summed in bfloat16 or wider, within the bound.
A program may use at most 192 MiB of HBM per device.

v0:
```python
import jax
import jax.numpy as jnp
from jax import lax
from jax.sharding import PartitionSpec as P

EPS = 1e-05


def shortened(shard):
    return jax.tree.map(lambda a: a.astype(jnp.bfloat16) if a.dtype == jnp.float32 else a, shard)


def frame_masks(heights, widths, rows, cols):
    tall = heights[:, None, None]
    broad = widths[:, None, None]
    row_in = jnp.arange(2 * rows, dtype=jnp.int32)[None, :, None]
    col_in = jnp.arange(2 * cols, dtype=jnp.int32)[None, None, :]
    row_out = jnp.arange(rows, dtype=jnp.int32)[None, :, None]
    col_out = jnp.arange(cols, dtype=jnp.int32)[None, None, :]
    inner = ((row_in < 2 * tall) & (col_in < 2 * broad)).astype(jnp.float32)[..., None]
    outer = ((row_out < tall) & (col_out < broad)).astype(jnp.float32)[..., None]
    return (inner, outer)


def silu_slope(value):
    sig = jax.nn.sigmoid(value)
    return sig * (1.0 + value * (1.0 - sig))


def convolve(source, kernel, stride, rows, cols):
    taps = kernel.shape[0]
    margin = taps // 2
    padded = jnp.pad(source, ((0, 0), (margin, margin), (margin, margin), (0, 0)))
    total = None
    for top in range(taps):
        for left in range(taps):
            window = padded[
                :, top : top + stride * rows : stride, left : left + stride * cols : stride, :
            ]
            term = jnp.einsum(
                "nhwc,cd->nhwd", window, kernel[top, left], preferred_element_type=jnp.float32
            )
            total = term if total is None else total + term
    return total


def kernel_grad(source, grad, stride, taps):
    rows, cols = (grad.shape[1], grad.shape[2])
    margin = taps // 2
    padded = jnp.pad(source, ((0, 0), (margin, margin), (margin, margin), (0, 0)))
    return jnp.stack(
        [
            jnp.stack(
                [
                    jnp.einsum(
                        "nhwc,nhwd->cd",
                        padded[
                            :,
                            top : top + stride * rows : stride,
                            left : left + stride * cols : stride,
                            :,
                        ],
                        grad,
                        preferred_element_type=jnp.float32,
                    )
                    for left in range(taps)
                ]
            )
            for top in range(taps)
        ]
    )


def spread_back(grad, kernel, stride):
    taps = kernel.shape[0]
    margin = taps // 2
    total = None
    for top in range(taps):
        for left in range(taps):
            term = jnp.einsum(
                "nhwd,cd->nhwc", grad, kernel[top, left], preferred_element_type=jnp.float32
            )
            placed = lax.pad(
                term,
                jnp.float32(0.0),
                (
                    (0, 0, 0),
                    (top, 2 * margin - top + stride - 1, stride - 1),
                    (left, 2 * margin - left + stride - 1, stride - 1),
                    (0, 0, 0),
                ),
            )
            total = placed if total is None else total + placed
    rows, cols = (grad.shape[1], grad.shape[2])
    return total[:, margin : margin + stride * rows, margin : margin + stride * cols, :]


def norm_forward(pre, mask, count, gain, bias):
    mean = lax.psum(jnp.sum(pre * mask, axis=(0, 1, 2)), "batch") / count
    centered = (pre - mean) * mask
    spread = lax.psum(jnp.sum(centered * centered, axis=(0, 1, 2)), "batch") / count
    inv = lax.rsqrt(spread + EPS)
    hat = (pre - mean) * inv
    return (hat * gain + bias, hat, inv, mean, spread)


def norm_backward(grad, hat, mask, count, gain, inv):
    masked = grad * mask
    bias_grad, gain_grad = lax.psum(
        (jnp.sum(masked, axis=(0, 1, 2)), jnp.sum(masked * hat, axis=(0, 1, 2))), "batch"
    )
    pre_grad = mask * gain * inv * (grad - (bias_grad + hat * gain_grad) / count)
    return (pre_grad.astype(jnp.bfloat16), gain_grad, bias_grad)


def widen(feature):
    return lax.all_gather(feature, "chan", axis=3, tiled=True)


def input_grad(grad, kernel, stride):
    return jax.tree.map(
        lambda part: part.astype(jnp.float32),
        lax.psum_scatter(
            shortened(spread_back(grad, kernel, stride)), "chan", scatter_dimension=3, tiled=True
        ),
    )


def image_back(grad_one, grad_side, kernels):
    summands = spread_back(grad_one, kernels[0], 1) + spread_back(grad_side, kernels[3], 2)
    return lax.psum_scatter(
        summands.astype(jnp.bfloat16), "chan", scatter_dimension=3, tiled=True
    ).astype(jnp.float32)


def on_device(
    images,
    heights,
    widths,
    reduce_first,
    spatial_first,
    expand_first,
    shortcut,
    reduce_second,
    spatial_second,
    expand_second,
    gain_mid,
    bias_mid,
    gain_out,
    bias_out,
    cotangent,
):
    local = images.shape[0]
    rows, cols = (cotangent.shape[1], cotangent.shape[2])
    offset = lax.axis_index("batch") * local
    inner, outer = frame_masks(
        lax.dynamic_slice_in_dim(heights, offset, local),
        lax.dynamic_slice_in_dim(widths, offset, local),
        rows,
        cols,
    )
    count_out = jnp.sum(heights * widths).astype(jnp.float32)
    count_in = 4.0 * count_out
    kernels = (
        reduce_first[None, None],
        spatial_first,
        expand_first[None, None],
        shortcut[None, None],
        reduce_second[None, None],
        spatial_second,
        expand_second[None, None],
    )
    source = images * inner.astype(jnp.bfloat16)
    whole_source = lax.all_gather(source, "chan", axis=3, tiled=True)
    pre_one = convolve(whole_source, kernels[0], 1, 2 * rows, 2 * cols)
    normed_one, hat_one, inv_one, mean_one, spread_one = norm_forward(
        pre_one, inner, count_in, gain_mid[0], bias_mid[0]
    )
    whole_one = widen((jax.nn.silu(normed_one) * inner).astype(jnp.bfloat16))
    pre_two = convolve(whole_one, kernels[1], 2, rows, cols)
    normed_two, hat_two, inv_two, mean_two, spread_two = norm_forward(
        pre_two, outer, count_out, gain_mid[1], bias_mid[1]
    )
    whole_two = widen((jax.nn.silu(normed_two) * outer).astype(jnp.bfloat16))
    pre_three = convolve(whole_two, kernels[2], 1, rows, cols)
    normed_three, hat_three, inv_three, mean_three, spread_three = norm_forward(
        pre_three, outer, count_out, gain_out[0], bias_out[0]
    )
    pre_side = convolve(whole_source, kernels[3], 2, rows, cols)
    normed_side, hat_side, inv_side, mean_side, spread_side = norm_forward(
        pre_side, outer, count_out, gain_out[1], bias_out[1]
    )
    block_mid = jax.nn.silu(normed_three + normed_side) * outer
    whole_mid = widen(block_mid.astype(jnp.bfloat16))
    pre_four = convolve(whole_mid, kernels[4], 1, rows, cols)
    normed_four, hat_four, inv_four, mean_four, spread_four = norm_forward(
        pre_four, outer, count_out, gain_mid[2], bias_mid[2]
    )
    whole_four = widen((jax.nn.silu(normed_four) * outer).astype(jnp.bfloat16))
    pre_five = convolve(whole_four, kernels[5], 1, rows, cols)
    normed_five, hat_five, inv_five, mean_five, spread_five = norm_forward(
        pre_five, outer, count_out, gain_mid[3], bias_mid[3]
    )
    whole_five = widen((jax.nn.silu(normed_five) * outer).astype(jnp.bfloat16))
    pre_six = convolve(whole_five, kernels[6], 1, rows, cols)
    normed_six, hat_six, inv_six, mean_six, spread_six = norm_forward(
        pre_six, outer, count_out, gain_out[2], bias_out[2]
    )
    result = jax.nn.silu(normed_six + block_mid) * outer
    grad_sum_b = cotangent.astype(jnp.float32) * outer * silu_slope(normed_six + block_mid)
    grad_six, gain_six, bias_six = norm_backward(
        grad_sum_b, hat_six, outer, count_out, gain_out[2], inv_six
    )
    kern_six = kernel_grad(whole_five, grad_six, 1, 1)
    grad_feat_five = input_grad(grad_six, kernels[6], 1)
    grad_five, gain_five, bias_five = norm_backward(
        grad_feat_five * outer * silu_slope(normed_five),
        hat_five,
        outer,
        count_out,
        gain_mid[3],
        inv_five,
    )
    kern_five = kernel_grad(whole_four, grad_five, 1, 3)
    grad_feat_four = input_grad(grad_five, kernels[5], 1)
    grad_four, gain_four, bias_four = norm_backward(
        grad_feat_four * outer * silu_slope(normed_four),
        hat_four,
        outer,
        count_out,
        gain_mid[2],
        inv_four,
    )
    kern_four = kernel_grad(whole_mid, grad_four, 1, 1)
    grad_mid = grad_sum_b + input_grad(grad_four, kernels[4], 1)
    grad_sum_a = grad_mid * outer * silu_slope(normed_three + normed_side)
    grad_three, gain_three, bias_three = norm_backward(
        grad_sum_a, hat_three, outer, count_out, gain_out[0], inv_three
    )
    grad_side, gain_side, bias_side = norm_backward(
        grad_sum_a, hat_side, outer, count_out, gain_out[1], inv_side
    )
    kern_three = kernel_grad(whole_two, grad_three, 1, 1)
    kern_side = kernel_grad(whole_source, grad_side, 2, 1)
    grad_feat_two = input_grad(grad_three, kernels[2], 1)
    grad_two, gain_two, bias_two = norm_backward(
        grad_feat_two * outer * silu_slope(normed_two),
        hat_two,
        outer,
        count_out,
        gain_mid[1],
        inv_two,
    )
    kern_two = kernel_grad(whole_one, grad_two, 2, 3)
    grad_feat_one = input_grad(grad_two, kernels[1], 2)
    grad_one, gain_one, bias_one = norm_backward(
        grad_feat_one * inner * silu_slope(normed_one),
        hat_one,
        inner,
        count_in,
        gain_mid[0],
        inv_one,
    )
    kern_one = kernel_grad(whole_source, grad_one, 1, 1)
    images_grad = image_back(grad_one, grad_side, kernels) * inner
    summed = (
        lax.psum(kern_one.astype(jnp.bfloat16), "batch").astype(jnp.float32),
        lax.psum(kern_two.astype(jnp.bfloat16), "batch").astype(jnp.float32),
        lax.psum(kern_three.astype(jnp.bfloat16), "batch").astype(jnp.float32),
        lax.psum(kern_side.astype(jnp.bfloat16), "batch").astype(jnp.float32),
        lax.psum(kern_four.astype(jnp.bfloat16), "batch").astype(jnp.float32),
        lax.psum(kern_five.astype(jnp.bfloat16), "batch").astype(jnp.float32),
        lax.psum(kern_six.astype(jnp.bfloat16), "batch").astype(jnp.float32),
    )
    counts_mid = jnp.stack([count_in, count_out, count_out, count_out])[:, None]
    mean_mid_batch = jnp.stack([mean_one, mean_two, mean_four, mean_five])
    var_mid_batch = (
        jnp.stack([spread_one, spread_two, spread_four, spread_five])
        * counts_mid
        / (counts_mid - 1.0)
    )
    mean_out_batch = jnp.stack([mean_three, mean_side, mean_six])
    var_out_batch = (
        jnp.stack([spread_three, spread_side, spread_six]) * count_out / (count_out - 1.0)
    )
    return (
        result,
        images_grad,
        summed[0][0, 0],
        summed[1],
        summed[2][0, 0],
        summed[3][0, 0],
        summed[4][0, 0],
        summed[5],
        summed[6][0, 0],
        jnp.stack([gain_one, gain_two, gain_four, gain_five]),
        jnp.stack([bias_one, bias_two, bias_four, bias_five]),
        jnp.stack([gain_three, gain_side, gain_six]),
        jnp.stack([bias_three, bias_side, bias_six]),
        mean_mid_batch,
        var_mid_batch,
        mean_out_batch,
        var_out_batch,
    )


def solution(mesh):
    in_specs = (
        P("batch", None, None, "chan"),
        P(),
        P(),
        P(None, "chan"),
        P(None, None, None, "chan"),
        P(None, "chan"),
        P(None, "chan"),
        P(None, "chan"),
        P(None, None, None, "chan"),
        P(None, "chan"),
        P(None, "chan"),
        P(None, "chan"),
        P(None, "chan"),
        P(None, "chan"),
        P("batch", None, None, "chan"),
    )
    out_specs = (
        P("batch", None, None, "chan"),
        P("batch", None, None, "chan"),
        P(None, "chan"),
        P(None, None, None, "chan"),
        P(None, "chan"),
        P(None, "chan"),
        P(None, "chan"),
        P(None, None, None, "chan"),
        P(None, "chan"),
        P(None, "chan"),
        P(None, "chan"),
        P(None, "chan"),
        P(None, "chan"),
        P(None, "chan"),
        P(None, "chan"),
        P(None, "chan"),
        P(None, "chan"),
    )
    return jax.shard_map(
        on_device, mesh=mesh, in_specs=in_specs, out_specs=out_specs, check_vma=False
    )
```

profile of v0, /device:TPU:0, one launch (start us, length us, event | category | flops | bytes accessed | tf_op | source)
XLA Modules:
  0.0 1228.0 jit_solution(8842536787202095234)
XLA Ops:
  12.2 30.3 %all-gather.4.cloned.1.call-done = bf16[4,16,24,1024]{3,2,1,0:T(8,128)(2,1)} async-done(((bf16[4,16,24,256]{3,2,1,0:T(8,128)(2,1)}), bf16[4,16,24,1024]{3,2,1,0:T(8,128)(2,1)}) %all-gather.4.cloned.1.call-update) | async-done | bytes 3145744 | tf_op jit(solution)/shard_map/all_gather | solution.py:174
  45.5 21.4 %psum.241 = f32[128]{0:T(128)S(1)} all-reduce(f32[128]{0:T(128)S(1)} %get-tuple-element.137), channel_id=1, replica_groups=mesh['batch'=8,'chan'=4] {'batch'}, use_global_device_ids=true, to_apply=%region_1.2 | all-reduce | flops 128 | bytes 1024 | tf_op jit(solution)/shard_map/psum | solution.py:99
  67.8 17.2 %psum.242 = f32[128]{0:T(128)S(1)} all-reduce(f32[128]{0:T(128)S(1)} %multiply_reduce_fusion.12), channel_id=1, replica_groups=mesh['batch'=8,'chan'=4] {'batch'}, use_global_device_ids=true, to_apply=%region_4.5 | all-reduce | flops 128 | bytes 1024 | tf_op jit(solution)/shard_map/psum | solution.py:101
  86.9 17.4 %slice.227 = bf16[4,8,12,1024]{3,2,1,0:T(8,128)(2,1)} slice(bf16[4,16,24,1024]{3,2,1,0:T(8,128)(2,1)} %all-gather.4.cloned.1.call-done), slice={[0:4:1], [0:16:2], [0:24:2], [0:1024:1]} | slice | bytes 1572864 | tf_op jit(solution)/shard_map/slice | solution.py:37
  106.8 10.1 slice.205
  116.8 10.0 slice.207
  126.8 10.0 slice.209
  136.8 10.0 slice.211
  146.8 10.0 slice.213
  156.8 10.0 slice.215
  166.8 10.0 slice.217
  186.7 10.0 slice.221
  203.2 21.4 %psum.243 = f32[128]{0:T(128)S(1)} all-reduce(f32[128]{0:T(128)S(1)} %get-tuple-element.139), channel_id=1, replica_groups=mesh['batch'=8,'chan'=4] {'batch'}, use_global_device_ids=true, to_apply=%region_6.7 | all-reduce | flops 128 | bytes 1024 | tf_op jit(solution)/shard_map/psum | solution.py:99
  225.3 17.1 %psum.244 = f32[128]{0:T(128)S(1)} all-reduce(f32[128]{0:T(128)S(1)} %multiply_reduce_fusion.22), channel_id=1, replica_groups=mesh['batch'=8,'chan'=4] {'batch'}, use_global_device_ids=true, to_apply=%region_8.9 | all-reduce | flops 128 | bytes 1024 | tf_op jit(solution)/shard_map/psum | solution.py:101
  250.4 19.1 %psum.245 = f32[512]{0:T(512)S(1)} all-reduce(f32[512]{0:T(512)S(1)} %get-tuple-element.141), channel_id=1, replica_groups=mesh['batch'=8,'chan'=4] {'batch'}, use_global_device_ids=true, to_apply=%region_10.11 | all-reduce | flops 512 | bytes 4096 | tf_op jit(solution)/shard_map/psum | solution.py:99
  272.4 17.1 %psum.247 = f32[512]{0:T(512)S(1)} all-reduce(f32[512]{0:T(512)S(1)} %get-tuple-element.65), channel_id=1, replica_groups=mesh['batch'=8,'chan'=4] {'batch'}, use_global_device_ids=true, to_apply=%region_14.15 | all-reduce | flops 512 | bytes 4096 | tf_op jit(solution)/shard_map/psum | solution.py:99
  291.0 19.1 %all-reduce.27 = (f32[512]{0:T(512)S(1)}, f32[512]{0:T(512)S(1)}) all-reduce(f32[512]{0:T(512)S(1)} %multiply_reduce_fusion.5, f32[512]{0:T(512)S(1)} %get-tuple-element.64), channel_id=1, replica_groups=mesh['batch'=8,'chan'=4] {'batch'}, use_global_device_ids=true, to_apply=%region_16.17 | all-reduce | flops 1024 | bytes 8192 | tf_op jit(solution)/shard_map/psum | solution.py:101
  313.2 19.7 %all-gather.8.cloned.1.call-done = bf16[4,8,12,2048]{3,2,1,0:T(8,128)(2,1)} async-done(((bf16[4,8,12,512]{3,2,1,0:T(8,128)(2,1)}), bf16[4,8,12,2048]{3,2,1,0:T(8,128)(2,1)}) %all-gather.8.cloned.1.call-update) | async-done | bytes 1572880 | tf_op jit(solution)/shard_map/all_gather | solution.py:117
  335.2 21.4 %psum.249 = f32[128]{0:T(128)S(1)} all-reduce(f32[128]{0:T(128)S(1)} %get-tuple-element.144), channel_id=1, replica_groups=mesh['batch'=8,'chan'=4] {'batch'}, use_global_device_ids=true, to_apply=%region_18.19 | all-reduce | flops 128 | bytes 1024 | tf_op jit(solution)/shard_map/psum | solution.py:99
  357.3 17.1 %psum.250 = f32[128]{0:T(128)S(1)} all-reduce(f32[128]{0:T(128)S(1)} %multiply_reduce_fusion.20), channel_id=1, replica_groups=mesh['batch'=8,'chan'=4] {'batch'}, use_global_device_ids=true, to_apply=%region_20.21 | all-reduce | flops 128 | bytes 1024 | tf_op jit(solution)/shard_map/psum | solution.py:101
  386.5 19.1 %psum.251 = f32[128]{0:T(128)S(1)} all-reduce(f32[128]{0:T(128)S(1)} %get-tuple-element.146), channel_id=1, replica_groups=mesh['batch'=8,'chan'=4] {'batch'}, use_global_device_ids=true, to_apply=%region_22.23 | all-reduce | flops 128 | bytes 1024 | tf_op jit(solution)/shard_map/psum | solution.py:99
  406.2 17.1 %psum.252 = f32[128]{0:T(128)S(1)} all-reduce(f32[128]{0:T(128)S(1)} %multiply_reduce_fusion.18), channel_id=1, replica_groups=mesh['batch'=8,'chan'=4] {'batch'}, use_global_device_ids=true, to_apply=%region_24.25 | all-reduce | flops 128 | bytes 1024 | tf_op jit(solution)/shard_map/psum | solution.py:101
  432.4 19.1 %psum.253 = f32[512]{0:T(512)S(1)} all-reduce(f32[512]{0:T(512)S(1)} %get-tuple-element.148), channel_id=1, replica_groups=mesh['batch'=8,'chan'=4] {'batch'}, use_global_device_ids=true, to_apply=%region_26.27 | all-reduce | flops 512 | bytes 4096 | tf_op jit(solution)/shard_map/psum | solution.py:99
  453.0 17.1 %psum.254 = f32[512]{0:T(512)S(1)} all-reduce(f32[512]{0:T(512)S(1)} %multiply_reduce_fusion.3), channel_id=1, replica_groups=mesh['batch'=8,'chan'=4] {'batch'}, use_global_device_ids=true, to_apply=%region_28.29 | all-reduce | flops 512 | bytes 4096 | tf_op jit(solution)/shard_map/psum | solution.py:101
  473.9 19.1 %all-reduce.26 = (f32[512]{0:T(512)S(1)}, f32[512]{0:T(512)S(1)}) all-reduce(f32[512]{0:T(512)S(1)} %get-tuple-element.57, f32[512]{0:T(512)S(1)} %get-tuple-element.56), channel_id=1, replica_groups=mesh['batch'=8,'chan'=4] {'batch'}, use_global_device_ids=true, to_apply=%region_32.33 | all-reduce | flops 1024 | bytes 8192 | tf_op jit(solution)/shard_map/psum | solution.py:109
  514.1 17.6 %reduce-scatter.19.cloned.1.call-done = bf16[128,384]{1,0:T(8,128)(2,1)} async-done(((bf16[512,384]{1,0:T(8,128)(2,1)}), bf16[128,384]{1,0:T(8,128)(2,1)}) %reduce-scatter.19.cloned.1.call-update) | async-done | bytes 98320
  538.4 22.2 %all-reduce.25 = (f32[128]{0:T(128)S(1)}, f32[128]{0:T(128)}) all-reduce(f32[128]{0:T(128)S(1)} %get-tuple-element.63, f32[128]{0:T(128)S(1)} %get-tuple-element.62), channel_id=1, replica_groups=mesh['batch'=8,'chan'=4] {'batch'}, use_global_device_ids=true, to_apply=%region_37.38 | all-reduce | flops 256 | bytes 2048 | tf_op jit(solution)/shard_map/psum | solution.py:109
  584.6 17.2 %reduce-scatter.21.cloned.1.call-done = bf16[128,384]{1,0:T(8,128)(2,1)} async-done(((bf16[512,384]{1,0:T(8,128)(2,1)}), bf16[128,384]{1,0:T(8,128)(2,1)}) %reduce-scatter.21.cloned.1.call-update) | async-done | bytes 98320
  609.1 22.0 %all-reduce.24 = (f32[128]{0:T(128)}, f32[128]{0:T(128)}) all-reduce(f32[128]{0:T(128)} %get-tuple-element.61, f32[128]{0:T(128)S(1)} %get-tuple-element.60), channel_id=1, replica_groups=mesh['batch'=8,'chan'=4] {'batch'}, use_global_device_ids=true, to_apply=%region_42.43 | all-reduce | flops 256 | bytes 2048 | tf_op jit(solution)/shard_map/psum | solution.py:109
  642.8 19.4 %reduce-scatter.15.cloned.1.call-done = bf16[4,8,12,512]{3,2,1,0:T(8,128)(2,1)} async-done(((bf16[4,8,12,2048]{3,2,1,0:T(8,128)(2,1)}), bf16[4,8,12,512]{3,2,1,0:T(8,128)(2,1)}) %reduce-scatter.15.cloned.1.call-update) | async-done | bytes 393232 | tf_op jit(solution)/shard_map/reduce_scatter | solution.py:123
  665.9 21.4 %all-reduce.23 = (f32[512]{0:T(512)S(1)}, f32[512]{0:T(512)S(1)}) all-reduce(f32[512]{0:T(512)S(1)} %get-tuple-element.55, f32[512]{0:T(512)S(1)} %get-tuple-element.53), channel_id=1, replica_groups=mesh['batch'=8,'chan'=4] {'batch'}, use_global_device_ids=true, to_apply=%region_45.46 | all-reduce | flops 1024 | bytes 8192 | tf_op jit(solution)/shard_map/psum | solution.py:109
  710.0 13.1 %reduce-scatter.23.cloned.1.call-done = bf16[128,384]{1,0:T(8,128)(2,1)} async-done(((bf16[512,384]{1,0:T(8,128)(2,1)}), bf16[128,384]{1,0:T(8,128)(2,1)}) %reduce-scatter.23.cloned.1.call-update) | async-done | bytes 98320
  730.1 21.5 %all-reduce.22 = (f32[128]{0:T(128)S(1)}, f32[128]{0:T(128)S(1)}) all-reduce(f32[128]{0:T(128)S(1)} %get-tuple-element.59, f32[128]{0:T(128)S(1)} %get-tuple-element.58), channel_id=1, replica_groups=mesh['batch'=8,'chan'=4] {'batch'}, use_global_device_ids=true, to_apply=%region_52.53 | all-reduce | flops 256 | bytes 2048 | tf_op jit(solution)/shard_map/psum | solution.py:109
  762.4 17.7 %pad.78 = f32[4,18,26,512]{3,2,1,0:T(8,128)} pad(f32[4,8,12,512]{3,2,1,0:T(8,128)} %fusion.119, f32[]{:T(128)} %constant.19.clone.1), padding=0_0_0x0_3_1x0_3_1x0_0_0 | pad | bytes 4620292 | tf_op jit(solution)/shard_map/pad | solution.py:83
  780.1 12.4 %pad.79 = f32[4,18,26,512]{3,2,1,0:T(8,128)} pad(f32[4,8,12,512]{3,2,1,0:T(8,128)S(1)} %copy-done.13, f32[]{:T(128)} %constant.19.clone.1), padding=0_0_0x0_3_1x1_2_1x0_0_0 | pad | bytes 4620292 | tf_op jit(solution)/shard_map/pad | solution.py:83
  792.5 17.8 %pad.80 = f32[4,18,26,512]{3,2,1,0:T(8,128)} pad(f32[4,8,12,512]{3,2,1,0:T(8,128)} %fusion.113, f32[]{:T(128)} %constant.19.clone.1), padding=0_0_0x0_3_1x2_1_1x0_0_0 | pad | bytes 4620292 | tf_op jit(solution)/shard_map/pad | solution.py:83
  810.2 12.3 %pad.81 = f32[4,18,26,512]{3,2,1,0:T(8,128)} pad(f32[4,8,12,512]{3,2,1,0:T(8,128)S(1)} %copy-done.12, f32[]{:T(128)} %constant.19.clone.1), padding=0_0_0x1_2_1x0_3_1x0_0_0 | pad | bytes 4620292 | tf_op jit(solution)/shard_map/pad | solution.py:83
  822.5 17.6 %pad.245 = f32[4,16,25,512]{3,2,1,0:T(8,128)} pad(f32[4,8,12,512]{3,2,1,0:T(8,128)} %fusion.101, f32[]{:T(128)} %constant.19.clone.1), padding=0_0_0x1_0_1x0_2_1x0_0_0 | pad | bytes 4063236
  840.2 11.7 pad.149
  851.9 17.0 %pad.150 = f32[4,16,24,512]{3,2,1,0:T(8,128)} pad(f32[4,8,12,512]{3,2,1,0:T(8,128)} %fusion.104, f32[]{:T(128)} %constant.19.clone.1), padding=0_0_0x0_1_1x1_0_1x0_0_0 | pad | bytes 3932164 | tf_op jit(solution)/shard_map/slice | solution.py:95
  868.9 11.7 pad.152
  880.6 11.6 pad.153
  910.2 12.1 copy.180
  922.3 12.9 %reshape.272 = bf16[512,1536]{1,0:T(8,128)(2,1)} reshape(bf16[512,4,16,24]{3,2,1,0:T(8,128)(2,1)} %bitcast.540) | data formatting | bytes 3145728
  968.8 21.4 %all-reduce.21 = (f32[512]{0:T(512)S(1)}, f32[128]{0:T(128)S(1)}, f32[128]{0:T(128)S(1)}) all-reduce(f32[512]{0:T(512)S(1)} %get-tuple-element.54, f32[128]{0:T(128)S(1)} %get-tuple-element.52, f32[128]{0:T(128)S(1)} %get-tuple-element.51), channel_id=1, replica_groups=mesh['batch'=8,'chan'=4] {'batch'}, use_global_device_ids=true, to_apply=%region_59.60 | all-reduce | flops 768 | bytes 6144 | tf_op jit(solution)/shard_map/psum | solution.py:109
  998.8 19.5 %pad.87 = f32[4,16,24,1024]{3,2,1,0:T(8,128)} pad(f32[4,8,12,1024]{3,2,1,0:T(8,128)} %fusion.54, f32[]{:T(128)} %constant.19.clone.1), padding=0_0_0x0_1_1x0_1_1x0_0_0 | pad | bytes 7864324 | tf_op jit(solution)/shard_map/pad | solution.py:83
  1032.0 147.2 %all-reduce.31.cloned.1.call-done = (bf16[1024,128]{1,0:T(8,128)(2,1)}, bf16[3,3,512,128]{3,2,1,0:T(8,128)(2,1)}, bf16[512,512]{1,0:T(8,128)(2,1)}, bf16[1024,51...) async-done(((bf16[1024,128]{1,0:T(8,128)(2,1)}, bf16[3,3,512,128]{3,2,1,0:T(8,128)(2,1)}, ...) | async-done | bytes 5242896 | tf_op jit(solution)/shard_map/psum | solution.py:267
  1189.6 28.7 %reduce-scatter.17.cloned.1.call-done = bf16[4,16,24,256]{3,2,1,0:T(8,128)(2,1)} async-done(((bf16[4,16,24,1024]{3,2,1,0:T(8,128)(2,1)}), bf16[4,16,24,256]{3,2,1,0:T(8,128)(2,1)}) %reduce-scatter.17.cloned.1.call-update) | async-done | bytes 786448 | tf_op jit(solution)/shard_map/reduce_scatter | solution.py:131
  (415 shorter events, 275.8 us)
Async XLA Ops:
  7.2 262.3 %copy-start = (bf16[1024,512]{1,0:T(8,128)(2,1)S(1)}, bf16[1024,512]{1,0:T(8,128)(2,1)}, u32[]{:S(2)}) copy-start(bf16[1024,512]{1,0:T(8,128)(2,1)} %param.21) | copy-start | bytes 3145732
  7.2 35.3 %all-gather.4.cloned.1.call-start = ((), (), s32[]{:S(2)}) async-start(), calls=%async_computation.6 | async-start | bytes 3932160 | tf_op jit(solution)/shard_map/all_gather | solution.py:174
  8.4 34.2 %copy-start.57 = (bf16[1024,128]{1,0:T(8,128)(2,1)S(1)}, bf16[1024,128]{1,0:T(8,128)(2,1)}, u32[]{:S(2)}) copy-start(bf16[1024,128]{1,0:T(8,128)(2,1)} %param.18) | copy-start | bytes 786436
  10.7 93.5 %all-gather.6.cloned.1.call-start = ((), (), s32[]{:S(2)}) async-start(), calls=%async_computation.7 | async-start | bytes 1966080 | tf_op jit(solution)/shard_map/all_gather | solution.py:117
  12.1 73.3 %copy-start.66 = (f32[128]{0:T(128)}, f32[128]{0:T(128)S(1)}, u32[]{:S(2)}) copy-start(f32[128]{0:T(128)S(1)} %get-tuple-element.133) | copy-start | bytes 1540
  12.1 73.3 %copy-start.68 = (f32[128]{0:T(128)}, f32[128]{0:T(128)S(1)}, u32[]{:S(2)}) copy-start(f32[128]{0:T(128)S(1)} %get-tuple-element.153) | copy-start | bytes 1540
  12.1 362.8 %copy-start.70 = (f32[128]{0:T(128)}, f32[128]{0:T(128)S(1)}, u32[]{:S(2)}) copy-start(f32[128]{0:T(128)S(1)} %get-tuple-element.134) | copy-start | bytes 1540
  12.2 362.8 %copy-start.72 = (f32[128]{0:T(128)}, f32[128]{0:T(128)S(1)}, u32[]{:S(2)}) copy-start(f32[128]{0:T(128)S(1)} %get-tuple-element.152) | copy-start | bytes 1540
  45.4 41.1 %copy-start.2 = (f32[4,16,24,128]{3,2,1,0:T(8,128)}, f32[4,16,24,128]{3,2,1,0:T(8,128)S(1)}, u32[]{:S(2)}) copy-start(f32[4,16,24,128]{3,2,1,0:T(8,128)S(1)} %get-tuple-element.138) | copy-start | bytes 2359300
  67.5 19.3 %copy-start.78 = (f32[3,512]{1,0:T(4,128)S(1)}, f32[3,512]{1,0:T(4,128)}, u32[]{:S(2)}) copy-start(f32[3,512]{1,0:T(4,128)} %param.27) | copy-start | bytes 18436
  67.5 19.3 %copy-start.79 = (f32[3,512]{1,0:T(4,128)S(1)}, f32[3,512]{1,0:T(4,128)}, u32[]{:S(2)}) copy-start(f32[3,512]{1,0:T(4,128)} %param.28) | copy-start | bytes 18436
  86.5 246.4 %all-gather.8.cloned.1.call-start = ((), (), s32[]{:S(2)}) async-start(), calls=%async_computation.8 | async-start | bytes 2621440 | tf_op jit(solution)/shard_map/all_gather | solution.py:117
  202.9 46.7 %copy-start.19 = (bf16[512,512]{1,0:T(8,128)(2,1)S(1)}, bf16[512,512]{1,0:T(8,128)(2,1)}, u32[]{:S(2)}) copy-start(bf16[512,512]{1,0:T(8,128)(2,1)} %param.20) | copy-start | bytes 1572868
  310.2 22.7 %copy-start.102 = (bf16[2048,128]{1,0:T(8,128)(2,1)S(1)}, bf16[2048,128]{1,0:T(8,128)(2,1)}, u32[]{:S(2)}) copy-start(bf16[2048,128]{1,0:T(8,128)(2,1)} %param.22) | copy-start | bytes 1572868
  313.2 218.5 %reduce-scatter.19.cloned.1.call-start = ((), (), s32[]{:S(2)}) async-start(), calls=%async_computation.11 | async-start | bytes 491520
  335.2 49.1 %copy-start.14 = (f32[4,8,12,128]{3,2,1,0:T(8,128)}, f32[4,8,12,128]{3,2,1,0:T(8,128)S(1)}, u32[]{:S(2)}) copy-start(f32[4,8,12,128]{3,2,1,0:T(8,128)S(1)} %get-tuple-element.145) | copy-start | bytes 589828
  357.1 27.2 %copy-start.64 = (f32[128]{0:T(128)}, f32[128]{0:T(128)S(1)}, u32[]{:S(2)}) copy-start(f32[128]{0:T(128)S(1)} %broadcast_divide_fusion.9) | copy-start | bytes 1540
  374.9 9.4 copy-start.76
  423.3 7.6 copy-start.17
  514.0 87.7 %reduce-scatter.21.cloned.1.call-start = ((), (), s32[]{:S(2)}) async-start(), calls=%async_computation.12 | async-start | bytes 491520
  584.5 23.9 %copy-start.15 = (f32[4,8,12,128]{3,2,1,0:T(8,128)S(1)}, f32[4,8,12,128]{3,2,1,0:T(8,128)}, u32[]{:S(2)}) copy-start(f32[4,8,12,128]{3,2,1,0:T(8,128)} %copy-done.14) | copy-start | bytes 589828
  584.5 23.9 %copy-start.65 = (f32[128]{0:T(128)S(1)}, f32[128]{0:T(128)}, u32[]{:S(2)}) copy-start(f32[128]{0:T(128)} %copy-done.64) | copy-start | bytes 1540
  584.5 23.9 %copy-start.71 = (f32[128]{0:T(128)S(1)}, f32[128]{0:T(128)}, u32[]{:S(2)}) copy-start(f32[128]{0:T(128)} %copy-done.70) | copy-start | bytes 1540
  584.5 23.9 %copy-start.73 = (f32[128]{0:T(128)S(1)}, f32[128]{0:T(128)}, u32[]{:S(2)}) copy-start(f32[128]{0:T(128)} %copy-done.72) | copy-start | bytes 1540
  584.5 23.9 %copy-start.77 = (f32[128]{0:T(128)S(1)}, f32[128]{0:T(128)}, u32[]{:S(2)}) copy-start(f32[128]{0:T(128)} %copy-done.76) | copy-start | bytes 1540
  584.5 77.7 %reduce-scatter.15.cloned.1.call-start = ((), (), s32[]{:S(2)}) async-start(), calls=%async_computation.9 | async-start | bytes 2621440 | tf_op jit(solution)/shard_map/reduce_scatter | solution.py:123
  608.4 25.9 %copy-start.55 = (bf16[4,8,12,128]{3,2,1,0:T(8,128)(2,1)}, bf16[4,8,12,128]{3,2,1,0:T(8,128)(2,1)S(1)}, u32[]{:S(2)}) copy-start(bf16[4,8,12,128]{3,2,1,0:T(8,128)(2,1)S(1)} %copy.177) | copy-start | bytes 294916
  634.3 88.8 %reduce-scatter.23.cloned.1.call-start = ((), (), s32[]{:S(2)}) async-start(), calls=%async_computation.13 | async-start | bytes 491520
  697.1 8.8 copy-start.61
  697.1 8.8 copy-start.62
  697.1 8.8 copy-start.63
  705.9 254.0 %reduce-scatter.25.cloned.1.call-start = ((), (), s32[]{:S(2)}) async-start(), calls=%async_computation.14 | async-start | bytes 1966080
  727.3 24.5 %copy-start.6 = (bf16[3,3,512,128]{3,2,1,0:T(8,128)(2,1)S(1)}, bf16[3,3,512,128]{3,2,1,0:T(8,128)(2,1)}, u32[]{:S(2)}) copy-start(bf16[3,3,512,128]{3,2,1,0:T(8,128)(2,1)} %param.19) | copy-start | bytes 3538948
  762.3 17.7 %copy-start.13 = (f32[4,8,12,512]{3,2,1,0:T(8,128)S(1)}, f32[4,8,12,512]{3,2,1,0:T(8,128)}, u32[]{:S(2)}) copy-start(f32[4,8,12,512]{3,2,1,0:T(8,128)} %fusion.116) | copy-start | bytes 2359300
  792.5 17.8 %copy-start.12 = (f32[4,8,12,512]{3,2,1,0:T(8,128)S(1)}, f32[4,8,12,512]{3,2,1,0:T(8,128)}, u32[]{:S(2)}) copy-start(f32[4,8,12,512]{3,2,1,0:T(8,128)} %fusion.110) | copy-start | bytes 2359300
  822.5 17.6 %copy-start.10 = (f32[4,8,12,512]{3,2,1,0:T(8,128)S(1)}, f32[4,8,12,512]{3,2,1,0:T(8,128)}, u32[]{:S(2)}) copy-start(f32[4,8,12,512]{3,2,1,0:T(8,128)} %fusion.107) | copy-start | bytes 2359300
  851.9 17.0 %copy-start.9 = (f32[4,8,12,512]{3,2,1,0:T(8,128)S(1)}, f32[4,8,12,512]{3,2,1,0:T(8,128)}, u32[]{:S(2)}) copy-start(f32[4,8,12,512]{3,2,1,0:T(8,128)} %fusion.98) | copy-start | bytes 2359300
  935.2 244.0 %all-reduce.31.cloned.1.call-start = ((), (), s32[]{:S(2)}) async-start(), calls=%async_computation.15 | async-start | bytes 10485760 | tf_op jit(solution)/shard_map/psum | solution.py:267
  968.3 21.9 %copy-start.45 = (bf16[4,16,24,128]{3,2,1,0:T(8,128)(2,1)}, bf16[4,16,24,128]{3,2,1,0:T(8,128)(2,1)S(1)}, u32[]{:S(2)}) copy-start(bf16[4,16,24,128]{3,2,1,0:T(8,128)(2,1)S(1)} %copy.181) | copy-start | bytes 1179652
  968.3 21.9 %copy-start.1 = (f32[4,8,12,512]{3,2,1,0:T(8,128)S(1)}, f32[4,8,12,512]{3,2,1,0:T(8,128)}, u32[]{:S(2)}) copy-start(f32[4,8,12,512]{3,2,1,0:T(8,128)} %get-tuple-element.143) | copy-start | bytes 2359300
  990.2 28.2 %copy-start.98 = (f32[128]{0:T(128)}, f32[128]{0:T(128)S(1)}, u32[]{:S(2)}) copy-start(f32[128]{0:T(128)S(1)} %get-tuple-element.67) | copy-start | bytes 1540
  990.2 28.2 %copy-start.100 = (f32[128]{0:T(128)}, f32[128]{0:T(128)S(1)}, u32[]{:S(2)}) copy-start(f32[128]{0:T(128)S(1)} %get-tuple-element.68) | copy-start | bytes 1540
  996.4 221.9 %reduce-scatter.17.cloned.1.call-start = ((), (), s32[]{:S(2)}) async-start(), calls=%async_computation.10 | async-start | bytes 3932160 | tf_op jit(solution)/shard_map/reduce_scatter | solution.py:131
  998.8 19.5 %copy-start.58 = (bf16[1024,128]{1,0:T(8,128)(2,1)S(1)}, bf16[1024,128]{1,0:T(8,128)(2,1)}, u32[]{:S(2)}) copy-start(bf16[1024,128]{1,0:T(8,128)(2,1)} %param.18) | copy-start | bytes 786436
  1024.7 5.6 copy-start.82
  1024.7 6.1 copy-start.81
  1024.7 6.1 copy-start.84
  1024.7 6.1 copy-start.99
  (73 other events, 150.6 us)
Sparse Core Ops, SparseCore 0:
  10.9 31.6 all-gather.3
  86.6 17.5 all-gather.5
  313.3 19.5 all-gather.7
  514.2 17.4 reduce-scatter.18
  584.6 17.1 reduce-scatter.20
  634.5 27.7 reduce-scatter.14
  706.0 17.1 reduce-scatter.22
  935.3 24.4 reduce-scatter.24
  996.6 182.6 all-reduce.30
  1181.7 36.6 reduce-scatter.16
where the time goes:
time: 1250 us; the launch traced here: 1230 us
  blocking collectives  391 us (31%)
  local copies, waits for them, and re-layouts  380 us (30%)
  waiting for transfers between devices  302 us (24%)
  other arithmetic  70.7 us (6%)
  matrix products  65.8 us (5%)
  between operations  16.3 us (1%)
    psum x1, waiting for transfers between devices, on_device(): lax.psum(kern_one.astype(jnp.bfloat16), 'batch').astype(jnp.float32)  147 us
    psum x7, blocking collectives, norm_forward(): mean = lax.psum(jnp.sum(pre * mask, axis=(0, 1, 2)), 'batch') / count  139 us
    unnamed x240, local copies, waits for them, and re-layouts  137 us
    psum x6, blocking collectives, norm_backward(): lax.psum((jnp.sum(masked, axis=(0, 1, 2)), jnp.sum(masked * hat, axis=(0,...  128 us
    slice x11, local copies, waits for them, and re-layouts, convolve(): padded[:, top:top + stride * rows:stride, left:left + stride * cols:strid...  109 us
    psum x6, blocking collectives, norm_forward(): lax.psum(jnp.sum(centered * centered, axis=(0, 1, 2)), 'batch') / count  105 us
    pad x5, local copies, waits for them, and re-layouts, spread_back(): lax.pad(term, jnp.float32(0.0), ((0, 0, 0), (top, 2 * margin - top + stri...  79.7 us
    unnamed x14, waiting for transfers between devices  56.9 us
  transfers between devices with their start and end apart: 10, of which 9 were waited for; matrix products, arithmetic and copies ran while one was open for 7% of the time, Pallas kernels for 0%

commit v1 on v0

--- a/solution.py
+++ b/solution.py
@@ -1,9 +1,17 @@
+import functools
+import types
+
 import jax
 import jax.numpy as jnp
+import ml_dtypes
+import numpy as np
 from jax import lax
+from jax.experimental import pallas as pl
+from jax.experimental.pallas import tpu as pltpu
 from jax.sharding import PartitionSpec as P
 
 EPS = 1e-05
+VMEM_LIMIT = 60 * 1024 * 1024
 
 
 def shortened(shard):
@@ -304,6 +312,1050 @@
     )
 
 
+MESH = pl.DeviceIdType.MESH
+BF = jnp.bfloat16
+F32 = jnp.float32
+
+
+def flip(value, bit):
+    return value + bit - 2 * bit * lax.rem(lax.div(value, bit), 2)
+
+
+def gate(value):
+    return 0.5 * jnp.tanh(0.5 * value) + 0.5
+
+
+def tree(parts):
+    while len(parts) > 1:
+        parts = [parts[k] + parts[k + 1] for k in range(0, len(parts), 2)]
+    return parts[0]
+
+
+def wide_row(block):
+    return jnp.concatenate([block[j : j + 1] for j in range(block.shape[0])], axis=1)
+
+
+def fold(value):
+    return jnp.sum(value.reshape(value.shape[0] // 8, 8, value.shape[1]), axis=0)
+
+
+def mm(a, b):
+    return jnp.dot(a, b, preferred_element_type=F32)
+
+
+def mm_nt(a, b):
+    return lax.dot_general(a, b, (((1,), (1,)), ((), ())), preferred_element_type=F32)
+
+
+def mm_tn(a, b):
+    return lax.dot_general(a, b, (((0,), (0,)), ((), ())), preferred_element_type=F32)
+
+
+class Traffic:
+    def __init__(self, sems):
+        self.sems, self.used, self.sent = sems, 0, []
+
+    def take(self):
+        self.used += 1
+        return self.sems.at[self.used - 1]
+
+    def push(self, src, dst, device):
+        copy = pltpu.make_async_remote_copy(
+            src_ref=src,
+            dst_ref=dst,
+            send_sem=self.take(),
+            recv_sem=self.take(),
+            device_id=device,
+            device_id_type=MESH,
+        )
+        copy.start()
+        self.sent.append(copy)
+        return copy
+
+    def local(self, src, dst):
+        copy = pltpu.make_async_copy(src, dst, self.take())
+        copy.start()
+        return copy
+
+
+SEMS = 480
+
+
+def block_kernel(geo, names, *refs):
+    g = types.SimpleNamespace(**dict(zip(names, refs)))
+    R, QS, PS = geo.R, geo.QS, geo.PS
+    CI, MI, CO = geo.CI, geo.MI, geo.CO
+    NB = geo.NB
+    r = lax.axis_index("chan")
+    b = lax.axis_index("batch")
+    r1, r2 = flip(r, 1), flip(r, 2)
+    r3 = flip(r1, 2)
+    ranks = (r, r1, r2, r3)
+    core, far = (b, r1), (b, r2)
+    peers = []
+    for k in range(1, NB):
+        other = b
+        bit = 1
+        while bit < NB:
+            if k & bit:
+                other = flip(other, bit)
+            bit *= 2
+        peers.append((other, r))
+    net = Traffic(g.sems)
+
+    bar = pltpu.get_barrier_semaphore()
+    everyone = [core, far] + peers
+    for device in everyone:
+        pl.semaphore_signal(bar, 1, device_id=device, device_id_type=MESH)
+
+    def rows_of(ref, rank, size):
+        return ref.at[pl.ds(pl.multiple_of(rank * size, size), size)]
+
+    def taps_of(ref, rank, size):
+        return ref.at[:, pl.ds(pl.multiple_of(rank * size, size), size), :]
+
+    ld_src = net.local(g.src, g.SRC.at[0])
+    ld_w1 = [
+        net.local(rows_of(g.w1, rank, CI), g.W1C.at[pl.ds(s * CI, CI), pl.ds(MI, MI)])
+        for s, rank in enumerate((r, r1))
+    ]
+    ld_sc = [net.local(rows_of(g.wsc, rank, CI), g.WS.at[s]) for s, rank in enumerate(ranks)]
+    ld_w2 = [net.local(taps_of(g.w2, rank, MI), g.W2.at[:, s]) for s, rank in enumerate(ranks)]
+    ld_w3 = [net.local(rows_of(g.w3, rank, MI), g.W3.at[s]) for s, rank in enumerate(ranks)]
+    ld_w4 = [
+        net.local(rows_of(g.w4, rank, CO), g.W4C.at[pl.ds(s * CO, CO), pl.ds(MI, MI)])
+        for s, rank in enumerate((r, r1))
+    ]
+    ld_w5 = [net.local(taps_of(g.w5, rank, MI), g.W5.at[:, s]) for s, rank in enumerate(ranks)]
+    ld_w6 = [net.local(rows_of(g.w6, rank, MI), g.W6.at[s]) for s, rank in enumerate(ranks)]
+    ld_cot = net.local(g.cot, g.COT)
+
+    pl.semaphore_wait(bar, len(everyone))
+
+    rm_src = net.push(g.src, g.SRC.at[1], core)
+    rm_w1 = [
+        net.push(rows_of(g.w1, rank, CI), g.W1C.at[pl.ds(s * CI, CI), pl.ds(0, MI)], far)
+        for s, rank in enumerate((r2, r3))
+    ]
+    for ph in (1, 3):
+        for s in range(4):
+            g.F1[s, ph, 0:QS, :] = jnp.zeros((QS, MI), BF)
+    for s in range(4):
+        g.D1[1, s, 0:QS, :] = jnp.zeros((QS, MI), BF)
+        g.F4[s, 0:QS, :] = jnp.zeros((QS, MI), BF)
+        g.F4[s, QS + R :, :] = jnp.zeros((QS, MI), BF)
+        for d in range(2):
+            g.D4[d, s, 0:QS, :] = jnp.zeros((QS, MI), BF)
+            g.D4[d, s, QS + R :, :] = jnp.zeros((QS, MI), BF)
+    for d in range(3):
+        for s in range(2):
+            g.E5[d, s, 0:QS, :] = jnp.zeros((QS, MI), BF)
+            g.E5[d, s, QS + R :, :] = jnp.zeros((QS, MI), BF)
+    for d in range(2):
+        for s in range(2):
+            g.E2[d, s, R:, :] = jnp.zeros((QS, MI), BF)
+
+    ld_src.wait()
+    for copy in ld_w1:
+        copy.wait()
+    rm_src.wait_recv()
+    for copy in rm_w1:
+        copy.wait_recv()
+    rm_p1 = []
+    for ph in range(4):
+        span = slice(ph * R, (ph + 1) * R)
+        both = jnp.concatenate([g.SRC[0, span, :], g.SRC[1, span, :]], axis=1)
+        part = mm(both, g.W1C[...])
+        g.P1S[ph] = part[:, :MI].astype(BF)
+        rm_p1.append(net.push(g.P1S.at[ph], g.P1R.at[ph], far))
+        g.PRE1[span, :] = part[:, MI:]
+
+    rm_back = []
+    for s, rank in enumerate((r1, r3)):
+        rm_back.append(net.push(rows_of(g.w6, rank, MI), g.W6P.at[s], core))
+        rm_back.append(net.push(taps_of(g.w5, rank, MI), g.W5P.at[:, s], core))
+        rm_back.append(net.push(rows_of(g.w3, rank, MI), g.W3P.at[s], core))
+        rm_back.append(net.push(rows_of(g.wsc, rank, CI), g.WSP.at[s], core))
+        rm_back.append(net.push(taps_of(g.w2, rank, MI), g.W2P.at[:, s], core))
+    rm_back.append(net.push(rows_of(g.w4, r1, CO), g.W4P.at[0], core))
+    rm_back.append(net.push(rows_of(g.w1, r1, CI), g.W1P.at[0], core))
+    rm_back.append(
+        net.push(g.W1C.at[pl.ds(CI, CI), pl.ds(0, MI)], g.W1P.at[1], core)
+    )
+
+    aux = g.aux
+    inv_out = aux[16:17, :]
+    unb_out, unb_in = aux[17:18, :], aux[18:19, :]
+
+    def mask_rows(at, size):
+        return g.mask[pl.ds(at, size), :]
+
+    def over(total, size, body, init):
+        def step(i, carry):
+            return body(pl.multiple_of(i * size, size), carry)
+
+        return lax.fori_loop(0, total // size, step, init)
+
+    NCH = 128 if R % 128 == 0 else QS
+    WCH = QS
+
+    def bc(mask, width):
+        return jnp.concatenate([mask] * (width // 128), axis=1)
+
+    def exchange(slots, payload_rows):
+        return [net.push(slots.at[0], slots.at[k], peers[k - 1]) for k in range(1, NB)]
+
+    def narrow_local(pre, phases, prepare=None):
+        total = jnp.zeros((8, MI), F32)
+        for ph in range(phases):
+            if prepare is not None:
+                prepare(ph)
+
+            def add(at, acc, ph=ph):
+                return acc + fold(pre[pl.ds(ph * R + at, NCH), :] * mask_rows(at, NCH))
+
+            total = over(R, NCH, add, total)
+        total = jnp.sum(total, axis=0, keepdims=True)
+        mean = total * (aux[8:9, :] * (1.0 / phases))
+        squares = jnp.zeros((8, MI), F32)
+        for ph in range(phases):
+
+            def add2(at, acc, ph=ph):
+                d = (pre[pl.ds(ph * R + at, NCH), :] - mean) * mask_rows(at, NCH)
+                return acc + fold(d * d)
+
+            squares = over(R, NCH, add2, squares)
+        return total, jnp.sum(squares, axis=0, keepdims=True)
+
+    def narrow_send(idx, first, second):
+        slots = g.SN.at[idx]
+        g.SN[idx, 0, 0:1, :] = first
+        g.SN[idx, 0, 1:2, :] = second
+        return exchange(slots, 2)
+
+    def narrow_merge(idx, copies, phases):
+        for copy in copies:
+            copy.wait_recv()
+        sums = [g.SN[idx, k, 0:1, :] for k in range(NB)]
+        squares = [g.SN[idx, k, 1:2, :] for k in range(NB)]
+        return moments(sums, squares, phases)
+
+    def moments(sums, squares, phases):
+        inv_count = inv_out * (1.0 / phases)
+        mean = tree(list(sums)) * inv_count
+        terms = []
+        for k in range(NB):
+            d = sums[k] * (aux[8 + k : 9 + k, :] * (1.0 / phases)) - mean
+            terms.append(squares[k] + aux[k : k + 1, :] * float(phases) * d * d)
+        spread = tree(terms) * inv_count
+        return mean, spread
+
+    def wide_local(pre):
+        def add(at, acc):
+            m = bc(mask_rows(at, WCH), CO)
+            return acc + fold(pre[pl.ds(at, WCH), :] * m)
+
+        total = jnp.sum(over(R, WCH, add, jnp.zeros((8, CO), F32)), axis=0, keepdims=True)
+        mean = total * bc(aux[8:9, :], CO)
+
+        def add2(at, acc):
+            m = bc(mask_rows(at, WCH), CO)
+            d = (pre[pl.ds(at, WCH), :] - mean) * m
+            return acc + fold(d * d)
+
+        squares = jnp.sum(over(R, WCH, add2, jnp.zeros((8, CO), F32)), axis=0, keepdims=True)
+        return total, squares
+
+    NW = CO // 128
+
+    def wide_put(slots, row, value):
+        for j in range(NW):
+            slots[0, row + j : row + j + 1, :] = value[:, j * 128 : (j + 1) * 128]
+
+    def wide_send(idx, first, second):
+        slots = g.SW.at[idx]
+        wide_put(slots, 0, first)
+        wide_put(slots, NW, second)
+        return exchange(slots, 2 * NW)
+
+    def wide_merge(idx, copies):
+        for copy in copies:
+            copy.wait_recv()
+        sums = [g.SW[idx, k, 0:NW, :] for k in range(NB)]
+        squares = [g.SW[idx, k, NW : 2 * NW, :] for k in range(NB)]
+        mean, spread = moments(sums, squares, 1)
+        return wide_row(mean), wide_row(spread)
+
+    def gather(buf, at, size):
+        here = [buf(s).at[pl.ds(at, size)] for s in range(4)]
+        near = net.push(here[0], here[1], core)
+        away = net.push(here[0], here[2], far)
+        return [near, away, here]
+
+    def relay(chunk):
+        near, away, here = chunk
+        away.wait_recv()
+        chunk.append(net.push(here[2], here[3], core))
+
+    def landed(chunk):
+        chunk[0].wait_recv()
+        chunk[3].wait_recv()
+
+    def lanes(parts):
+        return jnp.concatenate(parts, axis=1)
+
+    place = lax.broadcasted_iota(jnp.int32, (QS, 128), 0)
+    keep_down = place >= PS
+    keep_up = place < QS - PS
+
+    def shifted(value, step):
+        if step < 0:
+            return jnp.where(keep_down, pltpu.roll(value, PS, 0), 0.0)
+        return jnp.where(keep_up, pltpu.roll(value, QS - PS, 0), 0.0)
+
+    def take_p1(ph):
+        rm_p1[ph].wait_recv()
+
+        def add(at, carry):
+            rows = pl.ds(ph * R + at, NCH)
+            g.PRE1[rows, :] = g.PRE1[rows, :] + g.P1R[ph, pl.ds(at, NCH), :].astype(F32)
+            return carry
+
+        over(R, NCH, add, 0)
+
+    sum_one, sq_one = narrow_local(g.PRE1, 4, take_p1)
+    st_one = narrow_send(0, sum_one, sq_one)
+    rm_xs = net.push(g.SRC.at[0, pl.ds(0, R)], g.XS.at[0], far)
+
+    def scale_of(spread, gain):
+        inv = lax.rsqrt(spread + EPS)
+        return inv, inv * gain
+
+    mean_one, spread_one = narrow_merge(0, st_one, 4)
+    inv_one, scale_one = scale_of(spread_one, g.gm[0:1, :])
+
+    def narrow_feature(pre, mean, scale, bias, out, ph, at0):
+        def body(at, carry):
+            v = (pre[pl.ds(ph * R + at, NCH), :] - mean) * scale + bias
+            out[pl.ds(at0 + at, NCH), :] = (v * gate(v) * mask_rows(at, NCH)).astype(BF)
+            return carry
+
+        over(R, NCH, body, 0)
+
+    ch_one = []
+    for ph in range(4):
+        narrow_feature(
+            g.PRE1, mean_one, scale_one, g.bm[0:1, :], g.F1.at[0, ph], ph, QS
+        )
+        ch_one.append(gather(lambda s, ph=ph: g.F1.at[s, ph], QS, R))
+
+    rm_xs.wait_recv()
+    rm_xs2 = net.push(g.XS.at[0], g.XS.at[1], core)
+    for copy in ld_sc:
+        copy.wait()
+    rm_xs2.wait_recv()
+
+    def strided():
+        return [g.SRC[0, 0:R, :], g.SRC[1, 0:R, :], g.XS[0], g.XS[1]]
+
+    pre_side = None
+    for s, block in enumerate(strided()):
+        term = mm(block, g.WS[s])
+        pre_side = term if pre_side is None else pre_side + term
+    g.PRES[...] = pre_side
+    st_side = wide_send(0, *wide_local(g.PRES))
+
+    for copy in ld_w2:
+        copy.wait()
+
+    def whole_one(ph, down, left):
+        rows = slice(0, R) if left else slice(QS, QS + R)
+        if down:
+            return lanes([g.D1[ph - 2, s, rows, :] for s in range(4)])
+        return lanes([g.F1[s, ph, rows, :] for s in range(4)])
+
+    def kernel_rows(ref, tap):
+        return jnp.concatenate([ref[tap, s] for s in range(4)], axis=0)
+
+    def taps_two(ph):
+        top = (1,) if ph < 2 else (0, 2)
+        left = (1,) if ph % 2 == 0 else (0, 2)
+        return [(t, l) for t in top for l in left]
+
+    relay(ch_one[0])
+    pre_two = None
+    for ph in range(4):
+        if ph < 3:
+            relay(ch_one[ph + 1])
+        landed(ch_one[ph])
+        if ph >= 2:
+
+            def move(at, carry, ph=ph):
+                for s in range(4):
+                    v = g.F1[s, ph, pl.ds(QS + at, QS), :].astype(F32)
+                    g.D1[ph - 2, s, pl.ds(QS + at, QS), :] = shifted(v, -1).astype(BF)
+                return carry
+
+            over(R, QS, move, 0)
+        for t, l in taps_two(ph):
+            term = mm(whole_one(ph, t == 0, l == 0), kernel_rows(g.W2, 3 * t + l))
+            pre_two = term if pre_two is None else pre_two + term
+    g.PRE2[...] = pre_two
+    rm_w4 = [
+        net.push(rows_of(g.w4, rank, CO), g.W4C.at[pl.ds(s * CO, CO), pl.ds(0, MI)], far)
+        for s, rank in enumerate((r2, r3))
+    ]
+    st_two = narrow_send(1, *narrow_local(g.PRE2, 1))
+    mean_two, spread_two = narrow_merge(1, st_two, 1)
+    inv_two, scale_two = scale_of(spread_two, g.gm[1:2, :])
+    narrow_feature(g.PRE2, mean_two, scale_two, g.bm[1:2, :], g.F2.at[0], 0, 0)
+    ch_two = gather(lambda s: g.F2.at[s], 0, R)
+    for copy in ld_w3:
+        copy.wait()
+    mean_side, spread_side = wide_merge(0, st_side)
+    inv_side, scale_side = scale_of(spread_side, g.go[1:2, :])
+    relay(ch_two)
+    landed(ch_two)
+
+    def four(ref):
+        return lanes([ref[s] for s in range(4)])
+
+    g.PRE3[...] = mm(four(g.F2), g.W3[...].reshape(4 * MI, CO))
+    st_three = wide_send(1, *wide_local(g.PRE3))
+    mean_three, spread_three = wide_merge(1, st_three)
+    inv_three, scale_three = scale_of(spread_three, g.go[0:1, :])
+    bias_three, bias_side = g.bo[0:1, :], g.bo[1:2, :]
+
+    def mid_value(rows):
+        return (
+            (g.PRE3[rows, :] - mean_three) * scale_three
+            + bias_three
+            + (g.PRES[rows, :] - mean_side) * scale_side
+            + bias_side
+        )
+
+    def mid_body(at, carry):
+        rows = pl.ds(at, WCH)
+        v = mid_value(rows)
+        out = v * gate(v) * bc(mask_rows(at, WCH), CO)
+        g.BM[rows, :] = out
+        g.MIDC[0, rows, :] = out.astype(BF)
+        return carry
+
+    over(R, WCH, mid_body, 0)
+    rm_mid = net.push(g.MIDC.at[0], g.MIDC.at[1], core)
+
+    for copy in ld_w4:
+        copy.wait()
+    for copy in rm_w4:
+        copy.wait_recv()
+    rm_back.append(net.push(g.W4C.at[pl.ds(CO, CO), pl.ds(0, MI)], g.W4P.at[1], core))
+    rm_mid.wait_recv()
+    part = mm(lanes([g.MIDC[0], g.MIDC[1]]), g.W4C[...])
+    g.P4S[...] = part[:, :MI].astype(BF)
+    rm_p4 = net.push(g.P4S, g.P4R, far)
+    g.PRE4[...] = part[:, MI:]
+
+    def take_p4(ph):
+        rm_p4.wait_recv()
+
+        def add(at, carry):
+            rows = pl.ds(at, NCH)
+            g.PRE4[rows, :] = g.PRE4[rows, :] + g.P4R[rows, :].astype(F32)
+            return carry
+
+        over(R, NCH, add, 0)
+
+    st_four = narrow_send(2, *narrow_local(g.PRE4, 1, take_p4))
+    mean_four, spread_four = narrow_merge(2, st_four, 1)
+    inv_four, scale_four = scale_of(spread_four, g.gm[2:3, :])
+    narrow_feature(g.PRE4, mean_four, scale_four, g.bm[2:3, :], g.F4.at[0], 0, QS)
+    ch_four = gather(lambda s: g.F4.at[s], QS, R)
+    for copy in ld_w5:
+        copy.wait()
+
+    def spread_rows(src, dst_up, dst_down):
+        def body(at, carry):
+            rows = pl.ds(QS + at, QS)
+            v = src[rows, :].astype(F32)
+            dst_up[rows, :] = shifted(v, -1).astype(BF)
+            dst_down[rows, :] = shifted(v, 1).astype(BF)
+            return carry
+
+        over(R, QS, body, 0)
+
+    def fill_four(s):
+        spread_rows(g.F4.at[s], g.D4.at[0, s], g.D4.at[1, s])
+
+    fill_four(0)
+    relay(ch_four)
+    ch_four[0].wait_recv()
+    fill_four(1)
+    fill_four(2)
+    ch_four[3].wait_recv()
+    fill_four(3)
+
+    def whole_four(t, l):
+        rows = slice(l * QS, l * QS + R)
+        if t == 1:
+            return lanes([g.F4[s, rows, :] for s in range(4)])
+        return lanes([g.D4[t // 2, s, rows, :] for s in range(4)])
+
+    pre_five = None
+    for t in range(3):
+        for l in range(3):
+            term = mm(whole_four(t, l), kernel_rows(g.W5, 3 * t + l))
+            pre_five = term if pre_five is None else pre_five + term
+    g.PRE5[...] = pre_five
+    st_five = narrow_send(3, *narrow_local(g.PRE5, 1))
+    mean_five, spread_five = narrow_merge(3, st_five, 1)
+    inv_five, scale_five = scale_of(spread_five, g.gm[3:4, :])
+    narrow_feature(g.PRE5, mean_five, scale_five, g.bm[3:4, :], g.F5.at[0], 0, 0)
+    ch_five = gather(lambda s: g.F5.at[s], 0, R)
+    for copy in ld_w6:
+        copy.wait()
+    ld_cot.wait()
+    relay(ch_five)
+    landed(ch_five)
+    g.PRE6[...] = mm(four(g.F5), g.W6[...].reshape(4 * MI, CO))
+    st_six = wide_send(2, *wide_local(g.PRE6))
+    mean_six, spread_six = wide_merge(2, st_six)
+    inv_six, scale_six = scale_of(spread_six, g.go[2:3, :])
+    bias_six = g.bo[2:3, :]
+
+    def last_body(at, carry):
+        acc_b, acc_g = carry
+        rows = pl.ds(at, WCH)
+        m = bc(mask_rows(at, WCH), CO)
+        hat = (g.PRE6[rows, :] - mean_six) * inv_six
+        v = (g.PRE6[rows, :] - mean_six) * scale_six + bias_six + g.BM[rows, :]
+        s = gate(v)
+        g.OUT[rows, :] = v * s * m
+        grad = g.COT[rows, :].astype(F32) * m * (s * (1.0 + v * (1.0 - s)))
+        g.GSB[rows, :] = grad
+        return acc_b + fold(grad), acc_g + fold(grad * hat)
+
+    zero_w = jnp.zeros((8, CO), F32)
+    acc_b, acc_g = over(R, WCH, last_body, (zero_w, zero_w))
+
+    def down(value):
+        return jnp.sum(value, axis=0, keepdims=True)
+
+    st = wide_send(3, down(acc_b), down(acc_g))
+
+    out = g.OUT[...]
+    high = out.astype(BF)
+    low = (out - high.astype(F32)).astype(BF)
+    g.OUTP[...] = mm(g.po[...], high) + mm(g.po[...], low)
+    out_block = net.local(g.OUTP, g.block_out)
+
+    def wide_sums(ref, copies, count):
+        for copy in copies:
+            copy.wait_recv()
+        return [
+            wide_row(tree([ref[k, j * NW : (j + 1) * NW, :] for k in range(NB)]))
+            for j in range(count)
+        ]
+
+    def narrow_sums(idx, copies):
+        for copy in copies:
+            copy.wait_recv()
+        return [tree([g.SN[idx, k, j : j + 1, :] for k in range(NB)]) for j in range(2)]
+
+    bsum_six, gsum_six = wide_sums(g.SW.at[3], st, 2)
+    inv_wide = bc(inv_out, CO)
+
+    def wide_pre_grad(grad, pre, mean, inv, scale, bsum, gsum, out):
+        mb, mg = bsum * inv_wide, gsum * inv_wide
+
+        def body(at, carry):
+            rows = pl.ds(at, WCH)
+            hat = (pre[rows, :] - mean) * inv
+            e = bc(mask_rows(at, WCH), CO) * scale * (grad[rows, :] - (mb + hat * mg))
+            out[rows, :] = e.astype(BF)
+            return carry
+
+        over(R, WCH, body, 0)
+
+    wide_pre_grad(
+        g.GSB, g.PRE6, mean_six, inv_six, scale_six, bsum_six, gsum_six, g.E6.at[0]
+    )
+    for copy in rm_back:
+        copy.wait_recv()
+
+    def swap(ref):
+        return net.push(ref.at[0], ref.at[1], core)
+
+    def reduce_back(part, sent, got):
+        sent[...] = part[:, MI:].astype(BF)
+        return net.push(sent, got, far)
+
+    def wide_back(e, own, other):
+        near = lanes([own[0], other[0]])
+        away = lanes([own[2], other[1]])
+        return mm_nt(lanes([e[0], e[1]]), jnp.concatenate([near, away], axis=0))
+
+    def narrow_back(idx, near, got, copy, phases, pre, mean, inv, scale, bias, order=None):
+        acc_b = jnp.zeros((8, MI), F32)
+        acc_g = jnp.zeros((8, MI), F32)
+        for ph in range(phases):
+            copy[ph].wait_recv()
+
+            def body(at, carry, ph=ph):
+                b_acc, g_acc = carry
+                rows = pl.ds(ph * R + at, NCH)
+                hat = (pre[rows, :] - mean) * inv
+                v = (pre[rows, :] - mean) * scale + bias
+                s = gate(v)
+                feat = near[rows, :] + got[rows, :].astype(F32)
+                grad = feat * mask_rows(at, NCH) * (s * (1.0 + v * (1.0 - s)))
+                near[rows, :] = grad
+                return b_acc + fold(grad), g_acc + fold(grad * hat)
+
+            acc_b, acc_g = over(R, NCH, body, (acc_b, acc_g))
+        return narrow_send(idx, down(acc_b), down(acc_g))
+
+    def narrow_pre_grad(grad, pre, mean, inv, scale, bsum, gsum, phases, ph, out, at0):
+        inv_count = inv_out * (1.0 / phases)
+        mb, mg = bsum * inv_count, gsum * inv_count
+
+        def body(at, carry):
+            rows = pl.ds(ph * R + at, NCH)
+            hat = (pre[rows, :] - mean) * inv
+            e = mask_rows(at, NCH) * scale * (grad[rows, :] - (mb + hat * mg))
+            out[pl.ds(at0 + at, NCH), :] = e.astype(BF)
+            return carry
+
+        over(R, NCH, body, 0)
+
+    outs = []
+
+    def give(src, dst):
+        outs.append(net.local(src, dst))
+
+    cp = swap(g.E6)
+    cp.wait_recv()
+    part = wide_back(g.E6, g.W6, g.W6P)
+    cp = [reduce_back(part, g.B5S, g.B5R)]
+    g.GF5[...] = part[:, :MI]
+    for s in range(4):
+        g.K6[s] = mm_tn(g.F5[s], g.E6[0]).astype(BF)
+        give(g.K6.at[s], rows_of(g.k6, ranks[s], MI))
+    st = narrow_back(
+        4, g.GF5, g.B5R, cp, 1, g.PRE5, mean_five, inv_five, scale_five, g.bm[3:4, :]
+    )
+    bsum_five, gsum_five = narrow_sums(4, st)
+    narrow_pre_grad(
+        g.GF5, g.PRE5, mean_five, inv_five, scale_five, bsum_five, gsum_five, 1, 0,
+        g.E5.at[1, 0], QS,
+    )
+    cp = net.push(g.E5.at[1, 0, pl.ds(QS, R)], g.E5.at[1, 1, pl.ds(QS, R)], core)
+    spread_rows(g.E5.at[1, 0], g.E5.at[0, 0], g.E5.at[2, 0])
+    cp.wait_recv()
+    spread_rows(g.E5.at[1, 1], g.E5.at[0, 1], g.E5.at[2, 1])
+
+    def taps_back(own, other, tap):
+        near = lanes([own[tap, 0], other[tap, 0]])
+        away = lanes([own[tap, 2], other[tap, 1]])
+        return jnp.concatenate([near, away], axis=0)
+
+    part = None
+    for t in range(3):
+        for l in range(3):
+            rows = slice((2 - l) * QS, (2 - l) * QS + R)
+            e = lanes([g.E5[2 - t, s, rows, :] for s in range(2)])
+            term = mm_nt(e, taps_back(g.W5, g.W5P, 3 * t + l))
+            part = term if part is None else part + term
+    cp = [reduce_back(part, g.B4S, g.B4R)]
+    g.GF4[...] = part[:, :MI]
+    own_five = g.E5[1, 0, QS : QS + R, :]
+    for t in range(3):
+        for l in range(3):
+            g.K5[3 * t + l] = mm_tn(whole_four(t, l), own_five).astype(BF)
+    for s in range(4):
+        give(g.K5.at[:, pl.ds(s * MI, MI), :], taps_of(g.k5, ranks[s], MI))
+    st = narrow_back(
+        5, g.GF4, g.B4R, cp, 1, g.PRE4, mean_four, inv_four, scale_four, g.bm[2:3, :]
+    )
+    bsum_four, gsum_four = narrow_sums(5, st)
+    narrow_pre_grad(
+        g.GF4, g.PRE4, mean_four, inv_four, scale_four, bsum_four, gsum_four, 1, 0,
+        g.G4.at[0], 0,
+    )
+    ch = gather(lambda s: g.G4.at[s], 0, R)
+    relay(ch)
+    landed(ch)
+    mid_back = mm_nt(
+        four(g.G4),
+        lanes([g.W4C[0:CO, MI:], g.W4P[0], g.W4C[0:CO, :MI], g.W4P[1]]),
+    )
+    g.GMID[...] = mid_back
+
+    def mid_back_body(at, carry):
+        a_b, a_3, a_s = carry
+        rows = pl.ds(at, WCH)
+        v = mid_value(rows)
+        s = gate(v)
+        grad = (g.GSB[rows, :] + g.GMID[rows, :]) * bc(mask_rows(at, WCH), CO)
+        grad = grad * (s * (1.0 + v * (1.0 - s)))
+        g.GMID[rows, :] = grad
+        hat3 = (g.PRE3[rows, :] - mean_three) * inv_three
+        hats = (g.PRES[rows, :] - mean_side) * inv_side
+        return a_b + fold(grad), a_3 + fold(grad * hat3), a_s + fold(grad * hats)
+
+    a_b, a_3, a_s = over(R, WCH, mid_back_body, (zero_w, zero_w, zero_w))
+    for j, value in enumerate((a_b, a_3, a_s, zero_w)):
+        wide_put(g.SA, j * NW, down(value))
+    st = exchange(g.SA, 4 * NW)
+    e4 = lanes([g.G4[0], g.G4[2]])
+    for s in range(2):
+        k4 = mm_tn(g.MIDC[s], e4)
+        g.K4[0, s] = k4[:, :MI].astype(BF)
+        g.K4[1, s] = k4[:, MI:].astype(BF)
+    cp_k4 = net.push(g.K4.at[1], g.K4R, far)
+    bsum_a, gsum_three, gsum_side = wide_sums(g.SA, st, 3)
+    wide_pre_grad(
+        g.GMID, g.PRE3, mean_three, inv_three, scale_three, bsum_a, gsum_three,
+        g.E3.at[0],
+    )
+    cp = swap(g.E3)
+    wide_pre_grad(
+        g.GMID, g.PRES, mean_side, inv_side, scale_side, bsum_a, gsum_side, g.ES.at[0]
+    )
+    cp_side = swap(g.ES)
+    cp.wait_recv()
+    part = wide_back(g.E3, g.W3, g.W3P)
+    cp = [reduce_back(part, g.B2S, g.B2R)]
+    g.GF2[...] = part[:, :MI]
+    for s in range(4):
+        g.K3[s] = mm_tn(g.F2[s], g.E3[0]).astype(BF)
+        give(g.K3.at[s], rows_of(g.k3, ranks[s], MI))
+    st = narrow_back(
+        6, g.GF2, g.B2R, cp, 1, g.PRE2, mean_two, inv_two, scale_two, g.bm[1:2, :]
+    )
+    cp_side.wait_recv()
+    es = lanes([g.ES[0], g.ES[1]])
+    g.IGS[...] = mm_nt(es, lanes([g.WS[0], g.WSP[0]]))
+    bsum_two, gsum_two = narrow_sums(6, st)
+    narrow_pre_grad(
+        g.GF2, g.PRE2, mean_two, inv_two, scale_two, bsum_two, gsum_two, 1, 0,
+        g.E2.at[0, 0], 0,
+    )
+    cp = net.push(g.E2.at[0, 0, pl.ds(0, R)], g.E2.at[0, 1, pl.ds(0, R)], core)
+
+    def lift(s):
+        def body(at, carry):
+            rows = pl.ds(at, QS)
+            v = g.E2[0, s, rows, :].astype(F32)
+            g.E2[1, s, rows, :] = shifted(v, 1).astype(BF)
+            return carry
+
+        over(R, QS, body, 0)
+
+    lift(0)
+    cp.wait_recv()
+    lift(1)
+    cp = []
+    for ph in range(4):
+        part = None
+        for t, l in taps_two(ph):
+            rows = slice(QS, QS + R) if l == 0 else slice(0, R)
+            e = lanes([g.E2[1 if t == 0 else 0, s, rows, :] for s in range(2)])
+            term = mm_nt(e, taps_back(g.W2, g.W2P, 3 * t + l))
+            part = term if part is None else part + term
+        cp.append(
+            reduce_back(part, g.B1S.at[pl.ds(ph * R, R)], g.B1R.at[pl.ds(ph * R, R)])
+        )
+        g.GF1[ph * R : (ph + 1) * R, :] = part[:, :MI]
+    own_two = g.E2[0, 0, 0:R, :]
+    for ph in range(4):
+        for t, l in taps_two(ph):
+            g.K2[3 * t + l] = mm_tn(whole_one(ph, t == 0, l == 0), own_two).astype(BF)
+    for s in range(4):
+        give(g.K2.at[:, pl.ds(s * MI, MI), :], taps_of(g.k2, ranks[s], MI))
+    st = narrow_back(
+        7, g.GF1, g.B1R, cp, 4, g.PRE1, mean_one, inv_one, scale_one, g.bm[0:1, :]
+    )
+    side_far = mm_nt(es, lanes([g.WS[2], g.WSP[1]]))
+    g.BSS[...] = side_far.astype(BF)
+    cp_bs = net.push(g.BSS, g.BSR, far)
+    bsum_one, gsum_one = narrow_sums(7, st)
+    ch = []
+    for ph in range(4):
+        narrow_pre_grad(
+            g.GF1, g.PRE1, mean_one, inv_one, scale_one, bsum_one, gsum_one, 4, ph,
+            g.G1.at[0, ph], 0,
+        )
+        ch.append(gather(lambda s, ph=ph: g.G1.at[s, ph], 0, R))
+    for s, block in enumerate(strided()):
+        g.KS[s] = mm_tn(block, g.ES[0]).astype(BF)
+        give(g.KS.at[s], rows_of(g.ks, ranks[s], CI))
+    w1_own = lanes([g.W1C[0:CI, MI:], g.W1P[0], g.W1C[0:CI, :MI], g.W1P[1]])
+    relay(ch[0])
+    for ph in range(4):
+        if ph < 3:
+            relay(ch[ph + 1])
+        landed(ch[ph])
+        whole = lanes([g.G1[s, ph] for s in range(4)])
+        g.IG[ph * R : (ph + 1) * R, :] = mm_nt(whole, w1_own)
+    cp_bs.wait_recv()
+    g.IG[0:R, :] = g.IG[0:R, :] + g.IGS[...] + g.BSR[...].astype(F32)
+    for a in range(2):
+        both = jnp.concatenate(
+            [
+                g.IG[(2 * a + h) * R : (2 * a + h + 1) * R, :] * bc(g.mask[...], CI)
+                for h in range(2)
+            ],
+            axis=0,
+        )
+        high = both.astype(BF)
+        low = (both - high.astype(F32)).astype(BF)
+        g.IGP[a] = (mm(g.pi[...], high) + mm(g.pi[...], low)).reshape(g.IGP.shape[1:])
+        give(g.IGP.at[a], g.images_grad.at[:, a])
+    for s in range(2):
+        k1 = None
+        for ph in range(4):
+            e1 = lanes([g.G1[0, ph], g.G1[2, ph]])
+            term = mm_tn(g.SRC[s, ph * R : (ph + 1) * R, :], e1)
+            k1 = term if k1 is None else k1 + term
+        g.K1[0, s] = k1[:, :MI].astype(BF)
+        g.K1[1, s] = k1[:, MI:].astype(BF)
+    cp_k1 = net.push(g.K1.at[1], g.K1R, far)
+    cp_k4.wait_recv()
+    cp_k1.wait_recv()
+    for s in range(2):
+        give(g.K4.at[0, s], rows_of(g.k4, ranks[s], CO))
+        give(g.K1.at[0, s], rows_of(g.k1, ranks[s], CI))
+        give(g.K4R.at[s], rows_of(g.k4, ranks[2 + s], CO))
+        give(g.K1R.at[s], rows_of(g.k1, ranks[2 + s], CI))
+
+    g.gain_mid_grad[...] = jnp.concatenate([gsum_one, gsum_two, gsum_four, gsum_five], axis=0)
+    g.bias_mid_grad[...] = jnp.concatenate([bsum_one, bsum_two, bsum_four, bsum_five], axis=0)
+    g.gain_out_grad[...] = jnp.concatenate([gsum_three, gsum_side, gsum_six], axis=0)
+    g.bias_out_grad[...] = jnp.concatenate([bsum_a, bsum_a, bsum_six], axis=0)
+    g.mean_mid[...] = jnp.concatenate([mean_one, mean_two, mean_four, mean_five], axis=0)
+    g.var_mid[...] = jnp.concatenate(
+        [spread_one * unb_in, spread_two * unb_out, spread_four * unb_out, spread_five * unb_out],
+        axis=0,
+    )
+    g.mean_out[...] = jnp.concatenate([mean_three, mean_side, mean_six], axis=0)
+    g.var_out[...] = jnp.concatenate([spread_three, spread_side, spread_six], axis=0) * bc(
+        unb_out, CO
+    )
+    out_block.wait()
+    for copy in outs:
+        copy.wait()
+    for copy in net.sent:
+        copy.wait_send()
+
+
+def fused_on_device(
+    images, heights, widths, reduce_first, spatial_first, expand_first, shortcut, reduce_second,
+    spatial_second, expand_second, gain_mid, bias_mid, gain_out, bias_out, cotangent,
+):
+    n, rows, cols, CO = cotangent.shape
+    CI, MI = images.shape[3], reduce_first.shape[1]
+    NB = heights.shape[0] // n
+    R, QS = n * rows * cols, n * rows
+    batch = lax.axis_index("batch")
+    valid = heights * widths
+    local_h = lax.dynamic_slice_in_dim(heights, batch * n, n)
+    local_w = lax.dynamic_slice_in_dim(widths, batch * n, n)
+    q, p, i = np.meshgrid(np.arange(cols), np.arange(rows), np.arange(n), indexing="ij")
+    q, p, i = (v.reshape(-1) for v in (q, p, i))
+    mask = (
+        (jnp.asarray(p)[:, None] < jnp.tile(local_h, rows * cols)[:, None])
+        & (jnp.asarray(q)[:, None] < jnp.tile(local_w, rows * cols)[:, None])
+    ).astype(F32)
+    where_out = (i * rows + p) * cols + q
+    pick_out = np.zeros((R, R), np.float32)
+    pick_out[np.arange(R), where_out] = 1.0
+    pick_in = np.zeros((2 * R, 2 * R), np.float32)
+    for h in range(2):
+        pick_in[h * R + np.arange(R), (i * rows + p) * 2 * cols + 2 * q + h] = 1.0
+    po = jnp.asarray(pick_out.T.astype(ml_dtypes.bfloat16))
+    pi = jnp.asarray(pick_in.T.astype(ml_dtypes.bfloat16))
+    mask_bf = mask.astype(BF)
+    cot = jnp.einsum(
+        "mk,kc->mc", po.T * mask_bf, cotangent.reshape(R, CO), preferred_element_type=F32
+    ).astype(BF)
+    parity = images.reshape(n, rows, 2, 2 * cols, CI).transpose(2, 0, 1, 3, 4).reshape(2, 2 * R, CI)
+    src = jnp.einsum(
+        "mk,akc->amc", pi.T * jnp.tile(mask_bf, (2, 1)), parity, preferred_element_type=F32
+    ).astype(BF).reshape(4 * R, CI)
+    order = np.arange(NB)
+    by_rank = jnp.sum(valid.reshape(NB, n), axis=1)
+    relative = jnp.take(by_rank, jnp.bitwise_xor(order, batch)).astype(F32)
+    count_out = jnp.sum(valid).astype(F32)
+    count_in = 4.0 * count_out
+    aux = jnp.concatenate(
+        [
+            relative,
+            1.0 / relative,
+            jnp.stack(
+                [1.0 / count_out, count_out / (count_out - 1.0), count_in / (count_in - 1.0)]
+            ),
+            jnp.zeros((5,), F32),
+        ]
+    )
+    aux = jnp.broadcast_to(aux[:, None], (24, 128))
+    ANY, VM = pl.BlockSpec(memory_space=pl.ANY), pl.BlockSpec(memory_space=pltpu.VMEM)
+    CM, MC = 4 * MI, 4 * CI
+    ins = dict(
+        src=(src, ANY),
+        cot=(cot, ANY),
+        w1=(reduce_first, ANY),
+        w2=(spatial_first.reshape(9, CM, MI), ANY),
+        w3=(expand_first, ANY),
+        wsc=(shortcut, ANY),
+        w4=(reduce_second, ANY),
+        w5=(spatial_second.reshape(9, CM, MI), ANY),
+        w6=(expand_second, ANY),
+        mask=(jnp.broadcast_to(mask, (R, 128)), VM),
+        aux=(aux, VM),
+        gm=(gain_mid, VM),
+        bm=(bias_mid, VM),
+        go=(gain_out, VM),
+        bo=(bias_out, VM),
+        po=(po, VM),
+        pi=(pi, VM),
+    )
+    outs = dict(
+        block_out=((R, CO), F32, ANY),
+        images_grad=((n * rows, 2, 2 * cols, CI), F32, ANY),
+        k1=((MC, MI), BF, ANY),
+        k2=((9, CM, MI), BF, ANY),
+        k3=((CM, CO), BF, ANY),
+        ks=((MC, CO), BF, ANY),
+        k4=((4 * CO, MI), BF, ANY),
+        k5=((9, CM, MI), BF, ANY),
+        k6=((CM, CO), BF, ANY),
+        gain_mid_grad=((4, MI), F32, VM),
+        bias_mid_grad=((4, MI), F32, VM),
+        gain_out_grad=((3, CO), F32, VM),
+        bias_out_grad=((3, CO), F32, VM),
+        mean_mid=((4, MI), F32, VM),
+        var_mid=((4, MI), F32, VM),
+        mean_out=((3, CO), F32, VM),
+        var_out=((3, CO), F32, VM),
+    )
+    NW = CO // 128
+    scratch = dict(
+        SRC=((2, 4 * R, CI), BF),
+        XS=((2, R, CI), BF),
+        W1C=((2 * CI, 2 * MI), BF),
+        W1P=((2, CI, MI), BF),
+        W2=((9, 4, MI, MI), BF),
+        W2P=((9, 2, MI, MI), BF),
+        W3=((4, MI, CO), BF),
+        W3P=((2, MI, CO), BF),
+        WS=((4, CI, CO), BF),
+        WSP=((2, CI, CO), BF),
+        W4C=((2 * CO, 2 * MI), BF),
+        W4P=((2, CO, MI), BF),
+        W5=((9, 4, MI, MI), BF),
+        W5P=((9, 2, MI, MI), BF),
+        W6=((4, MI, CO), BF),
+        W6P=((2, MI, CO), BF),
+        COT=((R, CO), BF),
+        P1S=((4, R, MI), BF),
+        P1R=((4, R, MI), BF),
+        P4S=((R, MI), BF),
+        P4R=((R, MI), BF),
+        PRE1=((4 * R, MI), F32),
+        PRE2=((R, MI), F32),
+        PRE3=((R, CO), F32),
+        PRES=((R, CO), F32),
+        PRE4=((R, MI), F32),
+        PRE5=((R, MI), F32),
+        PRE6=((R, CO), F32),
+        F1=((4, 4, QS + R, MI), BF),
+        D1=((2, 4, QS + R, MI), BF),
+        F2=((4, R, MI), BF),
+        BM=((R, CO), F32),
+        MIDC=((2, R, CO), BF),
+        F4=((4, R + 2 * QS, MI), BF),
+        D4=((2, 4, R + 2 * QS, MI), BF),
+        F5=((4, R, MI), BF),
+        OUT=((R, CO), F32),
+        OUTP=((R, CO), F32),
+        GSB=((R, CO), F32),
+        E6=((2, R, CO), BF),
+        B5S=((R, MI), BF),
+        B5R=((R, MI), BF),
+        GF5=((R, MI), F32),
+        E5=((3, 2, R + 2 * QS, MI), BF),
+        B4S=((R, MI), BF),
+        B4R=((R, MI), BF),
+        GF4=((R, MI), F32),
+        G4=((4, R, MI), BF),
+        GMID=((R, CO), F32),
+        E3=((2, R, CO), BF),
+        ES=((2, R, CO), BF),
+        B2S=((R, MI), BF),
+        B2R=((R, MI), BF),
+        GF2=((R, MI), F32),
+        E2=((2, 2, R + QS, MI), BF),
+        B1S=((4 * R, MI), BF),
+        B1R=((4 * R, MI), BF),
+        GF1=((4 * R, MI), F32),
+        G1=((4, 4, R, MI), BF),
+        IGS=((R, CI), F32),
+        BSS=((R, CI), BF),
+        BSR=((R, CI), BF),
+        IG=((4 * R, CI), F32),
+        IGP=((2, n * rows, 2 * cols, CI), F32),
+        K1=((2, 2, CI, MI), BF),
+        K1R=((2, CI, MI), BF),
+        K2=((9, CM, MI), BF),
+        K3=((4, MI, CO), BF),
+        KS=((4, CI, CO), BF),
+        K4=((2, 2, CO, MI), BF),
+        K4R=((2, CO, MI), BF),
+        K5=((9, CM, MI), BF),
+        K6=((4, MI, CO), BF),
+        SN=((8, NB, 2, MI), F32),
+        SW=((4, NB, 2 * NW, 128), F32),
+        SA=((NB, 4 * NW, 128), F32),
+    )
+    names = [*ins, *outs, *scratch, "sems"]
+    geo = types.SimpleNamespace(R=R, QS=QS, PS=n, CI=CI, MI=MI, CO=CO, NB=NB)
+    got = pl.pallas_call(
+        functools.partial(block_kernel, geo, names),
+        out_shape=[jax.ShapeDtypeStruct(s, d) for s, d, _ in outs.values()],
+        in_specs=[spec for _, spec in ins.values()],
+        out_specs=[spec for _, _, spec in outs.values()],
+        scratch_shapes=[pltpu.VMEM(s, d) for s, d in scratch.values()]
+        + [pltpu.SemaphoreType.DMA((SEMS,))],
+        compiler_params=pltpu.CompilerParams(
+            collective_id=0, has_side_effects=True, vmem_limit_bytes=VMEM_LIMIT
+        ),
+    )(*[value for value, _ in ins.values()])
+    o = types.SimpleNamespace(**dict(zip(outs, got)))
+    k1, k2, k3, ks, k4, k5, k6 = (
+        lax.psum(k, "batch").astype(F32) for k in (o.k1, o.k2, o.k3, o.ks, o.k4, o.k5, o.k6)
+    )
+    return (
+        o.block_out.reshape(n, rows, cols, CO),
+        o.images_grad.reshape(n, 2 * rows, 2 * cols, CI),
+        k1,
+        k2.reshape(3, 3, CM, MI),
+        k3,
+        ks,
+        k4,
+        k5.reshape(3, 3, CM, MI),
+        k6,
+        o.gain_mid_grad,
+        o.bias_mid_grad,
+        o.gain_out_grad,
+        o.bias_out_grad,
+        o.mean_mid,
+        o.var_mid,
+        o.mean_out,
+        o.var_out,
+    )
+
+
 def solution(mesh):
     in_specs = (
         P("batch", None, None, "chan"),
@@ -341,6 +1393,7 @@
         P(None, "chan"),
         P(None, "chan"),
     )
+    fused = mesh.shape["chan"] == 4 and mesh.shape["batch"] == 8
     return jax.shard_map(
-        on_device, mesh=mesh, in_specs=in_specs, out_specs=out_specs, check_vma=False
-    )
+        fused_on_device if fused else on_device, mesh=mesh, in_specs=in_specs, out_specs=out_specs, check_vma=False
+    )

time: 1250 us -> 399 us (0.32); the launches traced: 1230 us -> 398 us
  blocking collectives: 391 us -> 0 us
  local copies, waits for them, and re-layouts: 380 us -> 15.7 us
  Pallas kernels: 0 us -> 169 us
  waiting for transfers between devices: 302 us -> 183 us
  matrix products: 65.8 us -> 2.84 us
  other arithmetic: 70.7 us -> 12.7 us
    psum x19 -> x0, blocking collectives: 371 us -> none  [the longest x7 139 us: norm_forward(): mean = lax.psum(jnp.sum(pre * mask, axis=(0, 1, 2)), 'batch') / count]
    pallas_call x0 -> x1, Pallas kernels: none -> 169 us  [fused_on_device(): pl.pallas_call(functools.partial(block_kernel, geo, names), out_shape=[ja...]
    slice x17 -> x0, local copies, waits for them, and re-layouts: 161 us -> none  [the longest x11 109 us: convolve(): padded[:, top:top + stride * rows:stride, left:left + stride * cols:strid...]
    unnamed x240 -> x51, local copies, waits for them, and re-layouts: 137 us -> 10.3 us
    pad x6 -> x0, local copies, waits for them, and re-layouts: 82.2 us -> none  [the longest x5 79.7 us: spread_back(): lax.pad(term, jnp.float32(0.0), ((0, 0, 0), (top, 2 * margin - top + stri...]
    dot_general x69 -> x2, matrix products: 65.8 us -> 2.84 us  [the longest x1 1.69 us: fused_on_device(): jnp.einsum('mk,akc->amc', pi.T * jnp.tile(mask_bf, (2, 1)), parity, prefe...]
    unnamed x14 -> x1, waiting for transfers between devices: 56.9 us -> 0.02 us
    all_gather x3 -> x0, waiting for transfers between devices: 50.1 us -> none  [the longest x1 30.3 us: on_device(): whole_source = lax.all_gather(source, 'chan', axis=3, tiled=True)]
  transfers between devices with their start and end apart: 10 -> 1, of which waited for: 9 -> 1; matrix products, arithmetic and copies ran while one was open for 7% -> 0% of each run, Pallas kernels for 0% -> 0%
where the time goes in v1:
time: 399 us; the launch traced here: 398 us
  waiting for transfers between devices  183 us (46%)
  Pallas kernels  169 us (42%)
  local copies, waits for them, and re-layouts  15.7 us (4%)
  between operations  15 us (4%)
  other arithmetic  12.7 us (3%)
    psum x1, waiting for transfers between devices, fused_on_device(): lax.psum(k, 'batch').astype(F32)  183 us
    pallas_call x1, Pallas kernels, fused_on_device(): pl.pallas_call(functools.partial(block_kernel, geo, names), out_shape=[ja...  169 us
    unnamed x51, local copies, waits for them, and re-layouts  10.3 us
  transfers between devices with their start and end apart: 1, of which 1 were waited for; matrix products, arithmetic and copies ran while one was open for 0% of the time, Pallas kernels for 0%

profile of v1, /device:TPU:0, one launch (start us, length us, event | category | flops | bytes accessed | tf_op | source)
XLA Modules:
  0.0 398.4 jit_solution(15330211851172030579)
XLA Ops:
  7.2 0.0 copy-start.14
  7.2 0.0 copy-start.15
  7.2 0.0 all-reduce.3.cloned.1.call-start
  7.3 0.8 dynamic_slice.7
  8.0 0.7 dynamic_slice.6
  8.8 1.3 fusion.6
  10.1 1.2 copy.45
  11.3 0.0 copy-done.14
  11.3 0.1 and_convert_fusion
  11.4 0.1 copy.44
  11.5 0.1 reshape.115
  11.6 0.0 copy-start.9
  11.7 0.1 copy.47
  11.8 0.0 copy-start.2
  11.8 0.1 reshape.100
  11.9 0.1 reshape.103
  12.0 0.1 reduce_sum.18
  12.1 0.6 gather_fusion
  13.6 1.1 convolution_convert_fusion.1.refs_1_
  14.7 1.7 convolution_convert_fusion
  16.4 0.1 concatenate.3
  16.5 0.8 broadcast_in_dim.8.refs_9_
  17.3 0.7 broadcast_in_dim.10.refs_10_
  18.0 168.9 %shard_map.323 = (f32[384,512]{1,0:T(8,128)}, f32[32,2,24,256]{3,2,1,0:T(8,128)}, bf16[1024,128]{1,0:T(8,128)(2,1)}, bf16[9,512,128]{2,1,0:T(8,128)(2,1)}, bf16[...) custom-call(bf16[1536,256]{1,0:T(8,128)(2,1)} %bitcast.27, ...), custom_call_target="tpu_custom_call" | custom-call | tf_op jit(solution)/shard_map/pallas_call | solution.py:1323
  186.8 0.0 all-reduce.3.cloned.1.call-update
  186.9 1.1 copy-done.4
  188.0 0.1 reshape.104
  188.1 1.3 copy.48
  189.4 183.3 %all-reduce.3.cloned.1.call-done = (bf16[1024,128]{1,0:T(8,128)(2,1)}, bf16[3,3,512,128]{3,2,1,0:T(8,128)(2,1)}, bf16[512,512]{1,0:T(8,128)(2,1)}, bf16[1024,512...) async-done(((bf16[1024,128]{1,0:T(8,128)(2,1)}, bf16[3,3,512,128]{3,2,1,0:T(8,128)(2,1)}, ...) | async-done | bytes 5242896 | tf_op jit(solution)/shard_map/psum | solution.py:1336
  372.7 1.8 convert_element_type.47
  374.5 2.9 reshape.107
  377.4 1.1 convert_element_type.48
  378.5 0.5 copy-done.3
  379.0 1.6 convert_element_type.49
  380.6 1.0 convert_element_type.50
  381.7 0.6 copy-done.1
  382.3 1.6 reshape.109
  383.9 1.1 convert_element_type.51
  385.0 0.7 copy-done
  385.7 1.1 copy.67
  386.9 0.6 copy.68
  387.4 0.6 copy.69
  388.0 0.6 copy.70
  388.6 0.6 copy.71
  389.2 0.6 copy.72
  389.8 0.6 copy.73
  390.4 0.6 copy.74
  391.0 0.6 copy.75
  (38 shorter events, 0.1 us)
Async XLA Ops:
  7.2 4.1 %copy-start.14 = (s32[96,4]{0,1:T(4,128)S(1)}, s32[96,4]{0,1:T(4,128)}, u32[]{:S(2)}) copy-start(s32[96,4]{0,1:T(4,128)} %constant.54) | copy-start | bytes 4612
  7.2 4.1 %copy-start.15 = (s32[96,4]{0,1:T(4,128)S(1)}, s32[96,4]{0,1:T(4,128)}, u32[]{:S(2)}) copy-start(s32[96,4]{0,1:T(4,128)} %constant.53) | copy-start | bytes 4612
  7.2 4.4 %copy-start.8 = (bf16[4,8,12,512]{3,1,2,0:T(8,128)(2,1)S(1)}, bf16[4,8,12,512]{3,1,2,0:T(8,128)(2,1)}, u32[]{:S(2)}) copy-start(bf16[4,8,12,512]{3,1,2,0:T(8,128)(2,1)} %param.34) | copy-start | bytes 1179652
  7.2 365.5 %all-reduce.3.cloned.1.call-start = ((), (), s32[]{:S(2)}) async-start(), calls=%async_computation | async-start | bytes 10485760 | tf_op jit(solution)/shard_map/psum | solution.py:1336
  11.6 1.9 copy-start.9
  11.8 2.9 copy-start.2
  186.8 1.1 copy-start.4
  374.5 2.9 copy-start.7
  377.4 1.6 copy-start.3
  379.0 1.6 copy-start.6
  380.6 1.6 copy-start.1
  382.3 1.6 copy-start.5
  383.9 1.8 copy-start
  385.7 1.2 copy-start.19
  385.7 1.8 copy-start.18
  385.7 2.4 copy-start.13
  385.7 3.0 copy-start.12
  385.7 3.6 copy-start.17
  385.7 4.1 %copy-start.16 = (f32[4,128]{1,0:T(4,128)S(1)}, f32[4,128]{1,0:T(4,128)}, u32[]{:S(2)}) copy-start(f32[4,128]{1,0:T(4,128)} %get-tuple-element.144) | copy-start | bytes 6148
  385.7 4.7 %copy-start.11 = (f32[3,512]{1,0:T(4,128)S(1)}, f32[3,512]{1,0:T(4,128)}, u32[]{:S(2)}) copy-start(f32[3,512]{1,0:T(4,128)} %get-tuple-element.145) | copy-start | bytes 18436
  385.7 5.3 %copy-start.10 = (f32[3,512]{1,0:T(4,128)S(1)}, f32[3,512]{1,0:T(4,128)}, u32[]{:S(2)}) copy-start(f32[3,512]{1,0:T(4,128)} %get-tuple-element.146) | copy-start | bytes 18436
Sparse Core Ops, SparseCore 0:
  187.0 185.6 all-reduce.2

commit v2 on v1

--- a/solution.py
+++ b/solution.py
@@ -378,7 +378,68 @@
         return copy
 
 
-SEMS = 480
+class Summed:
+    def __init__(self, net, part, got, done, coords, across=None):
+        self.net, self.part, self.got, self.done = net, part, got, done
+        (self.i0, self.p0), (self.i1, self.p1), (self.i2, self.p2) = coords
+        self.across = across
+        self.todo = [self.halves, self.quarters, self.eighths, self.finish]
+        if across is not None:
+            self.todo.append(self.crossed)
+        self.todo += [self.pairs, self.fours, self.last]
+
+    def step(self):
+        self.todo.pop(0)()
+
+    def halves(self):
+        self.copy = self.net.push(self.part.at[:, :, 1 - self.i0], self.got[0], self.p0)
+
+    def quarters(self):
+        self.copy.wait_recv()
+        for k in range(2):
+            for j in range(2):
+                self.got[0][k, j] = self.got[0][k, j] + self.part[k, j, self.i0]
+        self.copy = self.net.push(self.got[0].at[:, 1 - self.i1], self.got[1], self.p1)
+
+    def eighths(self):
+        self.copy.wait_recv()
+        for k in range(2):
+            self.got[1][k] = self.got[1][k] + self.got[0][k, self.i1]
+        self.copy = self.net.push(self.got[1].at[1 - self.i2], self.got[2], self.p2)
+
+    def mine(self):
+        return self.done.at[self.i2, self.i1, self.i0]
+
+    def finish(self):
+        self.copy.wait_recv()
+        total = self.got[2][...] + self.got[1][self.i2]
+        if self.across is None:
+            self.done[self.i2, self.i1, self.i0] = total
+            self.copy = self.net.push(self.mine(), self.mine(), self.p2)
+        else:
+            self.done[self.i2, self.i1, self.i0, 0] = total[0]
+            self.got[2][1] = total[1]
+            self.copy = self.net.push(self.got[2].at[1], self.mine().at[1], self.across)
+
+    def crossed(self):
+        self.copy.wait_recv()
+        self.copy = self.net.push(self.mine(), self.mine(), self.p2)
+
+    def pairs(self):
+        self.copy.wait_recv()
+        block = self.done.at[:, self.i1, self.i0]
+        self.copy = self.net.push(block, block, self.p1)
+
+    def fours(self):
+        self.copy.wait_recv()
+        block = self.done.at[:, :, self.i0]
+        self.copy = self.net.push(block, block, self.p0)
+
+    def last(self):
+        self.copy.wait_recv()
+
+
+SEMS = 700
 
 
 def block_kernel(geo, names, *refs):
@@ -402,6 +463,10 @@
             bit *= 2
         peers.append((other, r))
     net = Traffic(g.sems)
+    x_way = (lax.rem(b, 2), (flip(b, 1), r))
+    z_way = (lax.rem(lax.div(b, 2), 2), (flip(b, 2), r))
+    s_way = (lax.div(b, 4), (flip(b, 4), r))
+    x_first, z_first = (x_way, z_way, s_way), (z_way, x_way, s_way)
 
     bar = pltpu.get_barrier_semaphore()
     everyone = [core, far] + peers
@@ -938,9 +1003,27 @@
     part = wide_back(g.E6, g.W6, g.W6P)
     cp = [reduce_back(part, g.B5S, g.B5R)]
     g.GF5[...] = part[:, :MI]
+    def rows_grad(part, value, s):
+        half = value.shape[0] // 2
+        for h in range(2):
+            part[s // 2, s % 2, h] = value[h * half : (h + 1) * half].astype(BF)
+
+    def taps_grad(part, tap, value):
+        half = MI // 2
+        for p in range(8):
+            part[p // 4, p // 2 % 2, p % 2, tap] = value[p * half : (p + 1) * half].astype(BF)
+
+    def job(part, got, done, coords, across=None):
+        work = Summed(net, part, got, done, coords, across)
+        jobs.append(work)
+        return work
+
+    jobs = []
+
     for s in range(4):
-        g.K6[s] = mm_tn(g.F5[s], g.E6[0]).astype(BF)
-        give(g.K6.at[s], rows_of(g.k6, ranks[s], MI))
+        rows_grad(g.K6, mm_tn(g.F5[s], g.E6[0]), s)
+    six = job(g.K6, (g.K6X, g.K6Z, g.K6E), g.A6, x_first)
+    six.step()
     st = narrow_back(
         4, g.GF5, g.B5R, cp, 1, g.PRE5, mean_five, inv_five, scale_five, g.bm[3:4, :]
     )
@@ -968,12 +1051,19 @@
             part = term if part is None else part + term
     cp = [reduce_back(part, g.B4S, g.B4R)]
     g.GF4[...] = part[:, :MI]
+    six.step()
     own_five = g.E5[1, 0, QS : QS + R, :]
-    for t in range(3):
-        for l in range(3):
-            g.K5[3 * t + l] = mm_tn(whole_four(t, l), own_five).astype(BF)
-    for s in range(4):
-        give(g.K5.at[:, pl.ds(s * MI, MI), :], taps_of(g.k5, ranks[s], MI))
+
+    def five_grad(part, first, last):
+        for tap in range(first, last):
+            taps_grad(part, tap - first, mm_tn(whole_four(tap // 3, tap % 3), own_five))
+
+    five_grad(g.K5A, 0, 5)
+    five_a = job(g.K5A, (g.K5AX, g.K5AZ, g.K5AE), g.A5A, x_first)
+    five_a.step()
+    five_grad(g.K5B, 5, 9)
+    five_b = job(g.K5B, (g.K5BX, g.K5BZ, g.K5BE), g.A5B, z_first)
+    five_b.step()
     st = narrow_back(
         5, g.GF4, g.B4R, cp, 1, g.PRE4, mean_four, inv_four, scale_four, g.bm[2:3, :]
     )
@@ -984,6 +1074,7 @@
     )
     ch = gather(lambda s: g.G4.at[s], 0, R)
     relay(ch)
+    six.step()
     landed(ch)
     mid_back = mm_nt(
         four(g.G4),
@@ -1008,11 +1099,19 @@
         wide_put(g.SA, j * NW, down(value))
     st = exchange(g.SA, 4 * NW)
     e4 = lanes([g.G4[0], g.G4[2]])
+
+    def chip_grad(part, s, value):
+        size = value.shape[0] // 4
+        for p in range(4):
+            for w in range(2):
+                block = value[p * size : (p + 1) * size, w * MI : (w + 1) * MI]
+                part[s, p // 2, p % 2, w] = block.astype(BF)
+
     for s in range(2):
-        k4 = mm_tn(g.MIDC[s], e4)
-        g.K4[0, s] = k4[:, :MI].astype(BF)
-        g.K4[1, s] = k4[:, MI:].astype(BF)
-    cp_k4 = net.push(g.K4.at[1], g.K4R, far)
+        chip_grad(g.K4, s, mm_tn(g.MIDC[s], e4))
+    four_w = job(g.K4, (g.K4X, g.K4Z, g.K4E), g.A4, x_first, far)
+    five_b.step()
+    four_w.step()
     bsum_a, gsum_three, gsum_side = wide_sums(g.SA, st, 3)
     wide_pre_grad(
         g.GMID, g.PRE3, mean_three, inv_three, scale_three, bsum_a, gsum_three,
@@ -1027,15 +1126,24 @@
     part = wide_back(g.E3, g.W3, g.W3P)
     cp = [reduce_back(part, g.B2S, g.B2R)]
     g.GF2[...] = part[:, :MI]
+    six.step()
+    five_a.step()
     for s in range(4):
-        g.K3[s] = mm_tn(g.F2[s], g.E3[0]).astype(BF)
-        give(g.K3.at[s], rows_of(g.k3, ranks[s], MI))
+        rows_grad(g.K3, mm_tn(g.F2[s], g.E3[0]), s)
+    three_w = job(g.K3, (g.K3X, g.K3Z, g.K3E), g.A3, x_first)
+    three_w.step()
     st = narrow_back(
         6, g.GF2, g.B2R, cp, 1, g.PRE2, mean_two, inv_two, scale_two, g.bm[1:2, :]
     )
     cp_side.wait_recv()
     es = lanes([g.ES[0], g.ES[1]])
     g.IGS[...] = mm_nt(es, lanes([g.WS[0], g.WSP[0]]))
+    half = CO // 2
+    for s, block in enumerate(strided()):
+        grad = mm_tn(block, g.ES[0])
+        rows_grad(g.KSA, grad[:, :half], s)
+        rows_grad(g.KSB, grad[:, half:], s)
+    five_b.step()
     bsum_two, gsum_two = narrow_sums(6, st)
     narrow_pre_grad(
         g.GF2, g.PRE2, mean_two, inv_two, scale_two, bsum_two, gsum_two, 1, 0,
@@ -1067,12 +1175,30 @@
             reduce_back(part, g.B1S.at[pl.ds(ph * R, R)], g.B1R.at[pl.ds(ph * R, R)])
         )
         g.GF1[ph * R : (ph + 1) * R, :] = part[:, :MI]
+    side_a = job(g.KSA, (g.KSAX, g.KSAZ, g.KSAE), g.ASA, x_first)
+    side_a.step()
+    side_b = job(g.KSB, (g.KSBX, g.KSBZ, g.KSBE), g.ASB, z_first)
+    side_b.step()
+    six.step()
+    five_a.step()
+    four_w.step()
+    five_b.step()
     own_two = g.E2[0, 0, 0:R, :]
-    for ph in range(4):
-        for t, l in taps_two(ph):
-            g.K2[3 * t + l] = mm_tn(whole_one(ph, t == 0, l == 0), own_two).astype(BF)
-    for s in range(4):
-        give(g.K2.at[:, pl.ds(s * MI, MI), :], taps_of(g.k2, ranks[s], MI))
+
+    def two_grad(part, first, last):
+        for ph in range(4):
+            for t, l in taps_two(ph):
+                tap = 3 * t + l
+                if first <= tap < last:
+                    grad = mm_tn(whole_one(ph, t == 0, l == 0), own_two)
+                    taps_grad(part, tap - first, grad)
+
+    two_grad(g.K2A, 0, 5)
+    two_grad(g.K2B, 5, 9)
+    three_w.step()
+    six.step()
+    five_a.step()
+    four_w.step()
     st = narrow_back(
         7, g.GF1, g.B1R, cp, 4, g.PRE1, mean_one, inv_one, scale_one, g.bm[0:1, :]
     )
@@ -1087,17 +1213,32 @@
             g.G1.at[0, ph], 0,
         )
         ch.append(gather(lambda s, ph=ph: g.G1.at[s, ph], 0, R))
-    for s, block in enumerate(strided()):
-        g.KS[s] = mm_tn(block, g.ES[0]).astype(BF)
-        give(g.KS.at[s], rows_of(g.ks, ranks[s], CI))
+    two_a = job(g.K2A, (g.K2AX, g.K2AZ, g.K2AE), g.A2A, x_first)
+    two_a.step()
+    two_b = job(g.K2B, (g.K2BX, g.K2BZ, g.K2BE), g.A2B, z_first)
+    two_b.step()
     w1_own = lanes([g.W1C[0:CI, MI:], g.W1P[0], g.W1C[0:CI, :MI], g.W1P[1]])
     relay(ch[0])
     for ph in range(4):
         if ph < 3:
             relay(ch[ph + 1])
         landed(ch[ph])
+        side_b.step() if ph == 1 else None
+        side_a.step() if ph == 2 else None
+        five_b.step() if ph == 3 else None
         whole = lanes([g.G1[s, ph] for s in range(4)])
         g.IG[ph * R : (ph + 1) * R, :] = mm_nt(whole, w1_own)
+    for s in range(2):
+        k1 = None
+        for ph in range(4):
+            e1 = lanes([g.G1[0, ph], g.G1[2, ph]])
+            term = mm_tn(g.SRC[s, ph * R : (ph + 1) * R, :], e1)
+            k1 = term if k1 is None else k1 + term
+        chip_grad(g.K1, s, k1)
+    one_w = job(g.K1, (g.K1X, g.K1Z, g.K1E), g.A1, x_first, far)
+    one_w.step()
+    three_w.step()
+    six.step()
     cp_bs.wait_recv()
     g.IG[0:R, :] = g.IG[0:R, :] + g.IGS[...] + g.BSR[...].astype(F32)
     for a in range(2):
@@ -1112,22 +1253,27 @@
         low = (both - high.astype(F32)).astype(BF)
         g.IGP[a] = (mm(g.pi[...], high) + mm(g.pi[...], low)).reshape(g.IGP.shape[1:])
         give(g.IGP.at[a], g.images_grad.at[:, a])
-    for s in range(2):
-        k1 = None
-        for ph in range(4):
-            e1 = lanes([g.G1[0, ph], g.G1[2, ph]])
-            term = mm_tn(g.SRC[s, ph * R : (ph + 1) * R, :], e1)
-            k1 = term if k1 is None else k1 + term
-        g.K1[0, s] = k1[:, :MI].astype(BF)
-        g.K1[1, s] = k1[:, MI:].astype(BF)
-    cp_k1 = net.push(g.K1.at[1], g.K1R, far)
-    cp_k4.wait_recv()
-    cp_k1.wait_recv()
-    for s in range(2):
-        give(g.K4.at[0, s], rows_of(g.k4, ranks[s], CO))
-        give(g.K1.at[0, s], rows_of(g.k1, ranks[s], CI))
-        give(g.K4R.at[s], rows_of(g.k4, ranks[2 + s], CO))
-        give(g.K1R.at[s], rows_of(g.k1, ranks[2 + s], CI))
+    while any(work.todo for work in jobs):
+        for work in jobs:
+            if work.todo:
+                work.step()
+    for s in range(4):
+        for done, out in ((g.A6, g.k6), (g.A3, g.k3)):
+            give(done.at[s // 2, s % 2], out.at[ranks[s]])
+        for w, done in enumerate((g.ASA, g.ASB)):
+            give(done.at[s // 2, s % 2], g.ks.at[ranks[s], :, :, pl.ds(w * half, half)])
+        for h in range(2):
+            for done, out, first, last in (
+                (g.A5A, g.k5, 0, 5),
+                (g.A5B, g.k5, 5, 9),
+                (g.A2A, g.k2, 0, 5),
+                (g.A2B, g.k2, 5, 9),
+            ):
+                give(done.at[s // 2, s % 2, h], out.at[pl.ds(first, last - first), ranks[s], h])
+    for done, out in ((g.A4, g.k4), (g.A1, g.k1)):
+        for s in range(2):
+            for w in range(2):
+                give(done.at[s, :, :, w], out.at[ranks[2 * w + s]])
 
     g.gain_mid_grad[...] = jnp.concatenate([gsum_one, gsum_two, gsum_four, gsum_five], axis=0)
     g.bias_mid_grad[...] = jnp.concatenate([bsum_one, bsum_two, bsum_four, bsum_five], axis=0)
@@ -1223,13 +1369,13 @@
     outs = dict(
         block_out=((R, CO), F32, ANY),
         images_grad=((n * rows, 2, 2 * cols, CI), F32, ANY),
-        k1=((MC, MI), BF, ANY),
-        k2=((9, CM, MI), BF, ANY),
-        k3=((CM, CO), BF, ANY),
-        ks=((MC, CO), BF, ANY),
-        k4=((4 * CO, MI), BF, ANY),
-        k5=((9, CM, MI), BF, ANY),
-        k6=((CM, CO), BF, ANY),
+        k1=((4, 2, 2, CI // 4, MI), BF, ANY),
+        k2=((9, 4, 2, MI // 2, MI), BF, ANY),
+        k3=((4, 2, MI // 2, CO), BF, ANY),
+        ks=((4, 2, CI // 2, CO), BF, ANY),
+        k4=((4, 2, 2, CO // 4, MI), BF, ANY),
+        k5=((9, 4, 2, MI // 2, MI), BF, ANY),
+        k6=((4, 2, MI // 2, CO), BF, ANY),
         gain_mid_grad=((4, MI), F32, VM),
         bias_mid_grad=((4, MI), F32, VM),
         gain_out_grad=((3, CO), F32, VM),
@@ -1305,19 +1451,27 @@
         BSR=((R, CI), BF),
         IG=((4 * R, CI), F32),
         IGP=((2, n * rows, 2 * cols, CI), F32),
-        K1=((2, 2, CI, MI), BF),
-        K1R=((2, CI, MI), BF),
-        K2=((9, CM, MI), BF),
-        K3=((4, MI, CO), BF),
-        KS=((4, CI, CO), BF),
-        K4=((2, 2, CO, MI), BF),
-        K4R=((2, CO, MI), BF),
-        K5=((9, CM, MI), BF),
-        K6=((4, MI, CO), BF),
         SN=((8, NB, 2, MI), F32),
         SW=((4, NB, 2 * NW, 128), F32),
         SA=((NB, 4 * NW, 128), F32),
     )
+    for name, piece in dict(
+        K1=(2, CI // 4, MI),
+        K2A=(5, MI // 2, MI),
+        K2B=(4, MI // 2, MI),
+        K3=(MI // 2, CO),
+        KSA=(CI // 2, CO // 2),
+        KSB=(CI // 2, CO // 2),
+        K4=(2, CO // 4, MI),
+        K5A=(5, MI // 2, MI),
+        K5B=(4, MI // 2, MI),
+        K6=(MI // 2, CO),
+    ).items():
+        scratch[name] = ((2, 2, 2, *piece), BF)
+        scratch[name + "X"] = ((2, 2, *piece), BF)
+        scratch[name + "Z"] = ((2, *piece), BF)
+        scratch[name + "E"] = (piece, BF)
+        scratch["A" + name[1:]] = ((2, 2, 2, *piece), BF)
     names = [*ins, *outs, *scratch, "sems"]
     geo = types.SimpleNamespace(R=R, QS=QS, PS=n, CI=CI, MI=MI, CO=CO, NB=NB)
     got = pl.pallas_call(
@@ -1333,18 +1487,18 @@
     )(*[value for value, _ in ins.values()])
     o = types.SimpleNamespace(**dict(zip(outs, got)))
     k1, k2, k3, ks, k4, k5, k6 = (
-        lax.psum(k, "batch").astype(F32) for k in (o.k1, o.k2, o.k3, o.ks, o.k4, o.k5, o.k6)
+        k.astype(F32) for k in (o.k1, o.k2, o.k3, o.ks, o.k4, o.k5, o.k6)
     )
     return (
         o.block_out.reshape(n, rows, cols, CO),
         o.images_grad.reshape(n, 2 * rows, 2 * cols, CI),
-        k1,
+        k1.reshape(MC, MI),
         k2.reshape(3, 3, CM, MI),
-        k3,
-        ks,
-        k4,
+        k3.reshape(CM, CO),
+        ks.reshape(MC, CO),
+        k4.reshape(4 * CO, MI),
         k5.reshape(3, 3, CM, MI),
-        k6,
+        k6.reshape(CM, CO),
         o.gain_mid_grad,
         o.bias_mid_grad,
         o.gain_out_grad,

time: 399 us -> 281 us (0.70)
  waiting for transfers between devices: 183 us -> 0 us
  Pallas kernels: 169 us -> 251 us
  between operations: 15 us -> 1.64 us
    psum x1 -> x0, waiting for transfers between devices: 183 us -> none  [fused_on_device(): lax.psum(k, 'batch').astype(F32)]
    pallas_call x1, Pallas kernels: 169 us -> 251 us  [fused_on_device(): pl.pallas_call(functools.partial(block_kernel, geo, names), out_shape=[ja...]
    convert_element_type x5 -> x0, other arithmetic: 6.62 us -> none  [fused_on_device(): lax.psum(k, 'batch').astype(F32)]
    reshape x0 -> x4, other arithmetic: none -> 6.5 us  [the longest x1 2.9 us: fused_on_device(): k6.reshape(CM, CO)]
    unnamed x51 -> x47, local copies, waits for them, and re-layouts: 10.3 us -> 8.17 us
  transfers between devices with their start and end apart: 1 -> 0, of which waited for: 1 -> 0; matrix products, arithmetic and copies ran while one was open for 0% -> 0% of each run, Pallas kernels for 0% -> 0%
where the time goes in v2:
time: 281 us
  Pallas kernels  251 us (89%)
  local copies, waits for them, and re-layouts  13.5 us (5%)
  other arithmetic  12 us (4%)
  matrix products  2.84 us (1%)
    pallas_call x1, Pallas kernels, fused_on_device(): pl.pallas_call(functools.partial(block_kernel, geo, names), out_shape=[ja...  251 us
    unnamed x47, local copies, waits for them, and re-layouts  8.17 us

profile of v2, /device:TPU:0, one launch (start us, length us, event | category | flops | bytes accessed | tf_op | source)
XLA Modules:
  0.0 281.0 jit_solution(11251564786499722999)
XLA Ops:
  0.7 0.0 copy-start.3
  0.7 1.4 fusion.6
  2.8 0.1 reshape.133
  2.9 0.1 reduce_sum.18
  3.0 0.6 gather_fusion
  3.8 0.1 concatenate.3
  3.9 0.7 broadcast_in_dim.10.refs_10_
  4.5 0.7 dynamic_slice.6
  5.3 0.7 dynamic_slice.7
  6.0 0.8 and_convert_fusion
  6.8 0.1 copy.44
  6.9 0.1 reshape.169
  7.0 1.2 copy.45
  8.2 0.0 copy-start.7
  8.2 1.7 convolution_convert_fusion
  9.9 0.1 copy.47
  10.1 0.1 reshape.130
  10.2 0.7 copy-done.8
  10.9 1.1 convolution_convert_fusion.1.refs_1_
  12.0 0.8 broadcast_in_dim.8.refs_9_
  12.8 251.0 %shard_map.323 = (f32[384,512]{1,0:T(8,128)}, f32[32,2,24,256]{3,2,1,0:T(8,128)}, bf16[4,2,2,64,128]{4,3,2,1,0:T(8,128)(2,1)}, bf16[9,4,2,64,128]{4,3,2,1,0:T(8,...) custom-call(bf16[1536,256]{1,0:T(8,128)(2,1)} %bitcast.44, ...), custom_call_target="tpu_custom_call" | custom-call | tf_op jit(solution)/shard_map/pallas_call | solution.py:1477
  263.8 0.0 copy-start.2
  263.9 2.9 %bitcast_convert_fusion.1 = (f32[512,512]{1,0:T(8,128)}, f32[512,512]{1,0:T(8,128)}) fusion(bf16[4,2,64,512]{3,2,1,0:T(8,128)(2,1)} %get-tuple-element.42, bf16[4,2,64,512]{3,2,1,0:T(8,128)(2,1)} %get-tuple-element.38), kind=kLoop, calls=%fused_computation.7 | loop fusion | flops 524288 | bytes 3145728 | tf_op jit(solution)/shard_map/reshape | solution.py:1501
  266.8 1.6 convert.12
  268.4 0.1 copy-done.1
  268.4 1.6 convert.8
  270.0 1.7 bitcast_convert_fusion
  271.7 0.1 reshape.134
  271.8 0.0 copy-start.9
  271.8 1.3 copy.48
  273.1 0.0 copy-done.6
  273.1 1.1 bitcast_convert_fusion.2
  274.2 0.8 bitcast_convert_fusion.4
  275.1 0.0 copy-start.12
  275.1 0.0 copy-start.15
  275.1 0.0 copy-start.14
  275.1 0.0 copy-start.11
  275.1 0.0 copy-start.10
  275.1 1.1 copy.60
  276.3 0.6 copy.61
  276.8 0.6 copy.62
  277.4 0.6 copy.63
  278.0 0.6 copy.64
  278.6 0.6 copy.65
  279.2 0.6 copy.66
  279.8 0.0 copy-done.11
  279.8 0.6 copy.67
  280.4 0.6 copy.68
  (30 shorter events, 0.1 us)
Async XLA Ops:
  0.7 7.5 %copy-start.3 = (bf16[768,768]{1,0:T(8,128)(2,1)S(1)}, bf16[768,768]{1,0:T(8,128)(2,1)}, u32[]{:S(2)}) copy-start(bf16[768,768]{1,0:T(8,128)(2,1)} %constant.50.clone.refs_16_) | copy-start | bytes 3538948
  8.2 1.7 copy-start.7
  9.9 1.0 copy-start.8
  263.8 2.9 %copy-start.2 = (bf16[9,4,2,64,128]{4,3,2,1,0:T(8,128)(2,1)S(1)}, bf16[9,4,2,64,128]{4,3,2,1,0:T(8,128)(2,1)}, u32[]{:S(2)}) copy-start(bf16[9,4,2,64,128]{4,3,2,1,0:T(8,128)(2,1)} %get-tuple-element.41) | copy-start | bytes 3538948
  266.8 1.6 copy-start.1
  268.4 1.6 copy-start.4
  270.0 1.7 copy-start.5
  271.7 1.4 copy-start.6
  271.8 2.4 copy-start.9
  273.1 1.9 copy-start
  275.1 1.2 copy-start.17
  275.1 1.8 copy-start.16
  275.1 2.4 copy-start.13
  275.1 3.0 %copy-start.12 = (f32[3,512]{1,0:T(4,128)S(1)}, f32[3,512]{1,0:T(4,128)}, u32[]{:S(2)}) copy-start(f32[3,512]{1,0:T(4,128)} %get-tuple-element.137) | copy-start | bytes 18436
  275.1 3.6 %copy-start.15 = (f32[4,128]{1,0:T(4,128)S(1)}, f32[4,128]{1,0:T(4,128)}, u32[]{:S(2)}) copy-start(f32[4,128]{1,0:T(4,128)} %get-tuple-element.138) | copy-start | bytes 6148
  275.1 4.1 %copy-start.14 = (f32[4,128]{1,0:T(4,128)S(1)}, f32[4,128]{1,0:T(4,128)}, u32[]{:S(2)}) copy-start(f32[4,128]{1,0:T(4,128)} %get-tuple-element.139) | copy-start | bytes 6148
  275.1 4.7 %copy-start.11 = (f32[3,512]{1,0:T(4,128)S(1)}, f32[3,512]{1,0:T(4,128)}, u32[]{:S(2)}) copy-start(f32[3,512]{1,0:T(4,128)} %get-tuple-element.140) | copy-start | bytes 18436
  275.1 5.3 %copy-start.10 = (f32[3,512]{1,0:T(4,128)S(1)}, f32[3,512]{1,0:T(4,128)}, u32[]{:S(2)}) copy-start(f32[3,512]{1,0:T(4,128)} %get-tuple-element.141) | copy-start | bytes 18436

commit v3 on v1

--- a/solution.py
+++ b/solution.py
@@ -1,4 +1,5 @@
 import functools
+import math
 import types
 
 import jax
@@ -359,26 +360,133 @@
         self.used += 1
         return self.sems.at[self.used - 1]
 
-    def push(self, src, dst, device):
-        copy = pltpu.make_async_remote_copy(
+    def plan(self, src, dst, device, recv_sem=None):
+        return pltpu.make_async_remote_copy(
             src_ref=src,
             dst_ref=dst,
             send_sem=self.take(),
-            recv_sem=self.take(),
+            recv_sem=self.take() if recv_sem is None else recv_sem,
             device_id=device,
             device_id_type=MESH,
         )
+
+    def push(self, src, dst, device):
+        copy = self.plan(src, dst, device)
         copy.start()
         self.sent.append(copy)
         return copy
 
+    def plan_local(self, src, dst):
+        return pltpu.make_async_copy(src, dst, self.take())
+
     def local(self, src, dst):
-        copy = pltpu.make_async_copy(src, dst, self.take())
+        copy = self.plan_local(src, dst)
         copy.start()
         return copy
 
 
-SEMS = 480
+class Summed:
+    def __init__(self, net, part, got, done, ring, spill, across=None):
+        at, ahead = ring
+        self.part, self.got, self.done, self.at, self.spill = part, got, done, at, spill
+        self.out = [net.plan(part.at[at[0]], got.at[0], ahead)]
+        self.out += [net.plan(got.at[k - 1], got.at[k], ahead) for k in range(1, 7)]
+        self.back = [
+            net.plan(done.at[at[(k + 7) % 8]], done.at[at[(k + 7) % 8]], ahead) for k in range(7)
+        ]
+        self.across = across is not None
+        if self.across:
+            self.crossing = net.plan(got.at[6, 1], done.at[at[7], 1], across)
+        self.todo = [self.begin] + [functools.partial(self.add, k) for k in range(6)]
+        self.todo += [self.finish] + ([self.crossed] if self.across else [])
+        self.todo += [functools.partial(self.pass_on, k) for k in range(6)] + [self.last]
+
+    def step(self):
+        self.todo.pop(0)()
+
+    def begin(self):
+        self.out[0].start()
+
+    def add(self, k):
+        self.out[k].wait_recv()
+        self.got[k] = self.got[k] + self.part[self.at[k + 1]]
+        self.out[k + 1].start()
+
+    def finish(self):
+        self.out[6].wait_recv()
+        total = self.got[6] + self.part[self.at[7]]
+        if self.across:
+            self.done[self.at[7], 0] = total[0]
+            self.got[6, 1] = total[1]
+            self.crossing.start()
+        else:
+            self.done[self.at[7]] = total
+            self.back[0].start()
+
+    def crossed(self):
+        self.crossing.wait_recv()
+        self.back[0].start()
+
+    def pass_on(self, k):
+        self.back[k].wait_recv()
+        self.back[k + 1].start()
+
+    def last(self):
+        self.back[6].wait_recv()
+        for copy in self.spill:
+            copy.start()
+
+    def drain(self):
+        for copy in self.out + self.back + ([self.crossing] if self.across else []):
+            copy.wait_send()
+        for copy in self.spill:
+            copy.wait()
+
+
+class Direct:
+    def __init__(self, net, part, got, done, place, peers, spill, across):
+        self.part, self.got, self.done, self.place, self.spill = part, got, done, place, spill
+        n = len(peers)
+        self.out = [net.plan(part.at[peers[k][0]], got.at[k], peers[k]) for k in range(n)]
+        self.back = [net.plan(done.at[place], done.at[place], peers[k]) for k in range(n)]
+        self.crossing = net.plan(got.at[n, 1], done.at[place, 1], across)
+        self.todo = [self.begin, self.finish, self.crossed, self.last]
+
+    def step(self):
+        self.todo.pop(0)()
+
+    def begin(self):
+        for copy in self.out:
+            copy.start()
+
+    def finish(self):
+        total = self.part[self.place].astype(F32)
+        for k, copy in enumerate(self.out):
+            copy.wait_recv()
+            total = total + self.got[k].astype(F32)
+        self.done[self.place, 0] = total[0].astype(BF)
+        self.got[len(self.out), 1] = total[1].astype(BF)
+        self.crossing.start()
+
+    def crossed(self):
+        self.crossing.wait_recv()
+        for copy in self.back:
+            copy.start()
+
+    def last(self):
+        for copy in self.back:
+            copy.wait_recv()
+        for copy in self.spill:
+            copy.start()
+
+    def drain(self):
+        for copy in self.out + self.back + [self.crossing]:
+            copy.wait_send()
+        for copy in self.spill:
+            copy.wait()
+
+
+SEMS = 900
 
 
 def block_kernel(geo, names, *refs):
@@ -388,8 +496,8 @@
     NB = geo.NB
     r = lax.axis_index("chan")
     b = lax.axis_index("batch")
-    r1, r2 = flip(r, 1), flip(r, 2)
-    r3 = flip(r1, 2)
+    r1, r3 = flip(r, 1), flip(r, 2)
+    r2 = flip(r1, 2)
     ranks = (r, r1, r2, r3)
     core, far = (b, r1), (b, r2)
     peers = []
@@ -402,6 +510,17 @@
             bit *= 2
         peers.append((other, r))
     net = Traffic(g.sems)
+    def seat(batch):
+        x, z = lax.rem(batch, 2), lax.div(batch, 2)
+        return z + x * (7 - 2 * z)
+
+    def batch_at(place):
+        x = lax.div(place, 4)
+        return 2 * (place + x * (7 - 2 * place)) + x
+
+    way = 1 - 2 * lax.rem(lax.rem(r, 2) + lax.div(r, 2), 2)
+    pieces = [lax.rem(seat(b) - way * k + 16, 8) for k in range(8)]
+    ring = (pieces, (batch_at(pieces[7]), r))
 
     bar = pltpu.get_barrier_semaphore()
     everyone = [core, far] + peers
@@ -414,7 +533,7 @@
     def taps_of(ref, rank, size):
         return ref.at[:, pl.ds(pl.multiple_of(rank * size, size), size), :]
 
-    ld_src = net.local(g.src, g.SRC.at[0])
+    ld_img = net.local(g.img, g.IMG)
     ld_w1 = [
         net.local(rows_of(g.w1, rank, CI), g.W1C.at[pl.ds(s * CI, CI), pl.ds(MI, MI)])
         for s, rank in enumerate((r, r1))
@@ -430,9 +549,49 @@
     ld_w6 = [net.local(rows_of(g.w6, rank, MI), g.W6.at[s]) for s, rank in enumerate(ranks)]
     ld_cot = net.local(g.cot, g.COT)
 
+    area = [g.heights[k] * g.widths[k] for k in range(NB * PS)]
+    first = lax.broadcasted_iota(jnp.int32, (R, 128), 0)
+
+    def of_image(ref, image):
+        value = jnp.full(image.shape, ref[b * PS], jnp.int32)
+        for k in range(1, PS):
+            value = jnp.where(image == k, ref[b * PS + k], value)
+        return value
+
+    def pixel(m):
+        image, row, column = lax.rem(m, PS), lax.rem(lax.div(m, PS), geo.rows), lax.div(m, QS)
+        good = (row < of_image(g.heights, image)) & (column < of_image(g.widths, image))
+        return column, row, image, good
+
+    g.mask[...] = jnp.where(pixel(first)[3], 1.0, 0.0)
+
+    def row(scalar):
+        return jnp.full((1, 128), scalar.astype(F32), F32)
+
+    for k in range(NB):
+        other = b if k == 0 else peers[k - 1][0]
+        own = 0
+        for j in range(PS):
+            own = own + g.heights[other * PS + j] * g.widths[other * PS + j]
+        g.aux[k : k + 1, :] = row(own)
+        g.aux[NB + k : NB + k + 1, :] = 1.0 / row(own)
+    count = row(sum(area))
+    g.aux[16:17, :] = 1.0 / count
+    g.aux[17:18, :] = count / (count - 1.0)
+    g.aux[18:19, :] = 4.0 * count / (4.0 * count - 1.0)
+
+    ld_img.wait()
+    lane = lax.broadcasted_iota(jnp.int32, (R, 4 * R), 1)
+    column, line, image, good = pixel(lax.broadcasted_iota(jnp.int32, (R, 1), 0))
+    corner = image * 4 * geo.rows * geo.cols + 2 * line * 2 * geo.cols + 2 * column
+    for ph in range(4):
+        source = jnp.where(good, corner + (ph // 2) * 2 * geo.cols + ph % 2, -1)
+        pick = jnp.where(lane == source, 1.0, 0.0).astype(BF)
+        g.SRC[0, ph * R : (ph + 1) * R, :] = mm(pick, g.IMG[...]).astype(BF)
+
     pl.semaphore_wait(bar, len(everyone))
 
-    rm_src = net.push(g.src, g.SRC.at[1], core)
+    rm_src = net.push(g.SRC.at[0], g.SRC.at[1], core)
     rm_w1 = [
         net.push(rows_of(g.w1, rank, CI), g.W1C.at[pl.ds(s * CI, CI), pl.ds(0, MI)], far)
         for s, rank in enumerate((r2, r3))
@@ -455,7 +614,6 @@
         for s in range(2):
             g.E2[d, s, R:, :] = jnp.zeros((QS, MI), BF)
 
-    ld_src.wait()
     for copy in ld_w1:
         copy.wait()
     rm_src.wait_recv()
@@ -815,6 +973,7 @@
     for copy in ld_w6:
         copy.wait()
     ld_cot.wait()
+    g.COTP[...] = mm_tn(g.po[...], g.COT[...])
     relay(ch_five)
     landed(ch_five)
     g.PRE6[...] = mm(four(g.F5), g.W6[...].reshape(4 * MI, CO))
@@ -831,7 +990,7 @@
         v = (g.PRE6[rows, :] - mean_six) * scale_six + bias_six + g.BM[rows, :]
         s = gate(v)
         g.OUT[rows, :] = v * s * m
-        grad = g.COT[rows, :].astype(F32) * m * (s * (1.0 + v * (1.0 - s)))
+        grad = g.COTP[rows, :] * m * (s * (1.0 + v * (1.0 - s)))
         g.GSB[rows, :] = grad
         return acc_b + fold(grad), acc_g + fold(grad * hat)
 
@@ -843,11 +1002,7 @@
 
     st = wide_send(3, down(acc_b), down(acc_g))
 
-    out = g.OUT[...]
-    high = out.astype(BF)
-    low = (out - high.astype(F32)).astype(BF)
-    g.OUTP[...] = mm(g.po[...], high) + mm(g.po[...], low)
-    out_block = net.local(g.OUTP, g.block_out)
+    out_block = net.local(g.OUT, g.block_out)
 
     def wide_sums(ref, copies, count):
         for copy in copies:
@@ -899,6 +1054,8 @@
         acc_b = jnp.zeros((8, MI), F32)
         acc_g = jnp.zeros((8, MI), F32)
         for ph in range(phases):
+            if ph:
+                pump(5)
             copy[ph].wait_recv()
 
             def body(at, carry, ph=ph):
@@ -928,7 +1085,7 @@
 
         over(R, NCH, body, 0)
 
-    outs = []
+    outs = [out_block]
 
     def give(src, dst):
         outs.append(net.local(src, dst))
@@ -938,12 +1095,45 @@
     part = wide_back(g.E6, g.W6, g.W6P)
     cp = [reduce_back(part, g.B5S, g.B5R)]
     g.GF5[...] = part[:, :MI]
+    def rows_grad(part, value, s):
+        half = value.shape[0] // 2
+        for h in range(2):
+            part[2 * s + h] = value[h * half : (h + 1) * half].astype(BF)
+
+    def taps_grad(part, tap, value):
+        half = MI // 2
+        for p in range(8):
+            part[p, tap] = value[p * half : (p + 1) * half].astype(BF)
+
+    jobs = []
+
+    def job(part, got, done, targets, across=None):
+        spill = [net.plan_local(source, place) for source, place in targets]
+        jobs.append(Summed(net, part, got, done, ring, spill, across))
+
+    def pump(most=99):
+        left = sorted((work for work in jobs if work.todo), key=lambda work: -len(work.todo))
+        for work in left[:most]:
+            work.step()
+
+    def slots_to(part, place):
+        return [(part.at[pl.ds(2 * s, 2)], place(ranks[s])) for s in range(4)]
+
+    def chips_to(part, out):
+        return [
+            (part.at[pl.ds(4 * s, 4), v], out.at[ranks[2 * v + s]])
+            for s in range(2)
+            for v in range(2)
+        ]
+
     for s in range(4):
-        g.K6[s] = mm_tn(g.F5[s], g.E6[0]).astype(BF)
-        give(g.K6.at[s], rows_of(g.k6, ranks[s], MI))
+        rows_grad(g.K6, mm_tn(g.F5[s], g.E6[0]), s)
+    job(g.K6, g.K6R, g.K6D, slots_to(g.K6D, lambda rank: g.k6.at[rank]))
+    pump()
     st = narrow_back(
         4, g.GF5, g.B5R, cp, 1, g.PRE5, mean_five, inv_five, scale_five, g.bm[3:4, :]
     )
+    pump()
     bsum_five, gsum_five = narrow_sums(4, st)
     narrow_pre_grad(
         g.GF5, g.PRE5, mean_five, inv_five, scale_five, bsum_five, gsum_five, 1, 0,
@@ -953,6 +1143,7 @@
     spread_rows(g.E5.at[1, 0], g.E5.at[0, 0], g.E5.at[2, 0])
     cp.wait_recv()
     spread_rows(g.E5.at[1, 1], g.E5.at[0, 1], g.E5.at[2, 1])
+    pump()
 
     def taps_back(own, other, tap):
         near = lanes([own[tap, 0], other[tap, 0]])
@@ -968,15 +1159,22 @@
             part = term if part is None else part + term
     cp = [reduce_back(part, g.B4S, g.B4R)]
     g.GF4[...] = part[:, :MI]
+    pump()
     own_five = g.E5[1, 0, QS : QS + R, :]
-    for t in range(3):
-        for l in range(3):
-            g.K5[3 * t + l] = mm_tn(whole_four(t, l), own_five).astype(BF)
-    for s in range(4):
-        give(g.K5.at[:, pl.ds(s * MI, MI), :], taps_of(g.k5, ranks[s], MI))
+
+    def five_grad(part, first, last):
+        for tap in range(first, last):
+            taps_grad(part, tap - first, mm_tn(whole_four(tap // 3, tap % 3), own_five))
+
+    five_grad(g.K5A, 0, 5)
+    job(g.K5A, g.K5AR, g.K5AD, slots_to(g.K5AD, lambda rank: g.k5.at[rank, :, pl.ds(0, 5)]))
+    five_grad(g.K5B, 5, 9)
+    job(g.K5B, g.K5BR, g.K5BD, slots_to(g.K5BD, lambda rank: g.k5.at[rank, :, pl.ds(5, 4)]))
+    pump()
     st = narrow_back(
         5, g.GF4, g.B4R, cp, 1, g.PRE4, mean_four, inv_four, scale_four, g.bm[2:3, :]
     )
+    pump()
     bsum_four, gsum_four = narrow_sums(5, st)
     narrow_pre_grad(
         g.GF4, g.PRE4, mean_four, inv_four, scale_four, bsum_four, gsum_four, 1, 0,
@@ -984,6 +1182,7 @@
     )
     ch = gather(lambda s: g.G4.at[s], 0, R)
     relay(ch)
+    pump()
     landed(ch)
     mid_back = mm_nt(
         four(g.G4),
@@ -1008,11 +1207,18 @@
         wide_put(g.SA, j * NW, down(value))
     st = exchange(g.SA, 4 * NW)
     e4 = lanes([g.G4[0], g.G4[2]])
+
+    def chip_grad(part, s, value):
+        size = value.shape[0] // 4
+        for p in range(4):
+            for w in range(2):
+                block = value[p * size : (p + 1) * size, w * MI : (w + 1) * MI]
+                part[4 * s + p, w] = block.astype(BF)
+
     for s in range(2):
-        k4 = mm_tn(g.MIDC[s], e4)
-        g.K4[0, s] = k4[:, :MI].astype(BF)
-        g.K4[1, s] = k4[:, MI:].astype(BF)
-    cp_k4 = net.push(g.K4.at[1], g.K4R, far)
+        chip_grad(g.K4, s, mm_tn(g.MIDC[s], e4))
+    job(g.K4, g.K4R, g.K4D, chips_to(g.K4D, g.k4), far)
+    pump()
     bsum_a, gsum_three, gsum_side = wide_sums(g.SA, st, 3)
     wide_pre_grad(
         g.GMID, g.PRE3, mean_three, inv_three, scale_three, bsum_a, gsum_three,
@@ -1023,19 +1229,31 @@
         g.GMID, g.PRES, mean_side, inv_side, scale_side, bsum_a, gsum_side, g.ES.at[0]
     )
     cp_side = swap(g.ES)
+    pump()
     cp.wait_recv()
     part = wide_back(g.E3, g.W3, g.W3P)
     cp = [reduce_back(part, g.B2S, g.B2R)]
     g.GF2[...] = part[:, :MI]
     for s in range(4):
-        g.K3[s] = mm_tn(g.F2[s], g.E3[0]).astype(BF)
-        give(g.K3.at[s], rows_of(g.k3, ranks[s], MI))
+        rows_grad(g.K3, mm_tn(g.F2[s], g.E3[0]), s)
+    job(g.K3, g.K3R, g.K3D, slots_to(g.K3D, lambda rank: g.k3.at[rank]))
+    pump()
     st = narrow_back(
         6, g.GF2, g.B2R, cp, 1, g.PRE2, mean_two, inv_two, scale_two, g.bm[1:2, :]
     )
+    pump()
     cp_side.wait_recv()
     es = lanes([g.ES[0], g.ES[1]])
     g.IGS[...] = mm_nt(es, lanes([g.WS[0], g.WSP[0]]))
+    half = CO // 2
+    for s, block in enumerate(strided()):
+        grad = mm_tn(block, g.ES[0])
+        rows_grad(g.KSA, grad[:, :half], s)
+        rows_grad(g.KSB, grad[:, half:], s)
+    job(g.KSA, g.KSAR, g.KSAD, slots_to(g.KSAD, lambda rank: g.ks.at[rank, :, :, pl.ds(0, half)]))
+    job(g.KSB, g.KSBR, g.KSBD, slots_to(g.KSBD, lambda rank: g.ks.at[rank, :, :, pl.ds(half, half)]))
+    pump()
+    pump()
     bsum_two, gsum_two = narrow_sums(6, st)
     narrow_pre_grad(
         g.GF2, g.PRE2, mean_two, inv_two, scale_two, bsum_two, gsum_two, 1, 0,
@@ -1067,18 +1285,30 @@
             reduce_back(part, g.B1S.at[pl.ds(ph * R, R)], g.B1R.at[pl.ds(ph * R, R)])
         )
         g.GF1[ph * R : (ph + 1) * R, :] = part[:, :MI]
+    pump()
     own_two = g.E2[0, 0, 0:R, :]
-    for ph in range(4):
-        for t, l in taps_two(ph):
-            g.K2[3 * t + l] = mm_tn(whole_one(ph, t == 0, l == 0), own_two).astype(BF)
-    for s in range(4):
-        give(g.K2.at[:, pl.ds(s * MI, MI), :], taps_of(g.k2, ranks[s], MI))
+
+    def two_grad(part, first, last):
+        for ph in range(4):
+            for t, l in taps_two(ph):
+                tap = 3 * t + l
+                if first <= tap < last:
+                    grad = mm_tn(whole_one(ph, t == 0, l == 0), own_two)
+                    taps_grad(part, tap - first, grad)
+
+    two_grad(g.K2A, 0, 5)
+    pump()
+    job(g.K2A, g.K2AR, g.K2AD, slots_to(g.K2AD, lambda rank: g.k2.at[rank, :, pl.ds(0, 5)]))
+    two_grad(g.K2B, 5, 9)
+    job(g.K2B, g.K2BR, g.K2BD, slots_to(g.K2BD, lambda rank: g.k2.at[rank, :, pl.ds(5, 4)]))
+    pump()
     st = narrow_back(
         7, g.GF1, g.B1R, cp, 4, g.PRE1, mean_one, inv_one, scale_one, g.bm[0:1, :]
     )
     side_far = mm_nt(es, lanes([g.WS[2], g.WSP[1]]))
     g.BSS[...] = side_far.astype(BF)
     cp_bs = net.push(g.BSS, g.BSR, far)
+    pump(5)
     bsum_one, gsum_one = narrow_sums(7, st)
     ch = []
     for ph in range(4):
@@ -1087,47 +1317,37 @@
             g.G1.at[0, ph], 0,
         )
         ch.append(gather(lambda s, ph=ph: g.G1.at[s, ph], 0, R))
-    for s, block in enumerate(strided()):
-        g.KS[s] = mm_tn(block, g.ES[0]).astype(BF)
-        give(g.KS.at[s], rows_of(g.ks, ranks[s], CI))
+    pump()
     w1_own = lanes([g.W1C[0:CI, MI:], g.W1P[0], g.W1C[0:CI, :MI], g.W1P[1]])
     relay(ch[0])
     for ph in range(4):
         if ph < 3:
             relay(ch[ph + 1])
         landed(ch[ph])
+        pump()
         whole = lanes([g.G1[s, ph] for s in range(4)])
         g.IG[ph * R : (ph + 1) * R, :] = mm_nt(whole, w1_own)
-    cp_bs.wait_recv()
-    g.IG[0:R, :] = g.IG[0:R, :] + g.IGS[...] + g.BSR[...].astype(F32)
-    for a in range(2):
-        both = jnp.concatenate(
-            [
-                g.IG[(2 * a + h) * R : (2 * a + h + 1) * R, :] * bc(g.mask[...], CI)
-                for h in range(2)
-            ],
-            axis=0,
-        )
-        high = both.astype(BF)
-        low = (both - high.astype(F32)).astype(BF)
-        g.IGP[a] = (mm(g.pi[...], high) + mm(g.pi[...], low)).reshape(g.IGP.shape[1:])
-        give(g.IGP.at[a], g.images_grad.at[:, a])
     for s in range(2):
         k1 = None
         for ph in range(4):
             e1 = lanes([g.G1[0, ph], g.G1[2, ph]])
             term = mm_tn(g.SRC[s, ph * R : (ph + 1) * R, :], e1)
             k1 = term if k1 is None else k1 + term
-        g.K1[0, s] = k1[:, :MI].astype(BF)
-        g.K1[1, s] = k1[:, MI:].astype(BF)
-    cp_k1 = net.push(g.K1.at[1], g.K1R, far)
-    cp_k4.wait_recv()
-    cp_k1.wait_recv()
-    for s in range(2):
-        give(g.K4.at[0, s], rows_of(g.k4, ranks[s], CO))
-        give(g.K1.at[0, s], rows_of(g.k1, ranks[s], CI))
-        give(g.K4R.at[s], rows_of(g.k4, ranks[2 + s], CO))
-        give(g.K1R.at[s], rows_of(g.k1, ranks[2 + s], CI))
+        chip_grad(g.K1, s, k1)
+    spill = [net.plan_local(source, place) for source, place in chips_to(g.K1D, g.k1)]
+    jobs.append(Direct(net, g.K1, g.K1R, g.K1D, b, peers, spill, far))
+    jobs[-1].step()
+    pump(5)
+    cp_bs.wait_recv()
+    g.IG[0:R, :] = g.IG[0:R, :] + g.IGS[...] + g.BSR[...].astype(F32)
+    for ph in range(4):
+        rows = slice(ph * R, (ph + 1) * R)
+        g.IG[rows, :] = g.IG[rows, :] * bc(g.mask[...], CI)
+    give(g.IG, g.images_grad)
+    while any(work.todo for work in jobs):
+        if jobs[-1].todo:
+            jobs[-1].step()
+        pump(5)
 
     g.gain_mid_grad[...] = jnp.concatenate([gsum_one, gsum_two, gsum_four, gsum_five], axis=0)
     g.bias_mid_grad[...] = jnp.concatenate([bsum_one, bsum_two, bsum_four, bsum_five], axis=0)
@@ -1142,11 +1362,13 @@
     g.var_out[...] = jnp.concatenate([spread_three, spread_side, spread_six], axis=0) * bc(
         unb_out, CO
     )
-    out_block.wait()
     for copy in outs:
         copy.wait()
     for copy in net.sent:
         copy.wait_send()
+
+    for work in jobs:
+        work.drain()
 
 
 def fused_on_device(
@@ -1157,52 +1379,21 @@
     CI, MI = images.shape[3], reduce_first.shape[1]
     NB = heights.shape[0] // n
     R, QS = n * rows * cols, n * rows
-    batch = lax.axis_index("batch")
-    valid = heights * widths
-    local_h = lax.dynamic_slice_in_dim(heights, batch * n, n)
-    local_w = lax.dynamic_slice_in_dim(widths, batch * n, n)
     q, p, i = np.meshgrid(np.arange(cols), np.arange(rows), np.arange(n), indexing="ij")
     q, p, i = (v.reshape(-1) for v in (q, p, i))
-    mask = (
-        (jnp.asarray(p)[:, None] < jnp.tile(local_h, rows * cols)[:, None])
-        & (jnp.asarray(q)[:, None] < jnp.tile(local_w, rows * cols)[:, None])
-    ).astype(F32)
-    where_out = (i * rows + p) * cols + q
     pick_out = np.zeros((R, R), np.float32)
-    pick_out[np.arange(R), where_out] = 1.0
+    pick_out[np.arange(R), (i * cols + q) * rows + p] = 1.0
     pick_in = np.zeros((2 * R, 2 * R), np.float32)
     for h in range(2):
         pick_in[h * R + np.arange(R), (i * rows + p) * 2 * cols + 2 * q + h] = 1.0
     po = jnp.asarray(pick_out.T.astype(ml_dtypes.bfloat16))
     pi = jnp.asarray(pick_in.T.astype(ml_dtypes.bfloat16))
-    mask_bf = mask.astype(BF)
-    cot = jnp.einsum(
-        "mk,kc->mc", po.T * mask_bf, cotangent.reshape(R, CO), preferred_element_type=F32
-    ).astype(BF)
-    parity = images.reshape(n, rows, 2, 2 * cols, CI).transpose(2, 0, 1, 3, 4).reshape(2, 2 * R, CI)
-    src = jnp.einsum(
-        "mk,akc->amc", pi.T * jnp.tile(mask_bf, (2, 1)), parity, preferred_element_type=F32
-    ).astype(BF).reshape(4 * R, CI)
-    order = np.arange(NB)
-    by_rank = jnp.sum(valid.reshape(NB, n), axis=1)
-    relative = jnp.take(by_rank, jnp.bitwise_xor(order, batch)).astype(F32)
-    count_out = jnp.sum(valid).astype(F32)
-    count_in = 4.0 * count_out
-    aux = jnp.concatenate(
-        [
-            relative,
-            1.0 / relative,
-            jnp.stack(
-                [1.0 / count_out, count_out / (count_out - 1.0), count_in / (count_in - 1.0)]
-            ),
-            jnp.zeros((5,), F32),
-        ]
-    )
-    aux = jnp.broadcast_to(aux[:, None], (24, 128))
+    cot = cotangent.transpose(0, 2, 1, 3).reshape(R, CO)
     ANY, VM = pl.BlockSpec(memory_space=pl.ANY), pl.BlockSpec(memory_space=pltpu.VMEM)
+    SM = pl.BlockSpec(memory_space=pltpu.SMEM)
     CM, MC = 4 * MI, 4 * CI
     ins = dict(
-        src=(src, ANY),
+        img=(images.reshape(4 * R, CI), ANY),
         cot=(cot, ANY),
         w1=(reduce_first, ANY),
         w2=(spatial_first.reshape(9, CM, MI), ANY),
@@ -1211,25 +1402,24 @@
         w4=(reduce_second, ANY),
         w5=(spatial_second.reshape(9, CM, MI), ANY),
         w6=(expand_second, ANY),
-        mask=(jnp.broadcast_to(mask, (R, 128)), VM),
-        aux=(aux, VM),
+        heights=(heights, SM),
+        widths=(widths, SM),
+        po=(po, VM),
         gm=(gain_mid, VM),
         bm=(bias_mid, VM),
         go=(gain_out, VM),
         bo=(bias_out, VM),
-        po=(po, VM),
-        pi=(pi, VM),
     )
     outs = dict(
         block_out=((R, CO), F32, ANY),
-        images_grad=((n * rows, 2, 2 * cols, CI), F32, ANY),
-        k1=((MC, MI), BF, ANY),
-        k2=((9, CM, MI), BF, ANY),
-        k3=((CM, CO), BF, ANY),
-        ks=((MC, CO), BF, ANY),
-        k4=((4 * CO, MI), BF, ANY),
-        k5=((9, CM, MI), BF, ANY),
-        k6=((CM, CO), BF, ANY),
+        images_grad=((4 * R, CI), F32, ANY),
+        k1=((4, 4, CI // 4, MI), BF, ANY),
+        k2=((4, 2, 9, MI // 2, MI), BF, ANY),
+        k3=((4, 2, MI // 2, CO), BF, ANY),
+        ks=((4, 2, CI // 2, CO), BF, ANY),
+        k4=((4, 4, CO // 4, MI), BF, ANY),
+        k5=((4, 2, 9, MI // 2, MI), BF, ANY),
+        k6=((4, 2, MI // 2, CO), BF, ANY),
         gain_mid_grad=((4, MI), F32, VM),
         bias_mid_grad=((4, MI), F32, VM),
         gain_out_grad=((3, CO), F32, VM),
@@ -1241,6 +1431,9 @@
     )
     NW = CO // 128
     scratch = dict(
+        IMG=((4 * R, CI), BF),
+        mask=((R, 128), F32),
+        aux=((24, 128), F32),
         SRC=((2, 4 * R, CI), BF),
         XS=((2, R, CI), BF),
         W1C=((2 * CI, 2 * MI), BF),
@@ -1258,6 +1451,7 @@
         W6=((4, MI, CO), BF),
         W6P=((2, MI, CO), BF),
         COT=((R, CO), BF),
+        COTP=((R, CO), F32),
         P1S=((4, R, MI), BF),
         P1R=((4, R, MI), BF),
         P4S=((R, MI), BF),
@@ -1278,7 +1472,6 @@
         D4=((2, 4, R + 2 * QS, MI), BF),
         F5=((4, R, MI), BF),
         OUT=((R, CO), F32),
-        OUTP=((R, CO), F32),
         GSB=((R, CO), F32),
         E6=((2, R, CO), BF),
         B5S=((R, MI), BF),
@@ -1304,22 +1497,29 @@
         BSS=((R, CI), BF),
         BSR=((R, CI), BF),
         IG=((4 * R, CI), F32),
-        IGP=((2, n * rows, 2 * cols, CI), F32),
-        K1=((2, 2, CI, MI), BF),
-        K1R=((2, CI, MI), BF),
-        K2=((9, CM, MI), BF),
-        K3=((4, MI, CO), BF),
-        KS=((4, CI, CO), BF),
-        K4=((2, 2, CO, MI), BF),
-        K4R=((2, CO, MI), BF),
-        K5=((9, CM, MI), BF),
-        K6=((4, MI, CO), BF),
         SN=((8, NB, 2, MI), F32),
         SW=((4, NB, 2 * NW, 128), F32),
         SA=((NB, 4 * NW, 128), F32),
     )
+    for name, piece in dict(
+        K1=(2, CI // 4, MI),
+        K2A=(5, MI // 2, MI),
+        K2B=(4, MI // 2, MI),
+        K3=(MI // 2, CO),
+        KSA=(CI // 2, CO // 2),
+        KSB=(CI // 2, CO // 2),
+        K4=(2, CO // 4, MI),
+        K5A=(5, MI // 2, MI),
+        K5B=(4, MI // 2, MI),
+        K6=(MI // 2, CO),
+    ).items():
+        scratch[name] = ((8, *piece), BF)
+        scratch[name + "D"] = ((8, *piece), BF)
+        scratch[name + "R"] = ((8 if name == "K1" else 7, *piece), BF)
     names = [*ins, *outs, *scratch, "sems"]
-    geo = types.SimpleNamespace(R=R, QS=QS, PS=n, CI=CI, MI=MI, CO=CO, NB=NB)
+    geo = types.SimpleNamespace(
+        R=R, QS=QS, PS=n, CI=CI, MI=MI, CO=CO, NB=NB, rows=rows, cols=cols
+    )
     got = pl.pallas_call(
         functools.partial(block_kernel, geo, names),
         out_shape=[jax.ShapeDtypeStruct(s, d) for s, d, _ in outs.values()],
@@ -1332,28 +1532,98 @@
         ),
     )(*[value for value, _ in ins.values()])
     o = types.SimpleNamespace(**dict(zip(outs, got)))
-    k1, k2, k3, ks, k4, k5, k6 = (
-        lax.psum(k, "batch").astype(F32) for k in (o.k1, o.k2, o.k3, o.ks, o.k4, o.k5, o.k6)
-    )
-    return (
-        o.block_out.reshape(n, rows, cols, CO),
-        o.images_grad.reshape(n, 2 * rows, 2 * cols, CI),
-        k1,
-        k2.reshape(3, 3, CM, MI),
-        k3,
-        ks,
-        k4,
-        k5.reshape(3, 3, CM, MI),
-        k6,
-        o.gain_mid_grad,
-        o.bias_mid_grad,
-        o.gain_out_grad,
-        o.bias_out_grad,
-        o.mean_mid,
-        o.var_mid,
-        o.mean_out,
-        o.var_out,
-    )
+    passed = [
+        o.gain_mid_grad, o.bias_mid_grad, o.gain_out_grad, o.bias_out_grad,
+        o.mean_mid, o.var_mid, o.mean_out, o.var_out,
+    ]
+    finals = [
+        jax.ShapeDtypeStruct(shape, F32)
+        for shape in (
+            (R, CO), (n, 2 * rows, 2 * cols, CI), (MC, MI), (3, 3, CM, MI), (CM, CO),
+            (MC, CO), (4 * CO, MI), (3, 3, CM, MI), (CM, CO),
+        )
+    ]
+    ks = (o.k1, o.k2, o.k3, o.ks, o.k4, o.k5, o.k6)
+    res = pl.pallas_call(
+        finish_kernel,
+        out_shape=finals + [jax.ShapeDtypeStruct(v.shape, F32) for v in passed],
+        in_specs=[ANY] * 9 + [VM] * 10,
+        out_specs=[ANY] * 9 + [VM] * 8,
+        scratch_shapes=[pltpu.VMEM((R, CO), F32), pltpu.VMEM((4 * R, CI), F32)]
+        + [pltpu.VMEM(k.shape, BF) for k in ks]
+        + [pltpu.VMEM(f.shape, F32) for f in finals]
+        + [pltpu.SemaphoreType.DMA((18,))],
+        compiler_params=pltpu.CompilerParams(vmem_limit_bytes=VMEM_LIMIT),
+    )(o.block_out, o.images_grad, *ks, po, pi, *passed)
+    block_out = res[0].reshape(n, cols, rows, CO).transpose(0, 2, 1, 3)
+    return (block_out, *res[1:])
+
+
+def exact(pick, value):
+    high = value.astype(BF)
+    low = (value - high.astype(F32)).astype(BF)
+    return mm(pick, high) + mm(pick, low)
+
+
+def finish_kernel(*refs):
+    ins, po, pi, small = refs[:9], refs[9], refs[10], refs[11:19]
+    outs, small_outs = refs[19:28], refs[28:36]
+    held, made, sems = refs[36:45], refs[45:54], refs[54]
+    loads = [pltpu.make_async_copy(a, v, sems.at[k]) for k, (a, v) in enumerate(zip(ins, held))]
+    stores = [
+        pltpu.make_async_copy(v, a, sems.at[9 + k]) for k, (v, a) in enumerate(zip(made, outs))
+    ]
+    for copy in loads:
+        copy.start()
+    for a, v in zip(small, small_outs):
+        v[...] = a[...]
+
+    def rows_of(k):
+        src, dst = held[k], made[k]
+        size = math.prod(src.shape[1:-1])
+        for rank in range(4):
+            dst[rank * size : (rank + 1) * size, :] = (
+                src[rank].reshape(size, src.shape[-1]).astype(F32)
+            )
+
+    def taps_of(k):
+        src, dst = held[k], made[k]
+        size = src.shape[3]
+
+        def tap(t):
+            for rank in range(4):
+                for h in range(2):
+                    at = (2 * rank + h) * size
+                    dst[t // 3, t % 3, at : at + size, :] = src[rank, h, t].astype(F32)
+
+        for t in range(src.shape[2]):
+            tap(t)
+
+    def block():
+        made[0][...] = exact(po[...], held[0][...])
+
+    def images():
+        half = held[1].shape[0] // 2
+        for a in range(2):
+            value = exact(pi[...], held[1][a * half : (a + 1) * half, :])
+            value = value.reshape(-1, *made[1].shape[2:])
+            rows = made[1].shape[1] // 2
+            for at in range(value.shape[0]):
+                made[1][at // rows, 2 * (at % rows) + a] = value[at]
+
+    for k in (3, 7, 5, 2, 4, 6, 8, 0, 1):
+        loads[k].wait()
+        if k == 0:
+            block()
+        elif k == 1:
+            images()
+        elif k in (3, 7):
+            taps_of(k)
+        else:
+            rows_of(k)
+        stores[k].start()
+    for copy in stores:
+        copy.wait()
 
 
 def solution(mesh):

time: 399 us -> 244 us (0.61)
  waiting for transfers between devices: 183 us -> 0 us
  Pallas kernels: 169 us -> 243 us
  local copies, waits for them, and re-layouts: 15.7 us -> 0 us
  between operations: 15 us -> 0.85 us
  other arithmetic: 12.7 us -> 0 us
    psum x1 -> x0, waiting for transfers between devices: 183 us -> none  [fused_on_device(): lax.psum(k, 'batch').astype(F32)]
    pallas_call x1, Pallas kernels: 169 us -> 234 us  [fused_on_device(): pl.pallas_call(functools.partial(block_kernel, geo, names), out_shape=[ja...]
    unnamed x51 -> x0, local copies, waits for them, and re-layouts: 10.3 us -> none
    pallas_call x0 -> x1, Pallas kernels: none -> 9.29 us  [fused_on_device(): pl.pallas_call(finish_kernel, out_shape=finals + [jax.ShapeDtypeStruct(v....]
    convert_element_type x7 -> x0, other arithmetic: 6.7 us -> none  [the longest x5 6.62 us: fused_on_device(): lax.psum(k, 'batch').astype(F32)]
    reshape x2 -> x0, other arithmetic: 4.51 us -> none  [the longest x1 2.92 us: fused_on_device(): k2.reshape(3, 3, CM, MI)]
  transfers between devices with their start and end apart: 1 -> 0, of which waited for: 1 -> 0; matrix products, arithmetic and copies ran while one was open for 0% -> 0% of each run, Pallas kernels for 0% -> 0%
where the time goes in v3:
time: 244 us
  Pallas kernels  243 us (100%)
    pallas_call x1, Pallas kernels, fused_on_device(): pl.pallas_call(functools.partial(block_kernel, geo, names), out_shape=[ja...  234 us
    pallas_call x1, Pallas kernels, fused_on_device(): pl.pallas_call(finish_kernel, out_shape=finals + [jax.ShapeDtypeStruct(v....  9.29 us

profile of v3, /device:TPU:0, one launch (start us, length us, event | category | flops | bytes accessed | tf_op | source)
XLA Modules:
  0.0 243.7 jit_solution(60722295322351062)
XLA Ops:
  0.7 233.5 %shard_map.296 = (f32[384,512]{1,0:T(8,128)}, f32[1536,256]{1,0:T(8,128)}, bf16[4,4,64,128]{3,2,1,0:T(8,128)(2,1)}, bf16[4,2,9,64,128]{4,3,2,1,0:T(8,128)(2,1)},...) custom-call(bf16[1536,256]{1,0:T(8,128)(2,1)} %bitcast.11, ...), custom_call_target="tpu_custom_call" | custom-call | tf_op jit(solution)/shard_map/pallas_call | solution.py:1523
  234.2 9.3 %shard_map.297 = (f32[384,512]{1,0:T(8,128)}, f32[4,16,24,256]{3,2,1,0:T(8,128)}, f32[1024,128]{1,0:T(8,128)}, f32[3,3,512,128]{3,2,1,0:T(8,128)}, f32[512,512]{...) custom-call(f32[384,512]{1,0:T(8,128)} %get-tuple-element.51.refs_0_, ...), custom_call_target="tpu_custom_call" | custom-call | tf_op jit(solution)/shard_map/pallas_call | solution.py:1547

commit v4 on v3

--- a/solution.py
+++ b/solution.py
@@ -360,15 +360,20 @@
         self.used += 1
         return self.sems.at[self.used - 1]
 
-    def plan(self, src, dst, device, recv_sem=None):
+    def plan(self, src, dst, device, send_sem=None, recv_sem=None):
         return pltpu.make_async_remote_copy(
             src_ref=src,
             dst_ref=dst,
-            send_sem=self.take(),
+            send_sem=self.take() if send_sem is None else send_sem,
             recv_sem=self.take() if recv_sem is None else recv_sem,
             device_id=device,
             device_id_type=MESH,
         )
+
+    def spread(self, src, dst, peers, all_of):
+        sems = self.take(), self.take()
+        copies = [self.plan(a, d, p, *sems) for a, d, p in zip(src, dst, peers)]
+        return copies, self.plan(all_of, all_of, peers[0], *sems)
 
     def push(self, src, dst, device):
         copy = self.plan(src, dst, device)
@@ -376,79 +381,115 @@
         self.sent.append(copy)
         return copy
 
-    def plan_local(self, src, dst):
-        return pltpu.make_async_copy(src, dst, self.take())
+    def plan_local(self, src, dst, sem=None):
+        return pltpu.make_async_copy(src, dst, self.take() if sem is None else sem)
 
     def local(self, src, dst):
         copy = self.plan_local(src, dst)
         copy.start()
         return copy
 
+    def load(self, pairs, all_of):
+        sem = self.take()
+        for src, dst in pairs:
+            pltpu.make_async_copy(src, dst, sem).start()
+        return pltpu.make_async_copy(all_of, all_of, sem)
+
 
 class Summed:
     def __init__(self, net, part, got, done, ring, spill, across=None):
-        at, ahead = ring
-        self.part, self.got, self.done, self.at, self.spill = part, got, done, at, spill
-        self.out = [net.plan(part.at[at[0]], got.at[0], ahead)]
-        self.out += [net.plan(got.at[k - 1], got.at[k], ahead) for k in range(1, 7)]
+        at, ahead, behind = ring
+        self.part, self.got, self.done, self.at = part, got, done, at
+        self.spill, self.spill_wait = spill
+        legs, legs_back = net.take(), net.take()
+        up = [part.at[at(4)]] + [got.at[k] for k in range(4)]
+        down = [part.at[at(-3)]] + [got.at[k] for k in range(4, 7)]
+        self.out = [
+            [net.plan(up[k], up[k + 1], ahead, legs)]
+            + ([net.plan(down[k], down[k + 1], behind, legs)] if k < 3 else [])
+            for k in range(4)
+        ]
         self.back = [
-            net.plan(done.at[at[(k + 7) % 8]], done.at[at[(k + 7) % 8]], ahead) for k in range(7)
+            ([net.plan(done.at[at(-k)], done.at[at(-k)], ahead, legs_back)] if k < 3 else [])
+            + [net.plan(done.at[at(k)], done.at[at(k)], behind, legs_back)]
+            for k in range(4)
+        ]
+        self.left = [
+            net.plan(got, got, ahead, legs, legs),
+            net.plan(done.at[pl.ds(0, 7)], done.at[pl.ds(0, 7)], ahead, legs_back, legs_back),
         ]
         self.across = across is not None
         if self.across:
-            self.crossing = net.plan(got.at[6, 1], done.at[at[7], 1], across)
-        self.todo = [self.begin] + [functools.partial(self.add, k) for k in range(6)]
+            self.crossing = net.plan(got.at[3, 1], done.at[at(0), 1], across)
+            self.left.append(self.crossing)
+        self.todo = [self.begin] + [functools.partial(self.add, k) for k in range(3)]
         self.todo += [self.finish] + ([self.crossed] if self.across else [])
-        self.todo += [functools.partial(self.pass_on, k) for k in range(6)] + [self.last]
+        self.todo += [functools.partial(self.pass_on, k) for k in range(3)] + [self.last]
 
     def step(self):
         self.todo.pop(0)()
 
+    def start(self, copies):
+        for copy in copies:
+            copy.start()
+
+    def arrived(self, copies):
+        for copy in copies:
+            copy.wait_recv()
+
     def begin(self):
-        self.out[0].start()
+        self.start(self.out[0])
 
     def add(self, k):
-        self.out[k].wait_recv()
-        self.got[k] = self.got[k] + self.part[self.at[k + 1]]
-        self.out[k + 1].start()
+        self.arrived(self.out[k])
+        self.got[k] = self.got[k] + self.part[self.at(3 - k)]
+        if k < 2:
+            self.got[4 + k] = self.got[4 + k] + self.part[self.at(k - 2)]
+        self.start(self.out[k + 1])
 
     def finish(self):
-        self.out[6].wait_recv()
-        total = self.got[6] + self.part[self.at[7]]
+        self.arrived(self.out[3])
+        total = self.got[3] + self.got[6] + self.part[self.at(0)]
         if self.across:
-            self.done[self.at[7], 0] = total[0]
-            self.got[6, 1] = total[1]
+            self.done[self.at(0), 0] = total[0]
+            self.got[3, 1] = total[1]
             self.crossing.start()
         else:
-            self.done[self.at[7]] = total
-            self.back[0].start()
+            self.done[self.at(0)] = total
+            self.start(self.back[0])
 
     def crossed(self):
         self.crossing.wait_recv()
-        self.back[0].start()
+        self.start(self.back[0])
 
     def pass_on(self, k):
-        self.back[k].wait_recv()
-        self.back[k + 1].start()
+        self.arrived(self.back[k])
+        self.start(self.back[k + 1])
 
     def last(self):
-        self.back[6].wait_recv()
-        for copy in self.spill:
-            copy.start()
+        self.arrived(self.back[3])
+        self.start(self.spill)
 
     def drain(self):
-        for copy in self.out + self.back + ([self.crossing] if self.across else []):
+        for copy in self.left:
             copy.wait_send()
-        for copy in self.spill:
-            copy.wait()
+        self.spill_wait.wait()
 
 
 class Direct:
     def __init__(self, net, part, got, done, place, peers, spill, across):
-        self.part, self.got, self.done, self.place, self.spill = part, got, done, place, spill
+        self.part, self.got, self.done, self.place = part, got, done, place
+        self.spill, self.spill_wait = spill
         n = len(peers)
-        self.out = [net.plan(part.at[peers[k][0]], got.at[k], peers[k]) for k in range(n)]
-        self.back = [net.plan(done.at[place], done.at[place], peers[k]) for k in range(n)]
+        self.out, self.whole = net.spread(
+            [part.at[peer[0]] for peer in peers],
+            [got.at[k] for k in range(n)],
+            peers,
+            got.at[pl.ds(0, n)],
+        )
+        self.back, self.whole_back = net.spread(
+            [done.at[place]] * n, [done.at[place]] * n, peers, done.at[pl.ds(0, n)]
+        )
         self.crossing = net.plan(got.at[n, 1], done.at[place, 1], across)
         self.todo = [self.begin, self.finish, self.crossed, self.last]
 
@@ -461,8 +502,8 @@
 
     def finish(self):
         total = self.part[self.place].astype(F32)
-        for k, copy in enumerate(self.out):
-            copy.wait_recv()
+        self.whole.wait_recv()
+        for k in range(len(self.out)):
             total = total + self.got[k].astype(F32)
         self.done[self.place, 0] = total[0].astype(BF)
         self.got[len(self.out), 1] = total[1].astype(BF)
@@ -474,19 +515,17 @@
             copy.start()
 
     def last(self):
-        for copy in self.back:
-            copy.wait_recv()
+        self.whole_back.wait_recv()
         for copy in self.spill:
             copy.start()
 
     def drain(self):
-        for copy in self.out + self.back + [self.crossing]:
+        for copy in (self.whole, self.whole_back, self.crossing):
             copy.wait_send()
-        for copy in self.spill:
-            copy.wait()
-
-
-SEMS = 900
+        self.spill_wait.wait()
+
+
+SEMS = 344
 
 
 def block_kernel(geo, names, *refs):
@@ -519,13 +558,20 @@
         return 2 * (place + x * (7 - 2 * place)) + x
 
     way = 1 - 2 * lax.rem(lax.rem(r, 2) + lax.div(r, 2), 2)
-    pieces = [lax.rem(seat(b) - way * k + 16, 8) for k in range(8)]
-    ring = (pieces, (batch_at(pieces[7]), r))
+    places = {k: lax.rem(seat(b) + way * k + 16, 8) for k in range(-3, 5)}
+    ring = (places.get, (batch_at(places[1]), r), (batch_at(places[-1]), r))
 
     bar = pltpu.get_barrier_semaphore()
     everyone = [core, far] + peers
     for device in everyone:
         pl.semaphore_signal(bar, 1, device_id=device, device_id_type=MESH)
+
+    def everywhere(src, dst, all_of):
+        copies, whole = net.spread(src, dst, peers, all_of)
+        for copy in copies:
+            copy.start()
+        net.sent.append(whole)
+        return whole
 
     def rows_of(ref, rank, size):
         return ref.at[pl.ds(pl.multiple_of(rank * size, size), size)]
@@ -538,16 +584,6 @@
         net.local(rows_of(g.w1, rank, CI), g.W1C.at[pl.ds(s * CI, CI), pl.ds(MI, MI)])
         for s, rank in enumerate((r, r1))
     ]
-    ld_sc = [net.local(rows_of(g.wsc, rank, CI), g.WS.at[s]) for s, rank in enumerate(ranks)]
-    ld_w2 = [net.local(taps_of(g.w2, rank, MI), g.W2.at[:, s]) for s, rank in enumerate(ranks)]
-    ld_w3 = [net.local(rows_of(g.w3, rank, MI), g.W3.at[s]) for s, rank in enumerate(ranks)]
-    ld_w4 = [
-        net.local(rows_of(g.w4, rank, CO), g.W4C.at[pl.ds(s * CO, CO), pl.ds(MI, MI)])
-        for s, rank in enumerate((r, r1))
-    ]
-    ld_w5 = [net.local(taps_of(g.w5, rank, MI), g.W5.at[:, s]) for s, rank in enumerate(ranks)]
-    ld_w6 = [net.local(rows_of(g.w6, rank, MI), g.W6.at[s]) for s, rank in enumerate(ranks)]
-    ld_cot = net.local(g.cot, g.COT)
 
     area = [g.heights[k] * g.widths[k] for k in range(NB * PS)]
     first = lax.broadcasted_iota(jnp.int32, (R, 128), 0)
@@ -596,11 +632,27 @@
         net.push(rows_of(g.w1, rank, CI), g.W1C.at[pl.ds(s * CI, CI), pl.ds(0, MI)], far)
         for s, rank in enumerate((r2, r3))
     ]
+    piece = MI // 4
+    rank = jnp.where(b < 4, r2, r3)
+    at = pl.multiple_of(rank * MI + lax.rem(b, 4) * piece, piece)
+    rm_w2 = net.push(g.w2.at[:, pl.ds(at, piece), :], g.W2F.at[b], far)
+    ld_sc = net.load([(rows_of(g.wsc, rank, CI), g.WS.at[s]) for s, rank in enumerate(ranks)], g.WS)
+    ld_w2 = net.load([(taps_of(g.w2, rank, MI), g.W2.at[:, s]) for s, rank in enumerate((r, r1))], g.W2)
+    ld_w3 = net.load([(rows_of(g.w3, rank, MI), g.W3.at[s]) for s, rank in enumerate(ranks)], g.W3)
+    ld_w4 = [
+        net.local(rows_of(g.w4, rank, CO), g.W4C.at[pl.ds(s * CO, CO), pl.ds(MI, MI)])
+        for s, rank in enumerate((r, r1))
+    ]
+    ld_w5 = net.load([(taps_of(g.w5, rank, MI), g.W5.at[:, s]) for s, rank in enumerate(ranks)], g.W5)
+    ld_w6 = net.load([(rows_of(g.w6, rank, MI), g.W6.at[s]) for s, rank in enumerate(ranks)], g.W6)
+    ld_cot = net.local(g.cot, g.COT)
+
     for ph in (1, 3):
-        for s in range(4):
+        for s in range(2):
             g.F1[s, ph, 0:QS, :] = jnp.zeros((QS, MI), BF)
+    for s in range(2):
+        g.D1[1, s, 0:QS, :] = jnp.zeros((QS, MI), BF)
     for s in range(4):
-        g.D1[1, s, 0:QS, :] = jnp.zeros((QS, MI), BF)
         g.F4[s, 0:QS, :] = jnp.zeros((QS, MI), BF)
         g.F4[s, QS + R :, :] = jnp.zeros((QS, MI), BF)
         for d in range(2):
@@ -611,7 +663,7 @@
             g.E5[d, s, 0:QS, :] = jnp.zeros((QS, MI), BF)
             g.E5[d, s, QS + R :, :] = jnp.zeros((QS, MI), BF)
     for d in range(2):
-        for s in range(2):
+        for s in range(4):
             g.E2[d, s, R:, :] = jnp.zeros((QS, MI), BF)
 
     for copy in ld_w1:
@@ -628,13 +680,16 @@
         rm_p1.append(net.push(g.P1S.at[ph], g.P1R.at[ph], far))
         g.PRE1[span, :] = part[:, MI:]
 
+    rm_w2.wait_recv()
+    rm_w2s = everywhere([g.W2F.at[b]] * (NB - 1), [g.W2F.at[b]] * (NB - 1), g.W2F.at[pl.ds(0, NB - 1)])
+
     rm_back = []
     for s, rank in enumerate((r1, r3)):
         rm_back.append(net.push(rows_of(g.w6, rank, MI), g.W6P.at[s], core))
         rm_back.append(net.push(taps_of(g.w5, rank, MI), g.W5P.at[:, s], core))
         rm_back.append(net.push(rows_of(g.w3, rank, MI), g.W3P.at[s], core))
         rm_back.append(net.push(rows_of(g.wsc, rank, CI), g.WSP.at[s], core))
-        rm_back.append(net.push(taps_of(g.w2, rank, MI), g.W2P.at[:, s], core))
+    rm_back.append(net.push(taps_of(g.w2, r1, MI), g.W2P, core))
     rm_back.append(net.push(rows_of(g.w4, r1, CO), g.W4P.at[0], core))
     rm_back.append(net.push(rows_of(g.w1, r1, CI), g.W1P.at[0], core))
     rm_back.append(
@@ -661,7 +716,12 @@
         return jnp.concatenate([mask] * (width // 128), axis=1)
 
     def exchange(slots, payload_rows):
-        return [net.push(slots.at[0], slots.at[k], peers[k - 1]) for k in range(1, NB)]
+        others = range(1, NB)
+        return everywhere(
+            [slots.at[0] for _ in others],
+            [slots.at[k] for k in others],
+            slots.at[pl.ds(1, NB - 1)],
+        )
 
     def narrow_local(pre, phases, prepare=None):
         total = jnp.zeros((8, MI), F32)
@@ -692,8 +752,7 @@
         return exchange(slots, 2)
 
     def narrow_merge(idx, copies, phases):
-        for copy in copies:
-            copy.wait_recv()
+        copies.wait_recv()
         sums = [g.SN[idx, k, 0:1, :] for k in range(NB)]
         squares = [g.SN[idx, k, 1:2, :] for k in range(NB)]
         return moments(sums, squares, phases)
@@ -737,8 +796,7 @@
         return exchange(slots, 2 * NW)
 
     def wide_merge(idx, copies):
-        for copy in copies:
-            copy.wait_recv()
+        copies.wait_recv()
         sums = [g.SW[idx, k, 0:NW, :] for k in range(NB)]
         squares = [g.SW[idx, k, NW : 2 * NW, :] for k in range(NB)]
         mean, spread = moments(sums, squares, 1)
@@ -805,12 +863,25 @@
         narrow_feature(
             g.PRE1, mean_one, scale_one, g.bm[0:1, :], g.F1.at[0, ph], ph, QS
         )
-        ch_one.append(gather(lambda s, ph=ph: g.F1.at[s, ph], QS, R))
+        span = pl.ds(QS, R)
+        ch_one.append(net.push(g.F1.at[0, ph, span], g.F1.at[1, ph, span], core))
+
+    def taking(copy, pre, got):
+        def take(ph):
+            copy.wait_recv()
+
+            def add(at, carry):
+                rows = pl.ds(at, NCH)
+                pre[rows, :] = pre[rows, :] + got[rows, :].astype(F32)
+                return carry
+
+            over(R, NCH, add, 0)
+
+        return take
 
     rm_xs.wait_recv()
     rm_xs2 = net.push(g.XS.at[0], g.XS.at[1], core)
-    for copy in ld_sc:
-        copy.wait()
+    ld_sc.wait()
     rm_xs2.wait_recv()
 
     def strided():
@@ -823,62 +894,72 @@
     g.PRES[...] = pre_side
     st_side = wide_send(0, *wide_local(g.PRES))
 
-    for copy in ld_w2:
-        copy.wait()
-
-    def whole_one(ph, down, left):
+    ld_w2.wait()
+
+    def chip_one(s, ph, down, left):
         rows = slice(0, R) if left else slice(QS, QS + R)
-        if down:
-            return lanes([g.D1[ph - 2, s, rows, :] for s in range(4)])
-        return lanes([g.F1[s, ph, rows, :] for s in range(4)])
-
-    def kernel_rows(ref, tap):
-        return jnp.concatenate([ref[tap, s] for s in range(4)], axis=0)
+        return g.D1[ph - 2, s, rows, :] if down else g.F1[s, ph, rows, :]
+
+    def far_two(tap, first):
+        return jnp.concatenate([g.W2F[first + k, tap] for k in range(4)], axis=0)
+
+    def both_two(tap):
+        near = jnp.concatenate([g.W2[tap, s] for s in range(2)], axis=0)
+        away = jnp.concatenate([far_two(tap, 0), far_two(tap, 4)], axis=0)
+        return lanes([away, near])
 
     def taps_two(ph):
         top = (1,) if ph < 2 else (0, 2)
         left = (1,) if ph % 2 == 0 else (0, 2)
         return [(t, l) for t in top for l in left]
 
-    relay(ch_one[0])
-    pre_two = None
+    def lower(ph, s):
+        def move(at, carry):
+            v = g.F1[s, ph, pl.ds(QS + at, QS), :].astype(F32)
+            g.D1[ph - 2, s, pl.ds(QS + at, QS), :] = shifted(v, -1).astype(BF)
+            return carry
+
+        over(R, QS, move, 0)
+
+    rm_w2s.wait_recv()
+    rm_back.append(net.push(g.W2F.at[pl.ds(4, 4)], g.W2Q, core))
+    part = None
     for ph in range(4):
-        if ph < 3:
-            relay(ch_one[ph + 1])
-        landed(ch_one[ph])
         if ph >= 2:
-
-            def move(at, carry, ph=ph):
-                for s in range(4):
-                    v = g.F1[s, ph, pl.ds(QS + at, QS), :].astype(F32)
-                    g.D1[ph - 2, s, pl.ds(QS + at, QS), :] = shifted(v, -1).astype(BF)
-                return carry
-
-            over(R, QS, move, 0)
+            lower(ph, 0)
+        ch_one[ph].wait_recv()
+        if ph >= 2:
+            lower(ph, 1)
         for t, l in taps_two(ph):
-            term = mm(whole_one(ph, t == 0, l == 0), kernel_rows(g.W2, 3 * t + l))
-            pre_two = term if pre_two is None else pre_two + term
-    g.PRE2[...] = pre_two
+            term = mm(lanes([chip_one(s, ph, t == 0, l == 0) for s in range(2)]), both_two(3 * t + l))
+            part = term if part is None else part + term
+    g.P2S[...] = part[:, :MI].astype(BF)
+    rm_p2 = net.push(g.P2S, g.P2R, far)
+    g.PRE2[...] = part[:, MI:]
     rm_w4 = [
         net.push(rows_of(g.w4, rank, CO), g.W4C.at[pl.ds(s * CO, CO), pl.ds(0, MI)], far)
         for s, rank in enumerate((r2, r3))
     ]
-    st_two = narrow_send(1, *narrow_local(g.PRE2, 1))
+    st_two = narrow_send(1, *narrow_local(g.PRE2, 1, taking(rm_p2, g.PRE2, g.P2R)))
     mean_two, spread_two = narrow_merge(1, st_two, 1)
     inv_two, scale_two = scale_of(spread_two, g.gm[1:2, :])
     narrow_feature(g.PRE2, mean_two, scale_two, g.bm[1:2, :], g.F2.at[0], 0, 0)
     ch_two = gather(lambda s: g.F2.at[s], 0, R)
-    for copy in ld_w3:
-        copy.wait()
+    ld_w3.wait()
     mean_side, spread_side = wide_merge(0, st_side)
     inv_side, scale_side = scale_of(spread_side, g.go[1:2, :])
-    relay(ch_two)
-    landed(ch_two)
 
     def four(ref):
         return lanes([ref[s] for s in range(4)])
 
-    g.PRE3[...] = mm(four(g.F2), g.W3[...].reshape(4 * MI, CO))
+    def chip_product(chunk, ref, weight):
+        chunk[0].wait_recv()
+        value = mm(lanes([ref[0], ref[1]]), weight[0:2].reshape(2 * MI, CO))
+        relay(chunk)
+        chunk[3].wait_recv()
+        return value + mm(lanes([ref[2], ref[3]]), weight[2:4].reshape(2 * MI, CO))
+
+    g.PRE3[...] = chip_product(ch_two, g.F2, g.W3)
     st_three = wide_send(1, *wide_local(g.PRE3))
     mean_three, spread_three = wide_merge(1, st_three)
     inv_three, scale_three = scale_of(spread_three, g.go[0:1, :])
@@ -914,23 +995,15 @@
     rm_p4 = net.push(g.P4S, g.P4R, far)
     g.PRE4[...] = part[:, MI:]
 
-    def take_p4(ph):
-        rm_p4.wait_recv()
-
-        def add(at, carry):
-            rows = pl.ds(at, NCH)
-            g.PRE4[rows, :] = g.PRE4[rows, :] + g.P4R[rows, :].astype(F32)
-            return carry
-
-        over(R, NCH, add, 0)
-
-    st_four = narrow_send(2, *narrow_local(g.PRE4, 1, take_p4))
+    st_four = narrow_send(2, *narrow_local(g.PRE4, 1, taking(rm_p4, g.PRE4, g.P4R)))
     mean_four, spread_four = narrow_merge(2, st_four, 1)
     inv_four, scale_four = scale_of(spread_four, g.gm[2:3, :])
     narrow_feature(g.PRE4, mean_four, scale_four, g.bm[2:3, :], g.F4.at[0], 0, QS)
     ch_four = gather(lambda s: g.F4.at[s], QS, R)
-    for copy in ld_w5:
-        copy.wait()
+    ld_w5.wait()
+
+    def kernel_rows(ref, tap, first=0):
+        return jnp.concatenate([ref[tap, s] for s in range(first, first + 2)], axis=0)
 
     def spread_rows(src, dst_up, dst_down):
         def body(at, carry):
@@ -946,37 +1019,40 @@
         spread_rows(g.F4.at[s], g.D4.at[0, s], g.D4.at[1, s])
 
     fill_four(0)
-    relay(ch_four)
     ch_four[0].wait_recv()
     fill_four(1)
-    fill_four(2)
-    ch_four[3].wait_recv()
-    fill_four(3)
-
-    def whole_four(t, l):
+
+    def four_blocks(t, l, slots):
         rows = slice(l * QS, l * QS + R)
         if t == 1:
-            return lanes([g.F4[s, rows, :] for s in range(4)])
-        return lanes([g.D4[t // 2, s, rows, :] for s in range(4)])
+            return lanes([g.F4[s, rows, :] for s in slots])
+        return lanes([g.D4[t // 2, s, rows, :] for s in slots])
+
+    def whole_four(t, l):
+        return four_blocks(t, l, range(4))
 
     pre_five = None
-    for t in range(3):
-        for l in range(3):
-            term = mm(whole_four(t, l), kernel_rows(g.W5, 3 * t + l))
-            pre_five = term if pre_five is None else pre_five + term
+    for first in (0, 2):
+        if first:
+            relay(ch_four)
+            fill_four(2)
+            ch_four[3].wait_recv()
+            fill_four(3)
+        for t in range(3):
+            for l in range(3):
+                blocks = four_blocks(t, l, range(first, first + 2))
+                term = mm(blocks, kernel_rows(g.W5, 3 * t + l, first))
+                pre_five = term if pre_five is None else pre_five + term
     g.PRE5[...] = pre_five
     st_five = narrow_send(3, *narrow_local(g.PRE5, 1))
     mean_five, spread_five = narrow_merge(3, st_five, 1)
     inv_five, scale_five = scale_of(spread_five, g.gm[3:4, :])
     narrow_feature(g.PRE5, mean_five, scale_five, g.bm[3:4, :], g.F5.at[0], 0, 0)
     ch_five = gather(lambda s: g.F5.at[s], 0, R)
-    for copy in ld_w6:
-        copy.wait()
+    ld_w6.wait()
     ld_cot.wait()
     g.COTP[...] = mm_tn(g.po[...], g.COT[...])
-    relay(ch_five)
-    landed(ch_five)
-    g.PRE6[...] = mm(four(g.F5), g.W6[...].reshape(4 * MI, CO))
+    g.PRE6[...] = chip_product(ch_five, g.F5, g.W6)
     st_six = wide_send(2, *wide_local(g.PRE6))
     mean_six, spread_six = wide_merge(2, st_six)
     inv_six, scale_six = scale_of(spread_six, g.go[2:3, :])
@@ -1005,16 +1081,14 @@
     out_block = net.local(g.OUT, g.block_out)
 
     def wide_sums(ref, copies, count):
-        for copy in copies:
-            copy.wait_recv()
+        copies.wait_recv()
         return [
             wide_row(tree([ref[k, j * NW : (j + 1) * NW, :] for k in range(NB)]))
             for j in range(count)
         ]
 
     def narrow_sums(idx, copies):
-        for copy in copies:
-            copy.wait_recv()
+        copies.wait_recv()
         return [tree([g.SN[idx, k, j : j + 1, :] for k in range(NB)]) for j in range(2)]
 
     bsum_six, gsum_six = wide_sums(g.SW.at[3], st, 2)
@@ -1054,9 +1128,8 @@
         acc_b = jnp.zeros((8, MI), F32)
         acc_g = jnp.zeros((8, MI), F32)
         for ph in range(phases):
-            if ph:
-                pump(5)
-            copy[ph].wait_recv()
+            if copy is not None:
+                copy[ph].wait_recv()
 
             def body(at, carry, ph=ph):
                 b_acc, g_acc = carry
@@ -1064,7 +1137,9 @@
                 hat = (pre[rows, :] - mean) * inv
                 v = (pre[rows, :] - mean) * scale + bias
                 s = gate(v)
-                feat = near[rows, :] + got[rows, :].astype(F32)
+                feat = near[rows, :]
+                if got is not None:
+                    feat = feat + got[rows, :].astype(F32)
                 grad = feat * mask_rows(at, NCH) * (s * (1.0 + v * (1.0 - s)))
                 near[rows, :] = grad
                 return b_acc + fold(grad), g_acc + fold(grad * hat)
@@ -1107,11 +1182,15 @@
 
     jobs = []
 
+    def spilled(done, targets):
+        sem = net.take()
+        copies = [net.plan_local(source, place, sem) for source, place in targets]
+        return copies, net.plan_local(done, done, sem)
+
     def job(part, got, done, targets, across=None):
-        spill = [net.plan_local(source, place) for source, place in targets]
-        jobs.append(Summed(net, part, got, done, ring, spill, across))
-
-    def pump(most=99):
+        jobs.append(Summed(net, part, got, done, ring, spilled(done, targets), across))
+
+    def pump(most=3):
         left = sorted((work for work in jobs if work.todo), key=lambda work: -len(work.todo))
         for work in left[:most]:
             work.step()
@@ -1119,9 +1198,12 @@
     def slots_to(part, place):
         return [(part.at[pl.ds(2 * s, 2)], place(ranks[s])) for s in range(4)]
 
-    def chips_to(part, out):
+    def chips_to(part, out, taps=None):
+        def place(rank):
+            return out.at[rank] if taps is None else out.at[rank, :, taps]
+
         return [
-            (part.at[pl.ds(4 * s, 4), v], out.at[ranks[2 * v + s]])
+            (part.at[pl.ds(4 * s, 4), v], place(ranks[2 * v + s]))
             for s in range(2)
             for v in range(2)
         ]
@@ -1259,7 +1341,7 @@
         g.GF2, g.PRE2, mean_two, inv_two, scale_two, bsum_two, gsum_two, 1, 0,
         g.E2.at[0, 0], 0,
     )
-    cp = net.push(g.E2.at[0, 0, pl.ds(0, R)], g.E2.at[0, 1, pl.ds(0, R)], core)
+    ch = gather(lambda s: g.E2.at[0, s], 0, R)
 
     def lift(s):
         def body(at, carry):
@@ -1270,45 +1352,55 @@
 
         over(R, QS, body, 0)
 
+    def two_grad(w, slot):
+        e = g.E2[0, slot, 0:R, :]
+        for ph in range(4):
+            for t, l in taps_two(ph):
+                tap = 3 * t + l
+                part, tap = (g.K2A, tap) if tap < 5 else (g.K2B, tap - 5)
+                for s in range(2):
+                    grad = mm_tn(chip_one(s, ph, t == 0, l == 0), e)
+                    for p in range(4):
+                        rows = grad[p * piece : (p + 1) * piece]
+                        part[4 * s + p, w, tap] = rows.astype(BF)
+
     lift(0)
-    cp.wait_recv()
+    pump()
+    two_grad(0, 0)
+    ch[0].wait_recv()
     lift(1)
-    cp = []
+    relay(ch)
+    two_grad(1, 2)
+    for name, first, count in (("K2A", 0, 5), ("K2B", 5, 4)):
+        bufs = [getattr(g, name + end) for end in ("", "R", "D")]
+        job(*bufs, chips_to(bufs[2], g.k2, pl.ds(first, count)), far)
+    pump()
+    lift(2)
+    ch[3].wait_recv()
+    lift(3)
+
+    def own_two(tap):
+        far_own = jnp.concatenate([g.W2F[k, tap] for k in range(4)], axis=0)
+        far_other = jnp.concatenate([g.W2Q[k, tap] for k in range(4)], axis=0)
+        return lanes([g.W2[tap, 0], g.W2P[tap], far_own, far_other])
+
     for ph in range(4):
         part = None
         for t, l in taps_two(ph):
             rows = slice(QS, QS + R) if l == 0 else slice(0, R)
-            e = lanes([g.E2[1 if t == 0 else 0, s, rows, :] for s in range(2)])
-            term = mm_nt(e, taps_back(g.W2, g.W2P, 3 * t + l))
+            e = lanes([g.E2[1 if t == 0 else 0, s, rows, :] for s in range(4)])
+            term = mm_nt(e, own_two(3 * t + l))
             part = term if part is None else part + term
-        cp.append(
-            reduce_back(part, g.B1S.at[pl.ds(ph * R, R)], g.B1R.at[pl.ds(ph * R, R)])
-        )
-        g.GF1[ph * R : (ph + 1) * R, :] = part[:, :MI]
-    pump()
-    own_two = g.E2[0, 0, 0:R, :]
-
-    def two_grad(part, first, last):
-        for ph in range(4):
-            for t, l in taps_two(ph):
-                tap = 3 * t + l
-                if first <= tap < last:
-                    grad = mm_tn(whole_one(ph, t == 0, l == 0), own_two)
-                    taps_grad(part, tap - first, grad)
-
-    two_grad(g.K2A, 0, 5)
-    pump()
-    job(g.K2A, g.K2AR, g.K2AD, slots_to(g.K2AD, lambda rank: g.k2.at[rank, :, pl.ds(0, 5)]))
-    two_grad(g.K2B, 5, 9)
-    job(g.K2B, g.K2BR, g.K2BD, slots_to(g.K2BD, lambda rank: g.k2.at[rank, :, pl.ds(5, 4)]))
-    pump()
+        g.GF1[ph * R : (ph + 1) * R, :] = part
+        if ph == 3:
+            pump()
     st = narrow_back(
-        7, g.GF1, g.B1R, cp, 4, g.PRE1, mean_one, inv_one, scale_one, g.bm[0:1, :]
+        7, g.GF1, None, None, 4, g.PRE1, mean_one, inv_one, scale_one, g.bm[0:1, :]
     )
     side_far = mm_nt(es, lanes([g.WS[2], g.WSP[1]]))
     g.BSS[...] = side_far.astype(BF)
     cp_bs = net.push(g.BSS, g.BSR, far)
-    pump(5)
+    pump()
     bsum_one, gsum_one = narrow_sums(7, st)
     ch = []
     for ph in range(4):
@@ -1334,10 +1426,10 @@
             term = mm_tn(g.SRC[s, ph * R : (ph + 1) * R, :], e1)
             k1 = term if k1 is None else k1 + term
         chip_grad(g.K1, s, k1)
-    spill = [net.plan_local(source, place) for source, place in chips_to(g.K1D, g.k1)]
+    spill = spilled(g.K1D, chips_to(g.K1D, g.k1))
     jobs.append(Direct(net, g.K1, g.K1R, g.K1D, b, peers, spill, far))
     jobs[-1].step()
-    pump(5)
+    pump()
     cp_bs.wait_recv()
     g.IG[0:R, :] = g.IG[0:R, :] + g.IGS[...] + g.BSR[...].astype(F32)
     for ph in range(4):
@@ -1347,7 +1439,7 @@
     while any(work.todo for work in jobs):
         if jobs[-1].todo:
             jobs[-1].step()
-        pump(5)
+        pump()
 
     g.gain_mid_grad[...] = jnp.concatenate([gsum_one, gsum_two, gsum_four, gsum_five], axis=0)
     g.bias_mid_grad[...] = jnp.concatenate([bsum_one, bsum_two, bsum_four, bsum_five], axis=0)
@@ -1414,7 +1506,7 @@
         block_out=((R, CO), F32, ANY),
         images_grad=((4 * R, CI), F32, ANY),
         k1=((4, 4, CI // 4, MI), BF, ANY),
-        k2=((4, 2, 9, MI // 2, MI), BF, ANY),
+        k2=((4, 4, 9, MI // 4, MI), BF, ANY),
         k3=((4, 2, MI // 2, CO), BF, ANY),
         ks=((4, 2, CI // 2, CO), BF, ANY),
         k4=((4, 4, CO // 4, MI), BF, ANY),
@@ -1438,8 +1530,12 @@
         XS=((2, R, CI), BF),
         W1C=((2 * CI, 2 * MI), BF),
         W1P=((2, CI, MI), BF),
-        W2=((9, 4, MI, MI), BF),
-        W2P=((9, 2, MI, MI), BF),
+        W2=((9, 2, MI, MI), BF),
+        W2F=((NB, 9, MI // 4, MI), BF),
+        W2P=((9, MI, MI), BF),
+        W2Q=((4, 9, MI // 4, MI), BF),
+        P2S=((R, MI), BF),
+        P2R=((R, MI), BF),
         W3=((4, MI, CO), BF),
         W3P=((2, MI, CO), BF),
         WS=((4, CI, CO), BF),
@@ -1463,8 +1559,8 @@
         PRE4=((R, MI), F32),
         PRE5=((R, MI), F32),
         PRE6=((R, CO), F32),
-        F1=((4, 4, QS + R, MI), BF),
-        D1=((2, 4, QS + R, MI), BF),
+        F1=((2, 4, QS + R, MI), BF),
+        D1=((2, 2, QS + R, MI), BF),
         F2=((4, R, MI), BF),
         BM=((R, CO), F32),
         MIDC=((2, R, CO), BF),
@@ -1488,9 +1584,7 @@
         B2S=((R, MI), BF),
         B2R=((R, MI), BF),
         GF2=((R, MI), F32),
-        E2=((2, 2, R + QS, MI), BF),
-        B1S=((4 * R, MI), BF),
-        B1R=((4 * R, MI), BF),
+        E2=((2, 4, R + QS, MI), BF),
         GF1=((4 * R, MI), F32),
         G1=((4, 4, R, MI), BF),
         IGS=((R, CI), F32),
@@ -1503,8 +1597,8 @@
     )
     for name, piece in dict(
         K1=(2, CI // 4, MI),
-        K2A=(5, MI // 2, MI),
-        K2B=(4, MI // 2, MI),
+        K2A=(2, 5, MI // 4, MI),
+        K2B=(2, 4, MI // 4, MI),
         K3=(MI // 2, CO),
         KSA=(CI // 2, CO // 2),
         KSB=(CI // 2, CO // 2),
@@ -1565,6 +1659,9 @@
     return mm(pick, high) + mm(pick, low)
 
 
+ORDER = (5, 3, 7, 6, 4, 8, 2, 1, 0)
+
+
 def finish_kernel(*refs):
     ins, po, pi, small = refs[:9], refs[9], refs[10], refs[11:19]
     outs, small_outs = refs[19:28], refs[28:36]
@@ -1573,8 +1670,8 @@
     stores = [
         pltpu.make_async_copy(v, a, sems.at[9 + k]) for k, (v, a) in enumerate(zip(made, outs))
     ]
-    for copy in loads:
-        copy.start()
+    for k in ORDER:
+        loads[k].start()
     for a, v in zip(small, small_outs):
         v[...] = a[...]
 
@@ -1592,12 +1689,14 @@
 
         def tap(t):
             for rank in range(4):
-                for h in range(2):
-                    at = (2 * rank + h) * size
+                for h in range(src.shape[1]):
+                    at = (src.shape[1] * rank + h) * size
                     dst[t // 3, t % 3, at : at + size, :] = src[rank, h, t].astype(F32)
 
         for t in range(src.shape[2]):
             tap(t)
+            store = pltpu.make_async_copy(dst.at[t // 3, t % 3], outs[k].at[t // 3, t % 3], sems.at[9 + k])
+            store.start()
 
     def block():
         made[0][...] = exact(po[...], held[0][...])
@@ -1611,7 +1710,7 @@
             for at in range(value.shape[0]):
                 made[1][at // rows, 2 * (at % rows) + a] = value[at]
 
-    for k in (3, 7, 5, 2, 4, 6, 8, 0, 1):
+    for k in ORDER:
         loads[k].wait()
         if k == 0:
             block()
@@ -1621,7 +1720,8 @@
             taps_of(k)
         else:
             rows_of(k)
-        stores[k].start()
+        if k not in (3, 7):
+            stores[k].start()
     for copy in stores:
         copy.wait()
 

time: 244 us -> 225 us (0.922)
  Pallas kernels: 243 us -> 224 us
    pallas_call x1, Pallas kernels: 234 us -> 214 us  [fused_on_device(): pl.pallas_call(functools.partial(block_kernel, geo, names), out_shape=[ja...]
where the time goes in v4:
time: 225 us; the launch traced here: 224 us
  Pallas kernels  224 us (100%)
    pallas_call x1, Pallas kernels, fused_on_device(): pl.pallas_call(functools.partial(block_kernel, geo, names), out_shape=[ja...  214 us
    pallas_call x1, Pallas kernels, fused_on_device(): pl.pallas_call(finish_kernel, out_shape=finals + [jax.ShapeDtypeStruct(v....  9.69 us

profile of v4, /device:TPU:0, one launch (start us, length us, event | category | flops | bytes accessed | tf_op | source)
XLA Modules:
  0.0 224.5 jit_solution(8446954780417381318)
XLA Ops:
  0.7 213.9 %shard_map.296 = (f32[384,512]{1,0:T(8,128)}, f32[1536,256]{1,0:T(8,128)}, bf16[4,4,64,128]{3,2,1,0:T(8,128)(2,1)}, bf16[4,4,9,32,128]{4,3,2,1,0:T(8,128)(2,1)},...) custom-call(bf16[1536,256]{1,0:T(8,128)(2,1)} %bitcast.11, ...), custom_call_target="tpu_custom_call" | custom-call | tf_op jit(solution)/shard_map/pallas_call | solution.py:1617
  214.6 9.7 %shard_map.297 = (f32[384,512]{1,0:T(8,128)}, f32[4,16,24,256]{3,2,1,0:T(8,128)}, f32[1024,128]{1,0:T(8,128)}, f32[3,3,512,128]{3,2,1,0:T(8,128)}, f32[512,512]{...) custom-call(f32[384,512]{1,0:T(8,128)} %get-tuple-element.51.refs_0_, ...), custom_call_target="tpu_custom_call" | custom-call | tf_op jit(solution)/shard_map/pallas_call | solution.py:1641

commit v5 on v4

--- a/solution.py
+++ b/solution.py
@@ -358,6 +358,7 @@
 
     def take(self):
         self.used += 1
+        assert self.used <= SEMS
         return self.sems.at[self.used - 1]
 
     def plan(self, src, dst, device, send_sem=None, recv_sem=None):
@@ -525,7 +526,7 @@
         self.spill_wait.wait()
 
 
-SEMS = 344
+SEMS = 356
 
 
 def block_kernel(geo, names, *refs):
@@ -535,8 +536,8 @@
     NB = geo.NB
     r = lax.axis_index("chan")
     b = lax.axis_index("batch")
-    r1, r3 = flip(r, 1), flip(r, 2)
-    r2 = flip(r1, 2)
+    r1, r2 = flip(r, 1), flip(r, 2)
+    r3 = flip(r1, 2)
     ranks = (r, r1, r2, r3)
     core, far = (b, r1), (b, r2)
     peers = []
@@ -557,7 +558,7 @@
         x = lax.div(place, 4)
         return 2 * (place + x * (7 - 2 * place)) + x
 
-    way = 1 - 2 * lax.rem(lax.rem(r, 2) + lax.div(r, 2), 2)
+    way = 1 - 2 * lax.rem(r, 2)
     places = {k: lax.rem(seat(b) + way * k + 16, 8) for k in range(-3, 5)}
     ring = (places.get, (batch_at(places[1]), r), (batch_at(places[-1]), r))
 
@@ -1410,26 +1411,26 @@
         )
         ch.append(gather(lambda s, ph=ph: g.G1.at[s, ph], 0, R))
     pump()
+    k1 = [None, None]
+    for ph in range(4):
+        relay(ch[ph])
+        if ph == 1:
+            pump()
+        e1 = lanes([g.G1[0, ph], g.G1[2, ph]])
+        for s in range(2):
+            term = mm_tn(g.SRC[s, ph * R : (ph + 1) * R, :], e1)
+            k1[s] = term if k1[s] is None else k1[s] + term
+    for s in range(2):
+        chip_grad(g.K1, s, k1[s])
+    job(g.K1, g.K1R, g.K1D, chips_to(g.K1D, g.k1), far)
+    pump()
     w1_own = lanes([g.W1C[0:CI, MI:], g.W1P[0], g.W1C[0:CI, :MI], g.W1P[1]])
-    relay(ch[0])
     for ph in range(4):
-        if ph < 3:
-            relay(ch[ph + 1])
         landed(ch[ph])
-        pump()
         whole = lanes([g.G1[s, ph] for s in range(4)])
         g.IG[ph * R : (ph + 1) * R, :] = mm_nt(whole, w1_own)
-    for s in range(2):
-        k1 = None
-        for ph in range(4):
-            e1 = lanes([g.G1[0, ph], g.G1[2, ph]])
-            term = mm_tn(g.SRC[s, ph * R : (ph + 1) * R, :], e1)
-            k1 = term if k1 is None else k1 + term
-        chip_grad(g.K1, s, k1)
-    spill = spilled(g.K1D, chips_to(g.K1D, g.k1))
-    jobs.append(Direct(net, g.K1, g.K1R, g.K1D, b, peers, spill, far))
-    jobs[-1].step()
-    pump()
+        if ph % 2:
+            pump()
     cp_bs.wait_recv()
     g.IG[0:R, :] = g.IG[0:R, :] + g.IGS[...] + g.BSR[...].astype(F32)
     for ph in range(4):
@@ -1437,8 +1438,6 @@
         g.IG[rows, :] = g.IG[rows, :] * bc(g.mask[...], CI)
     give(g.IG, g.images_grad)
     while any(work.todo for work in jobs):
-        if jobs[-1].todo:
-            jobs[-1].step()
         pump()
 
     g.gain_mid_grad[...] = jnp.concatenate([gsum_one, gsum_two, gsum_four, gsum_five], axis=0)
@@ -1609,7 +1608,7 @@
     ).items():
         scratch[name] = ((8, *piece), BF)
         scratch[name + "D"] = ((8, *piece), BF)
-        scratch[name + "R"] = ((8 if name == "K1" else 7, *piece), BF)
+        scratch[name + "R"] = ((7, *piece), BF)
     names = [*ins, *outs, *scratch, "sems"]
     geo = types.SimpleNamespace(
         R=R, QS=QS, PS=n, CI=CI, MI=MI, CO=CO, NB=NB, rows=rows, cols=cols

time: 225 us -> 217 us (0.964)
  Pallas kernels: 224 us -> 215 us
    pallas_call x1, Pallas kernels: 214 us -> 205 us  [fused_on_device(): pl.pallas_call(functools.partial(block_kernel, geo, names), out_shape=[ja...]
where the time goes in v5:
time: 217 us; the launch traced here: 216 us
  Pallas kernels  215 us (99%)
    pallas_call x1, Pallas kernels, fused_on_device(): pl.pallas_call(functools.partial(block_kernel, geo, names), out_shape=[ja...  205 us
    pallas_call x1, Pallas kernels, fused_on_device(): pl.pallas_call(finish_kernel, out_shape=finals + [jax.ShapeDtypeStruct(v....  9.69 us

profile of v5, /device:TPU:0, one launch (start us, length us, event | category | flops | bytes accessed | tf_op | source)
XLA Modules:
  0.0 216.0 jit_solution(16883127946138049179)
XLA Ops:
  0.7 205.4 %shard_map.296 = (f32[384,512]{1,0:T(8,128)}, f32[1536,256]{1,0:T(8,128)}, bf16[4,4,64,128]{3,2,1,0:T(8,128)(2,1)}, bf16[4,4,9,32,128]{4,3,2,1,0:T(8,128)(2,1)},...) custom-call(bf16[1536,256]{1,0:T(8,128)(2,1)} %bitcast.11, ...), custom_call_target="tpu_custom_call" | custom-call | tf_op jit(solution)/shard_map/pallas_call | solution.py:1616
  206.1 9.7 %shard_map.297 = (f32[384,512]{1,0:T(8,128)}, f32[4,16,24,256]{3,2,1,0:T(8,128)}, f32[1024,128]{1,0:T(8,128)}, f32[3,3,512,128]{3,2,1,0:T(8,128)}, f32[512,512]{...) custom-call(f32[384,512]{1,0:T(8,128)} %get-tuple-element.51.refs_0_, ...), custom_call_target="tpu_custom_call" | custom-call | tf_op jit(solution)/shard_map/pallas_call | solution.py:1640

commit v6 on v5

--- a/solution.py
+++ b/solution.py
@@ -405,16 +405,24 @@
         legs, legs_back = net.take(), net.take()
         up = [part.at[at(4)]] + [got.at[k] for k in range(4)]
         down = [part.at[at(-3)]] + [got.at[k] for k in range(4, 7)]
+        ends, ends_back = [[net.take() for k in range(4)] for _ in range(2)]
         self.out = [
-            [net.plan(up[k], up[k + 1], ahead, legs)]
-            + ([net.plan(down[k], down[k + 1], behind, legs)] if k < 3 else [])
+            [net.plan(up[k], up[k + 1], ahead, legs, ends[k])]
+            + ([net.plan(down[k], down[k + 1], behind, legs, ends[k])] if k < 3 else [])
             for k in range(4)
         ]
         self.back = [
-            ([net.plan(done.at[at(-k)], done.at[at(-k)], ahead, legs_back)] if k < 3 else [])
-            + [net.plan(done.at[at(k)], done.at[at(k)], behind, legs_back)]
+            ([net.plan(done.at[at(-k)], done.at[at(-k)], ahead, legs_back, ends_back[k])] if k < 3 else [])
+            + [net.plan(done.at[at(k)], done.at[at(k)], behind, legs_back, ends_back[k])]
             for k in range(4)
         ]
+        self.pair, self.pair_back = (
+            [
+                net.plan(got.at[pl.ds(0, 1 + (k < 3))], got.at[pl.ds(0, 1 + (k < 3))], ahead, legs, end)
+                for k, end in enumerate(some)
+            ]
+            for some in (ends, ends_back)
+        )
         self.left = [
             net.plan(got, got, ahead, legs, legs),
             net.plan(done.at[pl.ds(0, 7)], done.at[pl.ds(0, 7)], ahead, legs_back, legs_back),
@@ -434,22 +442,18 @@
         for copy in copies:
             copy.start()
 
-    def arrived(self, copies):
-        for copy in copies:
-            copy.wait_recv()
-
     def begin(self):
         self.start(self.out[0])
 
     def add(self, k):
-        self.arrived(self.out[k])
+        self.pair[k].wait_recv()
         self.got[k] = self.got[k] + self.part[self.at(3 - k)]
         if k < 2:
             self.got[4 + k] = self.got[4 + k] + self.part[self.at(k - 2)]
         self.start(self.out[k + 1])
 
     def finish(self):
-        self.arrived(self.out[3])
+        self.pair[3].wait_recv()
         total = self.got[3] + self.got[6] + self.part[self.at(0)]
         if self.across:
             self.done[self.at(0), 0] = total[0]
@@ -464,11 +468,11 @@
         self.start(self.back[0])
 
     def pass_on(self, k):
-        self.arrived(self.back[k])
+        self.pair_back[k].wait_recv()
         self.start(self.back[k + 1])
 
     def last(self):
-        self.arrived(self.back[3])
+        self.pair_back[3].wait_recv()
         self.start(self.spill)
 
     def drain(self):
@@ -526,7 +530,7 @@
         self.spill_wait.wait()
 
 
-SEMS = 356
+SEMS = 296
 
 
 def block_kernel(geo, names, *refs):
@@ -633,6 +637,7 @@
         net.push(rows_of(g.w1, rank, CI), g.W1C.at[pl.ds(s * CI, CI), pl.ds(0, MI)], far)
         for s, rank in enumerate((r2, r3))
     ]
+    rm_gain = [net.push(g.gm, g.GMF, far), net.push(g.bm, g.BMF, far)]
     piece = MI // 4
     rank = jnp.where(b < 4, r2, r3)
     at = pl.multiple_of(rank * MI + lax.rem(b, 4) * piece, piece)
@@ -867,18 +872,42 @@
         span = pl.ds(QS, R)
         ch_one.append(net.push(g.F1.at[0, ph, span], g.F1.at[1, ph, span], core))
 
-    def taking(copy, pre, got):
-        def take(ph):
-            copy.wait_recv()
-
-            def add(at, carry):
-                rows = pl.ds(at, NCH)
-                pre[rows, :] = pre[rows, :] + got[rows, :].astype(F32)
-                return carry
-
-            over(R, NCH, add, 0)
-
-        return take
+    def both_chips(part, sent, got, pre, pre_far):
+        sent[...] = part.astype(BF)
+        copy = net.push(sent, got, far)
+        pre[...] = part[:, MI:]
+        pre_far[...] = part[:, :MI]
+        return copy
+
+    def both_norms(idx, copy, got, pre, pre_far, row, feature, at0):
+        copy.wait_recv()
+
+        def add(at, carry):
+            rows = pl.ds(at, NCH)
+            pre[rows, :] = pre[rows, :] + got[rows, 0:MI].astype(F32)
+            pre_far[rows, :] = pre_far[rows, :] + got[rows, MI : 2 * MI].astype(F32)
+            return carry
+
+        over(R, NCH, add, 0)
+        slots = g.SB.at[idx]
+        for k, value in enumerate((*narrow_local(pre, 1), *narrow_local(pre_far, 1))):
+            g.SB[idx, 0, k : k + 1, :] = value
+        exchange(slots, 4).wait_recv()
+        results = []
+        for k, gains, biases in ((0, g.gm, g.bm), (2, g.GMF, g.BMF)):
+            sums = [g.SB[idx, j, k : k + 1, :] for j in range(NB)]
+            squares = [g.SB[idx, j, k + 1 : k + 2, :] for j in range(NB)]
+            mean, spread = moments(sums, squares, 1)
+            inv, scale = scale_of(spread, gains[row : row + 1, :])
+            here = pl.ds(at0, R)
+            source = pre_far if k else pre
+            narrow_feature(source, mean, scale, biases[row : row + 1, :], feature.at[k], 0, at0)
+            results.append(
+                net.push(feature.at[k, here], feature.at[k + 1, here], core)
+            )
+            if k == 0:
+                kept = mean, spread, inv, scale
+        return kept, results
 
     rm_xs.wait_recv()
     rm_xs2 = net.push(g.XS.at[0], g.XS.at[1], core)
@@ -934,18 +963,15 @@
         for t, l in taps_two(ph):
             term = mm(lanes([chip_one(s, ph, t == 0, l == 0) for s in range(2)]), both_two(3 * t + l))
             part = term if part is None else part + term
-    g.P2S[...] = part[:, :MI].astype(BF)
-    rm_p2 = net.push(g.P2S, g.P2R, far)
-    g.PRE2[...] = part[:, MI:]
+    rm_p2 = both_chips(part, g.P2S, g.P2R, g.PRE2, g.PRE2F)
     rm_w4 = [
         net.push(rows_of(g.w4, rank, CO), g.W4C.at[pl.ds(s * CO, CO), pl.ds(0, MI)], far)
         for s, rank in enumerate((r2, r3))
     ]
-    st_two = narrow_send(1, *narrow_local(g.PRE2, 1, taking(rm_p2, g.PRE2, g.P2R)))
-    mean_two, spread_two = narrow_merge(1, st_two, 1)
-    inv_two, scale_two = scale_of(spread_two, g.gm[1:2, :])
-    narrow_feature(g.PRE2, mean_two, scale_two, g.bm[1:2, :], g.F2.at[0], 0, 0)
-    ch_two = gather(lambda s: g.F2.at[s], 0, R)
+    for copy in rm_gain:
+        copy.wait_recv()
+    kept, ch_two = both_norms(0, rm_p2, g.P2R, g.PRE2, g.PRE2F, 1, g.F2, 0)
+    mean_two, spread_two, inv_two, scale_two = kept
     ld_w3.wait()
     mean_side, spread_side = wide_merge(0, st_side)
     inv_side, scale_side = scale_of(spread_side, g.go[1:2, :])
@@ -953,14 +979,13 @@
     def four(ref):
         return lanes([ref[s] for s in range(4)])
 
-    def chip_product(chunk, ref, weight):
-        chunk[0].wait_recv()
-        value = mm(lanes([ref[0], ref[1]]), weight[0:2].reshape(2 * MI, CO))
-        relay(chunk)
-        chunk[3].wait_recv()
-        return value + mm(lanes([ref[2], ref[3]]), weight[2:4].reshape(2 * MI, CO))
-
-    g.PRE3[...] = chip_product(ch_two, g.F2, g.W3)
+    def half_product(ref, weight, a, b):
+        return mm(lanes([ref[a], ref[b]]), jnp.concatenate([weight[a], weight[b]], axis=0))
+
+    pre_three = half_product(g.F2, g.W3, 0, 2)
+    for copy in ch_two:
+        copy.wait_recv()
+    g.PRE3[...] = pre_three + half_product(g.F2, g.W3, 1, 3)
     st_three = wide_send(1, *wide_local(g.PRE3))
     mean_three, spread_three = wide_merge(1, st_three)
     inv_three, scale_three = scale_of(spread_three, g.go[0:1, :])
@@ -992,19 +1017,14 @@
     rm_back.append(net.push(g.W4C.at[pl.ds(CO, CO), pl.ds(0, MI)], g.W4P.at[1], core))
     rm_mid.wait_recv()
     part = mm(lanes([g.MIDC[0], g.MIDC[1]]), g.W4C[...])
-    g.P4S[...] = part[:, :MI].astype(BF)
-    rm_p4 = net.push(g.P4S, g.P4R, far)
-    g.PRE4[...] = part[:, MI:]
-
-    st_four = narrow_send(2, *narrow_local(g.PRE4, 1, taking(rm_p4, g.PRE4, g.P4R)))
-    mean_four, spread_four = narrow_merge(2, st_four, 1)
-    inv_four, scale_four = scale_of(spread_four, g.gm[2:3, :])
-    narrow_feature(g.PRE4, mean_four, scale_four, g.bm[2:3, :], g.F4.at[0], 0, QS)
-    ch_four = gather(lambda s: g.F4.at[s], QS, R)
+    rm_p4 = both_chips(part, g.P4S, g.P4R, g.PRE4, g.PRE4F)
+
+    kept, ch_four = both_norms(1, rm_p4, g.P4R, g.PRE4, g.PRE4F, 2, g.F4, QS)
+    mean_four, spread_four, inv_four, scale_four = kept
     ld_w5.wait()
 
-    def kernel_rows(ref, tap, first=0):
-        return jnp.concatenate([ref[tap, s] for s in range(first, first + 2)], axis=0)
+    def kernel_rows(ref, tap, slots):
+        return jnp.concatenate([ref[tap, s] for s in slots], axis=0)
 
     def spread_rows(src, dst_up, dst_down):
         def body(at, carry):
@@ -1020,8 +1040,7 @@
         spread_rows(g.F4.at[s], g.D4.at[0, s], g.D4.at[1, s])
 
     fill_four(0)
-    ch_four[0].wait_recv()
-    fill_four(1)
+    fill_four(2)
 
     def four_blocks(t, l, slots):
         rows = slice(l * QS, l * QS + R)
@@ -1033,16 +1052,14 @@
         return four_blocks(t, l, range(4))
 
     pre_five = None
-    for first in (0, 2):
-        if first:
-            relay(ch_four)
-            fill_four(2)
-            ch_four[3].wait_recv()
-            fill_four(3)
+    for slots in ((0, 2), (1, 3)):
+        if slots[0]:
+            for s, copy in zip(slots, ch_four):
+                copy.wait_recv()
+                fill_four(s)
         for t in range(3):
             for l in range(3):
-                blocks = four_blocks(t, l, range(first, first + 2))
-                term = mm(blocks, kernel_rows(g.W5, 3 * t + l, first))
+                term = mm(four_blocks(t, l, slots), kernel_rows(g.W5, 3 * t + l, slots))
                 pre_five = term if pre_five is None else pre_five + term
     g.PRE5[...] = pre_five
     st_five = narrow_send(3, *narrow_local(g.PRE5, 1))
@@ -1053,7 +1070,11 @@
     ld_w6.wait()
     ld_cot.wait()
     g.COTP[...] = mm_tn(g.po[...], g.COT[...])
-    g.PRE6[...] = chip_product(ch_five, g.F5, g.W6)
+    ch_five[0].wait_recv()
+    pre_six = half_product(g.F5, g.W6, 0, 1)
+    relay(ch_five)
+    ch_five[3].wait_recv()
+    g.PRE6[...] = pre_six + half_product(g.F5, g.W6, 2, 3)
     st_six = wide_send(2, *wide_local(g.PRE6))
     mean_six, spread_six = wide_merge(2, st_six)
     inv_six, scale_six = scale_of(spread_six, g.go[2:3, :])
@@ -1533,8 +1554,13 @@
         W2F=((NB, 9, MI // 4, MI), BF),
         W2P=((9, MI, MI), BF),
         W2Q=((4, 9, MI // 4, MI), BF),
-        P2S=((R, MI), BF),
-        P2R=((R, MI), BF),
+        P2S=((R, 2 * MI), BF),
+        P2R=((R, 2 * MI), BF),
+        PRE2F=((R, MI), F32),
+        PRE4F=((R, MI), F32),
+        GMF=((4, MI), F32),
+        BMF=((4, MI), F32),
+        SB=((2, NB, 4, MI), F32),
         W3=((4, MI, CO), BF),
         W3P=((2, MI, CO), BF),
         WS=((4, CI, CO), BF),
@@ -1549,8 +1575,8 @@
         COTP=((R, CO), F32),
         P1S=((4, R, MI), BF),
         P1R=((4, R, MI), BF),
-        P4S=((R, MI), BF),
-        P4R=((R, MI), BF),
+        P4S=((R, 2 * MI), BF),
+        P4R=((R, 2 * MI), BF),
         PRE1=((4 * R, MI), F32),
         PRE2=((R, MI), F32),
         PRE3=((R, CO), F32),

time: 217 us -> 213 us (0.982)
  Pallas kernels: 215 us -> 212 us
    pallas_call x1, Pallas kernels: 205 us -> 202 us  [fused_on_device(): pl.pallas_call(functools.partial(block_kernel, geo, names), out_shape=[ja...]
where the time goes in v6:
time: 213 us
  Pallas kernels  212 us (100%)
    pallas_call x1, Pallas kernels, fused_on_device(): pl.pallas_call(functools.partial(block_kernel, geo, names), out_shape=[ja...  202 us
    pallas_call x1, Pallas kernels, fused_on_device(): pl.pallas_call(finish_kernel, out_shape=finals + [jax.ShapeDtypeStruct(v....  9.69 us

profile of v6, /device:TPU:0, one launch (start us, length us, event | category | flops | bytes accessed | tf_op | source)
XLA Modules:
  0.0 212.6 jit_solution(12482410861455123957)
XLA Ops:
  0.7 202.1 %shard_map.296 = (f32[384,512]{1,0:T(8,128)}, f32[1536,256]{1,0:T(8,128)}, bf16[4,4,64,128]{3,2,1,0:T(8,128)(2,1)}, bf16[4,4,9,32,128]{4,3,2,1,0:T(8,128)(2,1)},...) custom-call(bf16[1536,256]{1,0:T(8,128)(2,1)} %bitcast.11, ...), custom_call_target="tpu_custom_call" | custom-call | tf_op jit(solution)/shard_map/pallas_call | solution.py:1642
  202.8 9.7 %shard_map.297 = (f32[384,512]{1,0:T(8,128)}, f32[4,16,24,256]{3,2,1,0:T(8,128)}, f32[1024,128]{1,0:T(8,128)}, f32[3,3,512,128]{3,2,1,0:T(8,128)}, f32[512,512]{...) custom-call(f32[384,512]{1,0:T(8,128)} %get-tuple-element.51.refs_0_, ...), custom_call_target="tpu_custom_call" | custom-call | tf_op jit(solution)/shard_map/pallas_call | solution.py:1666

commit v7 on v6

--- a/solution.py
+++ b/solution.py
@@ -1456,8 +1456,8 @@
     g.IG[0:R, :] = g.IG[0:R, :] + g.IGS[...] + g.BSR[...].astype(F32)
     for ph in range(4):
         rows = slice(ph * R, (ph + 1) * R)
-        g.IG[rows, :] = g.IG[rows, :] * bc(g.mask[...], CI)
-    give(g.IG, g.images_grad)
+        g.IGB[rows, :] = (g.IG[rows, :] * bc(g.mask[...], CI)).astype(BF)
+    give(g.IGB, g.images_grad)
     while any(work.todo for work in jobs):
         pump()
 
@@ -1524,7 +1524,7 @@
     )
     outs = dict(
         block_out=((R, CO), F32, ANY),
-        images_grad=((4 * R, CI), F32, ANY),
+        images_grad=((4 * R, CI), BF, ANY),
         k1=((4, 4, CI // 4, MI), BF, ANY),
         k2=((4, 4, 9, MI // 4, MI), BF, ANY),
         k3=((4, 2, MI // 2, CO), BF, ANY),
@@ -1616,6 +1616,7 @@
         BSS=((R, CI), BF),
         BSR=((R, CI), BF),
         IG=((4 * R, CI), F32),
+        IGB=((4 * R, CI), BF),
         SN=((8, NB, 2, MI), F32),
         SW=((4, NB, 2 * NW, 128), F32),
         SA=((NB, 4 * NW, 128), F32),
@@ -1668,7 +1669,7 @@
         out_shape=finals + [jax.ShapeDtypeStruct(v.shape, F32) for v in passed],
         in_specs=[ANY] * 9 + [VM] * 10,
         out_specs=[ANY] * 9 + [VM] * 8,
-        scratch_shapes=[pltpu.VMEM((R, CO), F32), pltpu.VMEM((4 * R, CI), F32)]
+        scratch_shapes=[pltpu.VMEM((R, CO), F32), pltpu.VMEM((4 * R, CI), BF)]
         + [pltpu.VMEM(k.shape, BF) for k in ks]
         + [pltpu.VMEM(f.shape, F32) for f in finals]
         + [pltpu.SemaphoreType.DMA((18,))],
@@ -1729,7 +1730,7 @@
     def images():
         half = held[1].shape[0] // 2
         for a in range(2):
-            value = exact(pi[...], held[1][a * half : (a + 1) * half, :])
+            value = mm(pi[...], held[1][a * half : (a + 1) * half, :])
             value = value.reshape(-1, *made[1].shape[2:])
             rows = made[1].shape[1] // 2
             for at in range(value.shape[0]):

time: 213 us -> 212 us (level)
  no operation moved by 1% of the time
where the time goes in v7:
time: 212 us; the launch traced here: 211 us
  Pallas kernels  210 us (99%)
    pallas_call x1, Pallas kernels, fused_on_device(): pl.pallas_call(functools.partial(block_kernel, geo, names), out_shape=[ja...  202 us
    pallas_call x1, Pallas kernels, fused_on_device(): pl.pallas_call(finish_kernel, out_shape=finals + [jax.ShapeDtypeStruct(v....  8.36 us

profile of v7, /device:TPU:0, one launch (start us, length us, event | category | flops | bytes accessed | tf_op | source)
XLA Modules:
  0.0 211.3 jit_solution(15373400932323955550)
XLA Ops:
  0.7 202.1 %shard_map.296 = (f32[384,512]{1,0:T(8,128)}, bf16[1536,256]{1,0:T(8,128)(2,1)}, bf16[4,4,64,128]{3,2,1,0:T(8,128)(2,1)}, bf16[4,4,9,32,128]{4,3,2,1,0:T(8,128)(...) custom-call(bf16[1536,256]{1,0:T(8,128)(2,1)} %bitcast.11, ...), custom_call_target="tpu_custom_call" | custom-call | tf_op jit(solution)/shard_map/pallas_call | solution.py:1643
  202.8 8.4 %shard_map.297 = (f32[384,512]{1,0:T(8,128)}, f32[4,16,24,256]{3,2,1,0:T(8,128)}, f32[1024,128]{1,0:T(8,128)}, f32[3,3,512,128]{3,2,1,0:T(8,128)}, f32[512,512]{...) custom-call(f32[384,512]{1,0:T(8,128)} %get-tuple-element.51.refs_0_, ...), custom_call_target="tpu_custom_call" | custom-call | tf_op jit(solution)/shard_map/pallas_call | solution.py:1667
